TPU v7x, 32 devices: a whole 2x2x4 slice. The times are simulated.
32 devices in a mesh: section: 4 (over z), dp: 8 (over y, x, core).
Axes of the slice: x: 2, y: 2, z: 4, core: 2. Of those that a mesh axis runs over, the one named last changes fastest.
Arguments:
- act_in: float32 [4, 2, 8, 15, 15, 256], P('section', None, 'dp'), may hold values from -6 to 6
- act_mid: float32 [4, 2, 8, 15, 15, 256], P('section', None, 'dp'), may hold values from 0 to 2
- relu_mask: int32 [4, 2, 8, 15, 15, 256], P('section', None, 'dp'), may hold values 0 or 1
- arriving: float32 [4, 8, 15, 15, 256], P('section', 'dp'), may hold values from -6 to 6
- loss_grad: float32 [1, 8, 15, 15, 256], P(None, 'dp'), may hold values from -6 to 6
- w_first: float32 [4, 1792, 256], P('section', 'dp'), may hold values from -0.125 to 0.125
- w_second: float32 [4, 1792, 256], P('section', 'dp'), may hold values from -0.125 to 0.125
Outputs:
- data_grad: float32 [4, 2, 8, 15, 15, 256], P('section', None, 'dp')
- first_grad: float32 [4, 1792, 256], P('section', 'dp')
- second_grad: float32 [4, 1792, 256], P('section', 'dp')
All inputs are finite; a program needn't handle non-finite values. No bound on the sum of `relu_mask` on one device may be relied on, other than what follows from the above.
Results may differ from a plain program's by a relative error of at most 0.00011.
Values sent between devices are 32-bit elements; how exact they have to be, the bound alone decides.
No kernel may reach another device: no remote copies, remote signals or barrier semaphores. Data moves between devices by JAX's collectives and lax.ppermute only.
A program may use at most 64 MiB of HBM per device.

v0:
```python
import jax
import jax.numpy as jnp
from jax import lax
from jax.sharding import PartitionSpec as P


def shifted(shard, axis, by):
    peers = lax.axis_size(axis)
    pairs = [(i, i + by) for i in range(peers) if 0 <= i + by < peers]
    return lax.ppermute(shard, axis, pairs)


def spread_taps(values, spatial):
    widths = [(0, 0)] * 4
    widths[spatial] = (3, 3)
    padded = jnp.pad(values, widths)
    extent = values.shape[spatial]
    pieces = [
        lax.slice_in_dim(padded, offset, offset + extent, axis=spatial) for offset in range(7)
    ]
    return jnp.concatenate(pieces, axis=-1)


def fold_taps(products, spatial):
    channels = products.shape[-1] // 7
    widths = [(0, 0)] * 4
    widths[spatial] = (3, 3)
    padded = jnp.pad(products, widths)
    extent = products.shape[spatial]
    summed = jnp.zeros(products.shape[:-1] + (channels,), products.dtype)
    for offset in range(7):
        window = lax.slice_in_dim(padded, 6 - offset, 6 - offset + extent, axis=spatial)
        summed = summed + window[..., offset * channels : (offset + 1) * channels]
    return summed


def project_taps(values, weight):
    return jnp.einsum("nhwc,kc->nhwk", values, weight, precision=lax.Precision.HIGHEST)


def flat_patches(values, spatial):
    patches = spread_taps(values.reshape((-1,) + values.shape[2:]), spatial)
    return patches.reshape(-1, patches.shape[-1])


def correlate(patches, grad_rows, mean_scale):
    return jnp.einsum("rk,rc->kc", patches, grad_rows, precision=lax.Precision.HIGHEST) * mean_scale


def local(act_in, act_mid, relu_mask, arriving, loss_grad, w_first, w_second):
    tick_count = act_in.shape[1]
    channels = act_in.shape[-1]
    is_last = lax.axis_index("section") == lax.axis_size("section") - 1
    full_first, full_second = (
        lax.all_gather(w_first[0], "dp", axis=0, tiled=True),
        lax.all_gather(w_second[0], "dp", axis=0, tiled=True),
    )
    incoming = arriving[0]
    mid_grad = fold_taps(project_taps(incoming, full_second), 1)
    in_list = [incoming]
    pre_list = []
    out_list = []
    for tick_index in range(tick_count):
        if tick_index > 0:
            from_above = shifted(out_list[-1], "section", -1)
            incoming = jnp.where(is_last, loss_grad[tick_index - 1], from_above)
            in_list.append(incoming)
            mid_grad = fold_taps(project_taps(incoming, full_second), 1)
        pre_grad = mid_grad * relu_mask[0, tick_index].astype(jnp.float32)
        out_list.append(fold_taps(project_taps(pre_grad, full_first), 2))
        pre_list.append(pre_grad)
    data_grad = jnp.stack(out_list, axis=0)[None]
    mean_scale = 1.0 / (tick_count * act_in.shape[2] * lax.axis_size("dp"))
    first_patches = flat_patches(act_in[0], 2)
    second_patches = flat_patches(act_mid[0], 1)
    pre_rows = jnp.stack(pre_list, axis=0).reshape(-1, channels)
    in_rows = jnp.stack(in_list, axis=0).reshape(-1, channels)
    summed = lax.psum_scatter(
        jnp.concatenate(
            [
                correlate(first_patches, pre_rows, mean_scale),
                correlate(second_patches, in_rows, mean_scale),
            ],
            axis=1,
        ),
        "dp",
        scatter_dimension=0,
        tiled=True,
    )
    first_grad = summed[:, :channels]
    second_grad = summed[:, channels:]
    return (data_grad, first_grad[None], second_grad[None])


def solution(mesh):
    return jax.shard_map(
        local,
        mesh=mesh,
        in_specs=(
            P("section", None, "dp", None, None, None),
            P("section", None, "dp", None, None, None),
            P("section", None, "dp", None, None, None),
            P("section", "dp", None, None, None),
            P(None, "dp", None, None, None),
            P("section", "dp", None),
            P("section", "dp", None),
        ),
        out_specs=(
            P("section", None, "dp", None, None, None),
            P("section", "dp", None),
            P("section", "dp", None),
        ),
        check_vma=False,
    )
```

profile of v0, /device:TPU:0, one launch (start us, length us, event | category | flops | bytes accessed | tf_op | source)
XLA Modules:
  0.0 164.2 jit_solution(3687185264678643865)
XLA Ops:
  8.7 1.3 copy.89
  10.0 2.1 %reduce.1 = f32[2,15,15,256]{3,2,1,0:T(8,128)S(1)} reduce(f32[1,2,1,15,15,256]{5,2,4,3,1,0:T(1,128)} %param.8, f32[]{:T(128)} %constant.31), dimensions={0,2}, to_apply=%param.8.reduce_sub_computation | reduce | bytes 921604 | tf_op args[1]
  12.1 2.0 %copy.90 = f32[1,2,1,15,15,256]{5,1,4,3,2,0:T(2,128)} copy(f32[1,2,1,15,15,256]{5,2,4,3,1,0:T(1,128)} %param.7) | data formatting | bytes 921600 | tf_op args[0]
  14.1 1.1 reduce
  15.2 1.7 %pad_slice_fusion.24 = (f32[2,15,15,256]{3,0,2,1:T(2,128)}, f32[2,15,15,256]{3,0,2,1:T(2,128)S(1)}, f32[2,15,15,256]{3,0,2,1:T(2,128)S(1)}, f32[2,15,15,256]{3,0...) fusion(f32[2,15,15,256]{3,0,2,1:T(2,128)S(1)} %bitcast.67), kind=kLoop, calls=%fused_computation.40 | loop fusion | bytes 3225600 | tf_op jit(solution)/shard_map/slice | solution.py:19
  17.5 1.1 copy.52
  19.4 1.1 copy.53
  21.4 1.6 %copy.54 = f32[1,1,15,15,256]{4,3,2,1,0:T(8,128)} copy(f32[1,1,15,15,256]{4,1,3,2,0:T(1,128)} %param.10) | data formatting | bytes 460800 | tf_op args[3]
  23.0 4.2 %pad_slice_fusion.30 = (f32[2,15,15,256]{3,0,2,1:T(2,128)}, f32[2,15,15,256]{3,0,2,1:T(2,128)}, f32[2,15,15,256]{3,0,2,1:T(2,128)}, f32[2,15,15,256]{3,0,2,1:T(2...) fusion(f32[2,15,15,256]{3,0,2,1:T(2,128)} %bitcast.66), kind=kLoop, calls=%fused_computation.46 | loop fusion | bytes 3225600 | tf_op jit(solution)/shard_map/slice | solution.py:19
  28.1 1.1 copy.42
  30.0 1.2 copy.43
  32.8 1.1 copy.44
  34.8 1.1 copy.45
  38.5 1.9 %constant_dynamic-update-slice_fusion.6 = f32[450,1792]{1,0:T(8,128)} fusion(f32[450,256]{1,0:T(8,128)} %concatenate.39), kind=kLoop, calls=%fused_computation.96 | loop fusion | bytes 927744
  48.7 1.0 fusion.39
  49.8 3.2 %convolution_bitcast_fusion.3 = f32[1,15,15,1792]{3,2,1,0:T(8,128)S(1)} fusion(f32[1,1792,256]{2,1,0:T(8,128)} %all-gather.5.cloned.1.call-done, f32[1,1,15,15,256]{4,1,3,2,0:T(1,128)S(1)} %copy-done.17), kind=kOutput, calls=%fused_computation.30 | convolution fusion | flops 1238630400 | bytes 3678208 | tf_op jit(solution)/shard_map/nhwc,kc->nhwk/dot_general | solution.py:38
  53.1 15.0 %all-gather.7.cloned.1.call-done = f32[1,1792,256]{2,1,0:T(8,128)} async-done(((f32[1,224,256]{2,1,0:T(8,128)}), f32[1,1792,256]{2,1,0:T(8,128)}) %all-gather.7.cloned.1.call-update) | async-done | bytes 1835024 | tf_op jit(solution)/shard_map/all_gather | solution.py:55
  68.1 3.3 %convolution_bitcast_fusion.2 = f32[1,15,15,1792]{3,2,1,0:T(8,128)S(1)} fusion(f32[1,1792,256]{2,1,0:T(8,128)} %all-gather.7.cloned.1.call-done, f32[1,15,15,256]{3,2,1,0:T(8,128)S(1)} %fusion.10), kind=kOutput, calls=%fused_computation.29 | convolution fusion | flops 1238630400 | bytes 3678208 | tf_op jit(solution)/shard_map/nhwc,kc->nhwk/dot_general | solution.py:38
  71.6 1.6 collective-permute-start
  73.2 0.9 constant_dynamic-update-slice_fusion.1
  75.0 6.8 %collective-permute-done = f32[1,15,15,256]{3,2,1,0:T(8,128)S(1)} collective-permute-done((f32[1,15,15,256]{3,2,1,0:T(8,128)S(1)}, f32[1,15,15,256]{3,2,1,0:T(8,128)S(1)}, u32[]{:S(2)}, u32[]{:S(2)}) %collective-permute-start) | collective-permute-done | bytes 230432 | tf_op jit(solution)/shard_map/ppermute | solution.py:10
  83.3 1.9 %reshape.78 = f32[450,256]{1,0:T(8,128)} reshape(f32[2,1,15,15,256]{4,3,2,1,0:T(8,128)} %pad_maximum_fusion.2) | data formatting | bytes 921600 | tf_op jit(solution)/shard_map/reshape | solution.py:77
  85.2 2.8 %convolution_bitcast_fusion.1 = f32[1,15,15,1792]{3,2,1,0:T(8,128)S(1)} fusion(f32[1,1792,256]{2,1,0:T(8,128)S(1)} %copy-done.1, f32[1,15,15,256]{3,2,1,0:T(8,128)} %copy-done.18, f32[1,15,15,256]{3,0,2,1:T(1,128)} %bitcast.70, pred[]{:T(512)S(6)} %eq.3), kind=kOutput, calls=%fused_computation.28 | convolution fusion | flops 1238688000 | bytes 3908609 | tf_op jit(solution)/shard_map/nhwc,kc->nhwk/dot_general | solution.py:38
  89.0 5.2 %convolution_multiply_fusion = f32[1792,256]{0,1:T(8,128)S(1)} fusion(f32[450,1792]{1,0:T(8,128)} %constant_dynamic-update-slice_fusion.7, f32[450,256]{1,0:T(8,128)S(1)} %copy-done.13), kind=kOutput, calls=%fused_computation.25 | convolution fusion | flops 2477719552 | bytes 5521408 | tf_op jit(solution)/shard_map/rk,rc->kc/dot_general | solution.py:47
  94.2 5.3 %convolution_multiply_fusion.1 = f32[1792,256]{0,1:T(8,128)S(1)} fusion(f32[450,1792]{1,0:T(8,128)} %constant_dynamic-update-slice_fusion, f32[450,256]{1,0:T(8,128)S(1)} %reshape.77), kind=kOutput, calls=%fused_computation.26 | convolution fusion | flops 2477719552 | bytes 5521408 | tf_op jit(solution)/shard_map/rk,rc->kc/dot_general | solution.py:47
  99.4 2.1 %pad_maximum_fusion = f32[1792,512]{0,1:T(8,128)} fusion(f32[1792,256]{0,1:T(8,128)S(1)} %convolution_multiply_fusion, f32[1792,256]{0,1:T(8,128)S(1)} %convolution_multiply_fusion.1), kind=kLoop, calls=%fused_computation.12 | loop fusion | flops 917504 | bytes 7340032 | tf_op jit(solution)/shard_map/concatenate | solution.py:79
  101.5 5.1 %copy.58 = f32[1792,512]{1,0:T(8,128)} copy(f32[1792,512]{0,1:T(8,128)} %pad_maximum_fusion) | data formatting | bytes 7340032
  106.9 1.3 copy-done
  108.2 2.6 %convolution_bitcast_fusion = f32[1,15,15,1792]{3,2,1,0:T(8,128)S(1)} fusion(f32[1,1792,256]{2,1,0:T(8,128)S(1)} %copy-done, f32[1,15,15,256]{3,2,1,0:T(8,128)} %copy-done.4), kind=kOutput, calls=%fused_computation.27 | convolution fusion | flops 1238630400 | bytes 3678208 | tf_op jit(solution)/shard_map/nhwc,kc->nhwk/dot_general | solution.py:38
  111.0 1.2 copy.55
  112.3 42.4 %reduce-scatter.4.cloned.1.call-done = f32[224,512]{1,0:T(8,128)} async-done(((f32[1792,512]{1,0:T(8,128)}), f32[224,512]{1,0:T(8,128)}) %reduce-scatter.4.cloned.1.call-update) | async-done | bytes 458768
  154.7 1.1 fusion.40
  (96 shorter events, 24.9 us)
Async XLA Ops:
  7.2 7.0 %copy-start.14 = (f32[1,2,1,15,15,256]{5,2,4,3,1,0:T(1,128)S(1)}, f32[1,2,1,15,15,256]{5,2,4,3,1,0:T(1,128)}, u32[]{:S(2)}) copy-start(f32[1,2,1,15,15,256]{5,2,4,3,1,0:T(1,128)} %param.7) | copy-start | bytes 1382404
  7.2 42.6 %all-gather.5.cloned.1.call-start = ((), (), s32[]{:S(2)}) async-start(), calls=%async_computation.1 | async-start | bytes 2064384 | tf_op jit(solution)/shard_map/all_gather | solution.py:56
  7.9 60.2 %all-gather.7.cloned.1.call-start = ((), (), s32[]{:S(2)}) async-start(), calls=%async_computation.2 | async-start | bytes 2064384 | tf_op jit(solution)/shard_map/all_gather | solution.py:55
  8.7 146.0 %reduce-scatter.4.cloned.1.call-start = ((), (), s32[]{:S(2)}) async-start(), calls=%async_computation.3 | async-start | bytes 4128768
  32.0 4.7 %copy-start.15 = (f32[2,15,15,256]{3,0,2,1:T(2,128)S(1)}, f32[2,15,15,256]{3,0,2,1:T(2,128)}, u32[]{:S(2)}) copy-start(f32[2,15,15,256]{3,0,2,1:T(2,128)} %get-tuple-element.12) | copy-start | bytes 1382404
  36.8 7.0 %copy-start.6 = (f32[450,256]{1,0:T(8,128)S(1)}, f32[450,256]{1,0:T(8,128)}, u32[]{:S(2)}) copy-start(f32[450,256]{1,0:T(8,128)} %concatenate.52) | copy-start | bytes 1382404
  37.6 6.9 %copy-start.8 = (f32[450,256]{1,0:T(8,128)S(1)}, f32[450,256]{1,0:T(8,128)}, u32[]{:S(2)}) copy-start(f32[450,256]{1,0:T(8,128)} %concatenate.53) | copy-start | bytes 1382404
  38.5 6.9 %copy-start.9 = (f32[450,256]{1,0:T(8,128)S(1)}, f32[450,256]{1,0:T(8,128)}, u32[]{:S(2)}) copy-start(f32[450,256]{1,0:T(8,128)} %concatenate.40) | copy-start | bytes 1382404
  40.4 5.8 %copy-start.11 = (f32[450,256]{1,0:T(8,128)S(1)}, f32[450,256]{1,0:T(8,128)}, u32[]{:S(2)}) copy-start(f32[450,256]{1,0:T(8,128)} %concatenate.41) | copy-start | bytes 1382404
  41.2 5.8 %copy-start.10 = (f32[450,256]{1,0:T(8,128)S(1)}, f32[450,256]{1,0:T(8,128)}, u32[]{:S(2)}) copy-start(f32[450,256]{1,0:T(8,128)} %concatenate.42) | copy-start | bytes 1382404
  42.1 5.8 %copy-start.12 = (f32[450,256]{1,0:T(8,128)S(1)}, f32[450,256]{1,0:T(8,128)}, u32[]{:S(2)}) copy-start(f32[450,256]{1,0:T(8,128)} %concatenate.43) | copy-start | bytes 1382404
  42.9 5.8 %copy-start.21 = (s32[1,2,1,15,15,256]{5,2,4,3,1,0:T(1,128)S(1)}, s32[1,2,1,15,15,256]{5,2,4,3,1,0:T(1,128)}, u32[]{:S(2)}) copy-start(s32[1,2,1,15,15,256]{5,2,4,3,1,0:T(1,128)} %param.9) | copy-start | bytes 1382404
  43.7 6.0 %copy-start.17 = (f32[1,1,15,15,256]{4,1,3,2,0:T(1,128)S(1)}, f32[1,1,15,15,256]{4,1,3,2,0:T(1,128)}, u32[]{:S(2)}) copy-start(f32[1,1,15,15,256]{4,1,3,2,0:T(1,128)} %param.10) | copy-start | bytes 691204
  53.1 15.1 %copy-start.2 = (f32[1,15,15,256]{3,2,1,0:T(8,128)}, f32[1,15,15,256]{3,2,1,0:T(8,128)S(1)}, u32[]{:S(2)}) copy-start(f32[1,15,15,256]{3,2,1,0:T(8,128)S(1)} %fusion.10) | copy-start | bytes 691204
  68.1 5.1 %copy-start.5 = (f32[450,256]{1,0:T(8,128)S(1)}, f32[450,256]{1,0:T(8,128)}, u32[]{:S(2)}) copy-start(f32[450,256]{1,0:T(8,128)} %concatenate.44) | copy-start | bytes 1382404
  68.1 6.0 %copy-start.7 = (f32[450,256]{1,0:T(8,128)S(1)}, f32[450,256]{1,0:T(8,128)}, u32[]{:S(2)}) copy-start(f32[450,256]{1,0:T(8,128)} %concatenate.45) | copy-start | bytes 1382404
  68.1 13.6 %copy-start.16 = (f32[1,1,15,15,256]{4,1,3,2,0:T(1,128)S(1)}, f32[1,1,15,15,256]{4,1,3,2,0:T(1,128)}, u32[]{:S(2)}) copy-start(f32[1,1,15,15,256]{4,1,3,2,0:T(1,128)} %param.11) | copy-start | bytes 691204
  71.4 11.0 %copy-start.19 = (f32[1,1,15,15,256]{4,3,2,1,0:T(8,128)S(1)}, f32[1,1,15,15,256]{4,3,2,1,0:T(8,128)}, u32[]{:S(2)}) copy-start(f32[1,1,15,15,256]{4,3,2,1,0:T(8,128)} %copy.54) | copy-start | bytes 691204
  71.4 13.7 %copy-start.1 = (f32[1,1792,256]{2,1,0:T(8,128)S(1)}, f32[1,1792,256]{2,1,0:T(8,128)}, u32[]{:S(2)}) copy-start(f32[1,1792,256]{2,1,0:T(8,128)} %all-gather.5.cloned.1.call-done) | copy-start | bytes 5505028
  71.6 10.2 %collective-permute-start = (f32[1,15,15,256]{3,2,1,0:T(8,128)S(1)}, f32[1,15,15,256]{3,2,1,0:T(8,128)S(1)}, u32[]{:S(2)}, u32[]{:S(2)}) collective-permute-start(f32[1,15,15,256]{3,2,1,0:T(8,128)S(1)} %fusion.23), channel_id=1, source_target_pairs={{8,0},{16,8},{24,16},{9,1},{17,9},{25,17},{10,2},{18,10},{26,18},{... | collective-permute-start | bytes 691208 | tf_op jit(solution)/shard_map/ppermute | solution.py:10
  81.8 0.7 copy-start.18
  85.2 2.8 %copy-start.20 = (s32[1,1,1,15,15,256]{5,2,4,3,1,0:T(1,128)S(1)}, s32[1,1,1,15,15,256]{5,2,4,3,1,0:T(1,128)}, u32[]{:S(2)}) copy-start(s32[1,1,1,15,15,256]{5,2,4,3,1,0:T(1,128)} %get-tuple-element.24) | copy-start | bytes 691204
  85.2 3.6 %copy-start.3 = (f32[1,15,15,256]{3,2,1,0:T(8,128)S(1)}, f32[1,15,15,256]{3,2,1,0:T(8,128)}, u32[]{:S(2)}) copy-start(f32[1,15,15,256]{3,2,1,0:T(8,128)} %copy-done.2) | copy-start | bytes 691204
  88.0 1.0 copy-start.13
  88.1 0.7 copy-start.4
  106.7 1.5 copy-start
Sparse Core Ops, SparseCore 0:
  9.9 29.4 all-gather.4
  41.3 26.7 all-gather.6
  106.8 47.7 reduce-scatter.3
where the time goes:
time: 165 us; the launch traced here: 164 us
  waiting for transfers between devices  65.6 us (40%)
  local copies, waits for them, and re-layouts  53.4 us (32%)
  matrix products  22.3 us (14%)
  between operations  14.1 us (9%)
  other arithmetic  7.04 us (4%)
  starting transfers between devices  1.72 us (1%)
    unnamed x4, waiting for transfers between devices  43.8 us
    unnamed x65, local copies, waits for them, and re-layouts  27.1 us
    all_gather x1, waiting for transfers between devices, local(): lax.all_gather(w_first[0], 'dp', axis=0, tiled=True)  15 us
    slice x14, local copies, waits for them, and re-layouts, spread_taps(): lax.slice_in_dim(padded, offset, offset + extent, axis=spatial)  12.7 us
    dot_general x4, matrix products, project_taps(): jnp.einsum('nhwc,kc->nhwk', values, weight, precision=lax.Precision.HIGHEST)  11.9 us
    dot_general x2, matrix products, correlate(): jnp.einsum('rk,rc->kc', patches, grad_rows, precision=lax.Precision.HIGHEST)  10.4 us
    concatenate x16, local copies, waits for them, and re-layouts, spread_taps(): return jnp.concatenate(pieces, axis=-1)  9.54 us
    ppermute x1, waiting for transfers between devices, shifted(): return lax.ppermute(shard, axis, pairs)  6.81 us
  transfers between devices with their start and end apart: 4, of which 3 were waited for; matrix products, arithmetic and copies ran while one was open for 31% of the time, Pallas kernels for 0%

commit v1 on v0

v1 whole, which is shorter than its diff:
```python
import functools

import jax
import jax.numpy as jnp
from jax import lax
from jax.experimental import pallas as pl
from jax.experimental.pallas import tpu as pltpu
from jax.sharding import PartitionSpec as P

TAPS = 7
REACH = TAPS // 2
GROUP = 16
LANES = 128
F32 = jnp.float32
BF16 = jnp.bfloat16
NT = (((1,), (1,)), ((), ()))
NN = (((1,), (0,)), ((), ()))
VMEM = pl.BlockSpec(memory_space=pltpu.VMEM)
SMEM = pl.BlockSpec(memory_space=pltpu.SMEM)


def call(kernel, out_shapes, scratch, flops, *operands, scalars=0):
    moved = sum(x.size * x.dtype.itemsize for x in operands)
    moved += sum(s.size * s.dtype.itemsize for s in out_shapes)
    return pl.pallas_call(
        kernel,
        out_shape=out_shapes,
        in_specs=[SMEM] * scalars + [VMEM] * (len(operands) - scalars),
        out_specs=[VMEM] * len(out_shapes),
        scratch_shapes=scratch,
        compiler_params=pltpu.CompilerParams(vmem_limit_bytes=40 * 1024 * 1024),
        cost_estimate=pl.CostEstimate(flops=flops, bytes_accessed=moved, transcendentals=0),
    )(*operands)


def split(value):
    high = value.astype(BF16)
    return high, (value - high.astype(F32)).astype(BF16)


def padded_rows(rows):
    return rows + 2 * REACH * GROUP


def fill(rows_ref, high_ref, low_ref):
    rows, channels = rows_ref.shape
    edge = REACH * GROUP
    border = jnp.zeros((edge, channels), BF16)
    high, low = split(rows_ref[...])
    for ref, body in ((high_ref, high), (low_ref, low)):
        ref[pl.ds(0, edge), :] = border
        ref[pl.ds(edge, rows), :] = body
        ref[pl.ds(edge + rows, edge), :] = border


def dot(a, b, dims):
    return lax.dot_general(a, b, dims, preferred_element_type=F32)


def window(ref, tap, rows):
    return ref[pl.ds((TAPS - 1 - tap) * GROUP, rows), :]


def convolve(high_ref, low_ref, w_high, w_low, rows):
    channels = w_high.shape[0] // TAPS
    total = jnp.zeros((rows, channels), F32)
    for tap in range(TAPS):
        taken = pl.ds(tap * channels, channels)
        high, low = window(high_ref, tap, rows), window(low_ref, tap, rows)
        total += dot(high, w_high[taken, :], NT)
        total += dot(low, w_high[taken, :], NT)
        total += dot(high, w_low[taken, :], NT)
    return total


def regroup(source_ref, out_ref, groups, members):
    tail = jnp.zeros((GROUP - groups, out_ref.shape[-1]), F32)
    for member in range(members):
        for lane in range(source_ref.shape[0]):
            taken = source_ref[lane, pl.ds(member, groups, stride=GROUP), :]
            out_ref[pl.ds(member * GROUP, groups), lane * LANES : (lane + 1) * LANES] = taken
        out_ref[pl.ds(member * GROUP + groups, GROUP - groups), :] = tail


def place(starts_ref, pieces, w_high, w_low):
    for index, piece in enumerate(pieces):
        high, low = split(piece[...])
        taken = pl.ds(pl.multiple_of(starts_ref[index], GROUP), piece.shape[0])
        w_high[taken, :] = high
        w_low[taken, :] = low


def conv_kernel(piece_count, masked, members, *refs):
    refs = list(refs)
    if piece_count:
        starts = refs.pop(0)
    rows_ref = refs.pop(0)
    mask_ref = refs.pop(0) if masked else None
    if piece_count:
        pieces = [refs.pop(0) for _ in range(piece_count)]
        out_ref, w_high, w_low, high, low, flat = refs
        place(starts, pieces, w_high, w_low)
    else:
        w_high, w_low, out_ref, high, low, flat = refs
    rows = rows_ref.shape[0]
    fill(rows_ref, high, low)
    total = convolve(high, low, w_high, w_low, rows)
    if masked:
        total = total * mask_ref[...].astype(F32)
    for lane in range(flat.shape[0]):
        flat[lane] = total[:, lane * LANES : (lane + 1) * LANES]
    regroup(flat, out_ref, rows // GROUP, members)


def conv(rows, mask, members, weights=None, pieces=None):
    count, channels = rows.shape
    filter_rows = TAPS * channels
    out = [jax.ShapeDtypeStruct((members * GROUP, channels), F32)]
    operands, scalars = [rows], 0
    if mask is not None:
        operands.append(mask)
    if pieces is not None:
        starts, parts = pieces
        out += [jax.ShapeDtypeStruct((filter_rows, channels), BF16)] * 2
        operands = [starts] + operands + parts
        scalars = 1
    else:
        operands += weights
    scratch = [
        pltpu.VMEM((padded_rows(count), channels), BF16),
        pltpu.VMEM((padded_rows(count), channels), BF16),
        pltpu.VMEM((channels // LANES, count, LANES), F32),
    ]
    piece_count = 0 if pieces is None else len(pieces[1])
    kernel = functools.partial(conv_kernel, piece_count, mask is not None, members)
    result = call(kernel, out, scratch, 6 * count * filter_rows * channels, *operands, scalars=scalars)
    return result if pieces is not None else result[0]


def turn_kernel(in_ref, mid_ref, *outs):
    for ref, high, low in ((in_ref, outs[0], outs[1]), (mid_ref, outs[2], outs[3])):
        for tick in range(ref.shape[0]):
            taken_high, taken_low = split(ref[tick].T)
            high[tick] = taken_high
            low[tick] = taken_low


def turned(act_in, act_mid):
    out = []
    for act in (act_in, act_mid):
        out += [jax.ShapeDtypeStruct((act.shape[0], act.shape[2], act.shape[1]), BF16)] * 2
    return call(turn_kernel, out, [], 0, act_in, act_mid)


def correlate_kernel(scale, carried, *refs):
    if carried:
        act_high, act_low, rows_ref, before, out_ref, high, low = refs
    else:
        act_high, act_low, rows_ref, out_ref, high, low = refs
    fill(rows_ref, high, low)
    rows, channels = rows_ref.shape
    for tap in range(TAPS):
        taken = pl.ds(tap * channels, channels)
        here_high, here_low = window(high, tap, rows), window(low, tap, rows)
        total = dot(act_high[...], here_high, NN)
        total += dot(act_low[...], here_high, NN)
        total += dot(act_high[...], here_low, NN)
        total *= scale
        if carried:
            total += before[taken, :]
        out_ref[taken, :] = total


def correlate(act_high, act_low, rows, scale, before=None):
    count, channels = rows.shape
    out = [jax.ShapeDtypeStruct((TAPS * channels, channels), F32)]
    scratch = [pltpu.VMEM((padded_rows(count), channels), BF16)] * 2
    operands = [act_high, act_low, rows] + ([] if before is None else [before])
    kernel = functools.partial(correlate_kernel, scale, before is not None)
    return call(kernel, out, scratch, 6 * count * TAPS * channels * channels, *operands)[0]


def by_row(values):
    spare = GROUP - values.shape[-2]
    values = jnp.pad(values, [(0, 0)] * (values.ndim - 2) + [(0, spare), (0, 0)])
    return values.reshape(values.shape[:-3] + (-1, values.shape[-1]))


def by_column(values):
    return by_row(jnp.swapaxes(values, -3, -2))


def swap(shard, bit):
    peers = lax.axis_size("dp")
    return lax.ppermute(shard, "dp", [(i, i ^ bit) for i in range(peers)])


def four_chips():
    return lax.axis_size("dp") == 8


def gather(shards):
    if not four_chips():
        wholes = [lax.all_gather(shard, "dp", axis=0, tiled=True) for shard in shards]
        return [(jnp.zeros((1,), jnp.int32), [whole]) for whole in wholes]
    me = lax.axis_index("dp")
    first = [(swap(shard, 2), swap(shard, 4)) for shard in shards]
    result = []
    for shard, (by_x, by_y) in zip(shards, first):
        rows = shard.shape[0]
        half = rows // 2
        far_a = swap(by_x[:half], 4)
        far_b = swap(by_y[half:], 2)
        own = [(shard, 0, 0), (by_x, 2, 0), (by_y, 4, 0), (far_a, 6, 0), (far_b, 6, half)]
        pieces = own + [(swap(piece, 1), bits ^ 1, offset) for piece, bits, offset in own]
        starts = jnp.stack([(me ^ bits) * rows + offset for _, bits, offset in pieces])
        result.append((starts.astype(jnp.int32), [piece for piece, _, _ in pieces]))
    return result


def scatter(partial):
    if not four_chips():
        return lax.psum_scatter(partial, "dp", scatter_dimension=0, tiled=True)
    me = lax.axis_index("dp")
    rows = partial.shape[0] // 8
    half = rows // 2

    def block(bits):
        return lax.dynamic_slice_in_dim(partial, (me ^ bits) * rows, rows, axis=0)

    sent = swap(jnp.stack([block(bits) for bits in (1, 3, 5, 7)]), 1)
    kept = jnp.stack([block(bits) for bits in (0, 2, 4, 6)])
    chip = kept + sent
    a, b = chip[:, :half], chip[:, half:]
    a_there = swap(jnp.stack([a[1], a[3]]), 2)
    b_there = swap(jnp.stack([b[2], b[3]]), 4)
    a_near, a_far = a[0] + a_there[0], a[2] + a_there[1]
    b_near, b_far = b[0] + b_there[0], b[1] + b_there[1]
    a_last = swap(a_far, 4)
    b_last = swap(b_far, 2)
    return jnp.concatenate([a_near + a_last, b_near + b_last], axis=0)


def local(act_in, act_mid, relu_mask, arriving, loss_grad, w_first, w_second):
    ticks, images, height, width = act_in.shape[1:5]
    sections = lax.axis_size("section")
    is_last = lax.axis_index("section") == sections - 1
    scale = 1.0 / (ticks * images * lax.axis_size("dp"))
    second_pieces, first_pieces = gather([w_second[0], w_first[0]])
    in_high, in_low, mid_high, mid_low = turned(by_column(act_in[0, :, 0]), by_row(act_mid[0, :, 0]))
    mask = by_row(relu_mask[0, :, 0])
    loss = by_row(loss_grad[:, 0])
    incoming = by_row(arriving[0, 0])
    second = correlate(mid_high[0], mid_low[0], incoming, scale)
    pre, *w_second_parts = conv(incoming, mask[0], width, pieces=second_pieces)
    out, *w_first_parts = conv(pre, None, height, pieces=first_pieces)
    outs = [out]
    first = correlate(in_high[0], in_low[0], pre, scale)
    for tick in range(1, ticks):
        pairs = [(i, i - 1) for i in range(1, sections)]
        above = lax.ppermute(outs[-1], "section", pairs)
        incoming = jnp.where(is_last, loss[tick - 1], above)
        second = correlate(mid_high[tick], mid_low[tick], incoming, scale, second)
        pre = conv(incoming, mask[tick], width, weights=w_second_parts)
        first = correlate(in_high[tick], in_low[tick], pre, scale, first)
        outs.append(conv(pre, None, height, weights=w_first_parts))
    second_grad = scatter(second)
    first_grad = scatter(first)
    data_grad = jnp.stack(outs).reshape(ticks, height, GROUP, -1)[:, :, :width]
    return data_grad[None, :, None], first_grad[None], second_grad[None]


def solution(mesh):
    return jax.shard_map(
        local,
        mesh=mesh,
        in_specs=(
            P("section", None, "dp", None, None, None),
            P("section", None, "dp", None, None, None),
            P("section", None, "dp", None, None, None),
            P("section", "dp", None, None, None),
            P(None, "dp", None, None, None),
            P("section", "dp", None),
            P("section", "dp", None),
        ),
        out_specs=(
            P("section", None, "dp", None, None, None),
            P("section", "dp", None),
            P("section", "dp", None),
        ),
        check_vma=False,
    )
```

time: 165 us -> 80.4 us (0.49)
  local copies, waits for them, and re-layouts: 53.4 us -> 12.6 us
  waiting for transfers between devices: 65.6 us -> 30 us
  matrix products: 22.3 us -> 0 us
  starting transfers between devices: 1.72 us -> 23.6 us
  between operations: 14.1 us -> 1.26 us
  Pallas kernels: 0 us -> 10.3 us
  other arithmetic: 7.04 us -> 2.4 us
    unnamed x4 -> x0, waiting for transfers between devices: 43.8 us -> none
    ppermute x1 -> x29, waiting for transfers between devices: 6.81 us -> 30 us  [the longest x28 22.2 us: swap(): return lax.ppermute(shard, 'dp', [(i, i ^ bit) for i in range(peers)])]
    dot_general x6 -> x0, matrix products: 22.3 us -> none  [the longest x4 11.9 us: project_taps(): jnp.einsum('nhwc,kc->nhwk', values, weight, precision=lax.Precision.HIGHEST)]
    ppermute x1 -> x29, starting transfers between devices: 1.6 us -> 23.6 us  [the longest x28 22 us: swap(): return lax.ppermute(shard, 'dp', [(i, i ^ bit) for i in range(peers)])]
    unnamed x65 -> x42, local copies, waits for them, and re-layouts: 27.1 us -> 10.1 us
    all_gather x2 -> x0, waiting for transfers between devices: 15 us -> none  [the longest x1 15 us: local(): lax.all_gather(w_first[0], 'dp', axis=0, tiled=True)]
    slice x16 -> x7, local copies, waits for them, and re-layouts: 14.8 us -> 0.57 us  [the longest x1 0.5 us: local(): pre = conv(incoming, mask[tick], width, weights=w_second_parts)]
    pallas_call x0 -> x9, Pallas kernels: none -> 10.3 us  [call(): pl.pallas_call(kernel, out_shape=out_shapes, in_specs=[SMEM] * scalars +...]
  transfers between devices with their start and end apart: 4 -> 29, of which waited for: 3 -> 13; matrix products, arithmetic and copies ran while one was open for 31% -> 10% of each run, Pallas kernels for 0% -> 7%
where the time goes in v1:
time: 80.4 us; the launch traced here: 80.1 us
  waiting for transfers between devices  30 us (37%)
  starting transfers between devices  23.6 us (29%)
  local copies, waits for them, and re-layouts  12.6 us (16%)
  Pallas kernels  10.3 us (13%)
  other arithmetic  2.4 us (3%)
  between operations  1.26 us (2%)
    ppermute x28, waiting for transfers between devices, swap(): return lax.ppermute(shard, 'dp', [(i, i ^ bit) for i in range(peers)])  22.2 us
    ppermute x28, starting transfers between devices, swap(): return lax.ppermute(shard, 'dp', [(i, i ^ bit) for i in range(peers)])  22 us
    pallas_call x9, Pallas kernels, call(): pl.pallas_call(kernel, out_shape=out_shapes, in_specs=[SMEM] * scalars +...  10.3 us
    unnamed x42, local copies, waits for them, and re-layouts  10.1 us
    ppermute x1, waiting for transfers between devices, local(): above = lax.ppermute(outs[-1], 'section', pairs)  7.77 us
    broadcast_in_dim x3, other arithmetic, local(): return (data_grad[None, :, None], first_grad[None], second_grad[None])  1.82 us
  transfers between devices with their start and end apart: 29, of which 13 were waited for; matrix products, arithmetic and copies ran while one was open for 10% of the time, Pallas kernels for 7%

profile of v1, /device:TPU:0, one launch (start us, length us, event | category | flops | bytes accessed | tf_op | source)
XLA Modules:
  0.0 80.1 jit_solution(15253273292880602802)
XLA Ops:
  0.6 3.0 %collective-permute-start = (f32[224,256]{1,0:T(8,128)}, f32[224,256]{1,0:T(8,128)S(1)}, u32[]{:S(2)}, u32[]{:S(2)}) collective-permute-start(f32[224,256]{1,0:T(8,128)} %bitcast.122), channel_id=1, source_target_pairs={{0,2},{1,3},{2,0},{3,1},{4,6},{5,7},{6,4},{7,5},{8,10},{9,11},{10,... | collective-permute-start | bytes 688136 | tf_op jit(solution)/shard_map/ppermute | solution.py:195
  3.6 1.5 %collective-permute-start.1 = (f32[224,256]{1,0:T(8,128)}, f32[224,256]{1,0:T(8,128)S(1)}, u32[]{:S(2)}, u32[]{:S(2)}) collective-permute-start(f32[224,256]{1,0:T(8,128)} %bitcast.123), channel_id=1, source_target_pairs={{0,4},{1,5},{2,6},{3,7},{4,0},{5,1},{6,2},{7,3},{8,12},{9,13},{10,... | collective-permute-start | bytes 688136 | tf_op jit(solution)/shard_map/ppermute | solution.py:195
  5.8 4.5 %collective-permute-done.refs_4_ = f32[224,256]{1,0:T(8,128)S(1)} collective-permute-done((f32[224,256]{1,0:T(8,128)}, f32[224,256]{1,0:T(8,128)S(1)}, u32[]{:S(2)}, u32[]{:S(2)}) %collective-permute-start) | collective-permute-done | bytes 229408 | tf_op jit(solution)/shard_map/ppermute | solution.py:195
  10.3 2.1 %collective-permute-start.2 = (f32[112,256]{1,0:T(8,128)S(1)}, f32[112,256]{1,0:T(8,128)S(1)}, u32[]{:S(2)}, u32[]{:S(2)}) collective-permute-start(f32[112,256]{1,0:T(8,128)S(1)} %slice.168), channel_id=1, source_target_pairs={{0,4},{1,5},{2,6},{3,7},{4,0},{5,1},{6,2},{7,3},{8,12},{9,13},{10,... | collective-permute-start | bytes 344072 | tf_op jit(solution)/shard_map/ppermute | solution.py:195
  12.5 1.9 %collective-permute-done.9.refs_3_ = f32[224,256]{1,0:T(8,128)S(1)} collective-permute-done((f32[224,256]{1,0:T(8,128)}, f32[224,256]{1,0:T(8,128)S(1)}, u32[]{:S(2)}, u32[]{:S(2)}) %collective-permute-start.9) | collective-permute-done | bytes 229408 | tf_op jit(solution)/shard_map/ppermute | solution.py:195
  14.4 1.8 %collective-permute-start.3 = (f32[112,256]{1,0:T(8,128)S(1)}, f32[112,256]{1,0:T(8,128)S(1)}, u32[]{:S(2)}, u32[]{:S(2)}) collective-permute-start(f32[112,256]{1,0:T(8,128)S(1)} %slice.169), channel_id=1, source_target_pairs={{0,2},{1,3},{2,0},{3,1},{4,6},{5,7},{6,4},{7,5},{8,10},{9,11},{10,... | collective-permute-start | bytes 344072 | tf_op jit(solution)/shard_map/ppermute | solution.py:195
  17.1 1.5 %collective-permute-start.11 = (f32[112,256]{1,0:T(8,128)S(1)}, f32[112,256]{1,0:T(8,128)}, u32[]{:S(2)}, u32[]{:S(2)}) collective-permute-start(f32[112,256]{1,0:T(8,128)S(1)} %slice.170), channel_id=1, source_target_pairs={{0,4},{1,5},{2,6},{3,7},{4,0},{5,1},{6,2},{7,3},{8,12},{9,13},{10,... | collective-permute-start | bytes 344072 | tf_op jit(solution)/shard_map/ppermute | solution.py:195
  20.0 1.9 %collective-permute-done.11.refs_5_ = f32[112,256]{1,0:T(8,128)} collective-permute-done((f32[112,256]{1,0:T(8,128)S(1)}, f32[112,256]{1,0:T(8,128)}, u32[]{:S(2)}, u32[]{:S(2)}) %collective-permute-start.11) | collective-permute-done | bytes 114720 | tf_op jit(solution)/shard_map/ppermute | solution.py:195
  22.0 1.6 %collective-permute-done.12.refs_6_ = f32[112,256]{1,0:T(8,128)} collective-permute-done((f32[112,256]{1,0:T(8,128)S(1)}, f32[112,256]{1,0:T(8,128)}, u32[]{:S(2)}, u32[]{:S(2)}) %collective-permute-start.12) | collective-permute-done | bytes 114720 | tf_op jit(solution)/shard_map/ppermute | solution.py:195
  24.2 1.3 %copy.32 = s32[1,2,1,15,15,256]{5,1,4,3,2,0:T(2,128)S(1)} copy(s32[1,2,1,15,15,256]{5,2,4,3,1,0:T(1,128)} %param.9) | data formatting | bytes 921600 | tf_op args[2]
  29.1 1.3 %copy.30 = f32[1,2,1,15,15,256]{5,1,4,3,2,0:T(2,128)S(1)} copy(f32[1,2,1,15,15,256]{5,2,4,3,1,0:T(1,128)} %param.8) | data formatting | bytes 921600 | tf_op args[1]
  31.0 0.9 %copy-done.3 = f32[224,256]{1,0:T(8,128)S(1)} copy-done((f32[224,256]{1,0:T(8,128)S(1)}, f32[224,256]{1,0:T(8,128)}, u32[]{:S(2)}) %copy-start.3) | copy-done | bytes 229400
  31.9 0.9 %copy-done.5 = f32[224,256]{1,0:T(8,128)S(1)} copy-done((f32[224,256]{1,0:T(8,128)S(1)}, f32[224,256]{1,0:T(8,128)}, u32[]{:S(2)}) %copy-start.5) | copy-done | bytes 229400
  32.9 0.9 %copy-done.7 = f32[112,256]{1,0:T(8,128)S(1)} copy-done((f32[112,256]{1,0:T(8,128)S(1)}, f32[112,256]{1,0:T(8,128)}, u32[]{:S(2)}) %copy-start.7) | copy-done | bytes 114712
  33.8 0.9 %copy-done.9 = f32[112,256]{1,0:T(8,128)S(1)} copy-done((f32[112,256]{1,0:T(8,128)S(1)}, f32[112,256]{1,0:T(8,128)}, u32[]{:S(2)}) %copy-start.9) | copy-done | bytes 114712
  34.7 0.9 %copy-done.11 = f32[112,256]{1,0:T(8,128)S(1)} copy-done((f32[112,256]{1,0:T(8,128)S(1)}, f32[112,256]{1,0:T(8,128)}, u32[]{:S(2)}) %copy-start.11) | copy-done | bytes 114712
  35.6 1.8 %shard_map.94 = (f32[240,256]{1,0:T(8,128)S(1)}, bf16[1792,256]{1,0:T(8,128)(2,1)S(1)}, bf16[1792,256]{1,0:T(8,128)(2,1)S(1)}) custom-call(s32[10]{0:T(128)S(1)} %stack.135.refs_0_, f32[240,256]{1,0:T(8,128)S(1)} %bitcast.117, s32[240,256]{1,0:T(8,128)S(1)} %bitcast.120, f32[224,256]{1,0:T(8,128)S(1)} %bitcast.125, ...), custom_call_target="tpu_custom_call" | custom-call | flops 660602880 | bytes 4407336 | tf_op jit(solution)/shard_map/pallas_call | solution.py:25
  37.5 2.6 %shard_map.95 = (f32[240,256]{1,0:T(8,128)S(1)}, bf16[1792,256]{1,0:T(8,128)(2,1)S(1)}, bf16[1792,256]{1,0:T(8,128)(2,1)S(1)}) custom-call(s32[10]{0:T(128)S(1)} %stack.135.refs_0_, f32[240,256]{1,0:T(8,128)S(1)} %get-tuple-element.13.refs_1_.refs_2_, f32[224,256]{1,0:T(8,128)S(1)} %bitcast.129, f32[224,256]{1,0:T(8,128)S(1)} %collective-permute-done.9.refs_3_, ...), custom_call_target="tpu_custom_call" | custom-call | flops 660602880 | bytes 4161576 | tf_op jit(solution)/shard_map/pallas_call | solution.py:25
  40.1 1.6 %collective-permute-start.18 = (f32[240,256]{1,0:T(8,128)S(1)}, f32[240,256]{1,0:T(8,128)S(1)}, u32[]{:S(2)}, u32[]{:S(2)}) collective-permute-start(f32[240,256]{1,0:T(8,128)S(1)} %get-tuple-element.14), channel_id=1, source_target_pairs={{8,0},{16,8},{24,16},{9,1},{17,9},{25,17},{10,2},{18,10},{26,18},{... | collective-permute-start | bytes 737288 | tf_op jit(solution)/shard_map/ppermute | solution.py:261
  42.7 7.8 %collective-permute-done.18 = f32[240,256]{1,0:T(8,128)S(1)} collective-permute-done((f32[240,256]{1,0:T(8,128)S(1)}, f32[240,256]{1,0:T(8,128)S(1)}, u32[]{:S(2)}, u32[]{:S(2)}) %collective-permute-start.18) | collective-permute-done | bytes 245792 | tf_op jit(solution)/shard_map/ppermute | solution.py:261
  50.5 1.0 %shard_map.96.refs_0_.refs_2_ = f32[240,256]{1,0:T(8,128)S(1)} custom-call(f32[240,256]{1,0:T(8,128)S(1)} %bitcast_select_fusion.refs_0_.refs_2_, s32[240,256]{1,0:T(8,128)S(1)} %bitcast.116, bf16[1792,256]{1,0:T(8,128)(2,1)S(1)} %get-tuple-element.15.refs_2_, bf16[1792,256]{1,0:T(8,128)(2,1)S(1)} %get-tuple-element.16.refs_3_), custom_call_target="tpu_custom_call" | custom-call | flops 660602880 | bytes 2572288 | tf_op jit(solution)/shard_map/pallas_call | solution.py:25
  55.6 1.0 %shard_map.97 = f32[240,256]{1,0:T(8,128)S(1)} custom-call(f32[240,256]{1,0:T(8,128)S(1)} %shard_map.96.refs_0_.refs_2_, bf16[1792,256]{1,0:T(8,128)(2,1)S(1)} %get-tuple-element.17.refs_1_, bf16[1792,256]{1,0:T(8,128)(2,1)S(1)} %get-tuple-element.18.refs_2_), custom_call_target="tpu_custom_call" | custom-call | flops 660602880 | bytes 2326528 | tf_op jit(solution)/shard_map/pallas_call | solution.py:25
  57.3 1.2 %copy.18 = f32[1,2,1,15,15,256]{5,2,4,3,1,0:T(1,128)} copy(f32[1,2,1,15,15,256]{5,1,4,3,2,0:T(2,128)S(1)} %fusion) | data formatting | bytes 921600
  59.6 1.5 %collective-permute-start.22 = (f32[2,112,256]{2,1,0:T(8,128)S(1)}, f32[2,112,256]{2,1,0:T(8,128)S(1)}, u32[]{:S(2)}, u32[]{:S(2)}) collective-permute-start(f32[2,112,256]{2,1,0:T(8,128)S(1)} %stack.163), channel_id=1, source_target_pairs={{0,4},{1,5},{2,6},{3,7},{4,0},{5,1},{6,2},{7,3},{8,12},{9,13},{10,... | collective-permute-start | bytes 688136 | tf_op jit(solution)/shard_map/ppermute | solution.py:195
  61.3 0.9 %collective-permute-start.25 = (f32[2,112,256]{2,1,0:T(8,128)S(1)}, f32[2,112,256]{2,1,0:T(8,128)S(1)}, u32[]{:S(2)}, u32[]{:S(2)}) collective-permute-start(f32[2,112,256]{2,1,0:T(8,128)S(1)} %pad_maximum_fusion.4), channel_id=1, source_target_pairs={{0,2},{1,3},{2,0},{3,1},{4,6},{5,7},{6,4},{7,5},{8,10},{9,11},{10,... | collective-permute-start | bytes 688136 | tf_op jit(solution)/shard_map/ppermute | solution.py:195
  63.1 4.1 %collective-permute-done.20 = f32[2,112,256]{2,1,0:T(8,128)S(1)} collective-permute-done((f32[2,112,256]{2,1,0:T(8,128)S(1)}, f32[2,112,256]{2,1,0:T(8,128)S(1)}, u32[]{:S(2)}, u32[]{:S(2)}) %collective-permute-start.20) | collective-permute-done | bytes 229408 | tf_op jit(solution)/shard_map/ppermute | solution.py:195
  68.1 1.6 %collective-permute-start.21 = (f32[112,256]{1,0:T(8,128)S(1)}, f32[112,256]{1,0:T(8,128)S(1)}, u32[]{:S(2)}, u32[]{:S(2)}) collective-permute-start(f32[112,256]{1,0:T(8,128)S(1)} %get-tuple-element.50), channel_id=1, source_target_pairs={{0,4},{1,5},{2,6},{3,7},{4,0},{5,1},{6,2},{7,3},{8,12},{9,13},{10,... | collective-permute-start | bytes 344072 | tf_op jit(solution)/shard_map/ppermute | solution.py:195
  69.7 0.9 %collective-permute-start.23 = (f32[112,256]{1,0:T(8,128)S(1)}, f32[112,256]{1,0:T(8,128)S(1)}, u32[]{:S(2)}, u32[]{:S(2)}) collective-permute-start(f32[112,256]{1,0:T(8,128)S(1)} %get-tuple-element.51), channel_id=1, source_target_pairs={{0,2},{1,3},{2,0},{3,1},{4,6},{5,7},{6,4},{7,5},{8,10},{9,11},{10,... | collective-permute-start | bytes 344072 | tf_op jit(solution)/shard_map/ppermute | solution.py:195
  70.6 1.6 %collective-permute-done.25 = f32[2,112,256]{2,1,0:T(8,128)S(1)} collective-permute-done((f32[2,112,256]{2,1,0:T(8,128)S(1)}, f32[2,112,256]{2,1,0:T(8,128)S(1)}, u32[]{:S(2)}, u32[]{:S(2)}) %collective-permute-start.25) | collective-permute-done | bytes 229408 | tf_op jit(solution)/shard_map/ppermute | solution.py:195
  73.0 1.6 %collective-permute-start.26 = (f32[112,256]{1,0:T(8,128)S(1)}, f32[112,256]{1,0:T(8,128)S(1)}, u32[]{:S(2)}, u32[]{:S(2)}) collective-permute-start(f32[112,256]{1,0:T(8,128)S(1)} %get-tuple-element.44), channel_id=1, source_target_pairs={{0,4},{1,5},{2,6},{3,7},{4,0},{5,1},{6,2},{7,3},{8,12},{9,13},{10,... | collective-permute-start | bytes 344072 | tf_op jit(solution)/shard_map/ppermute | solution.py:195
  76.2 1.6 %collective-permute-done.26 = f32[112,256]{1,0:T(8,128)S(1)} collective-permute-done((f32[112,256]{1,0:T(8,128)S(1)}, f32[112,256]{1,0:T(8,128)S(1)}, u32[]{:S(2)}, u32[]{:S(2)}) %collective-permute-start.26) | collective-permute-done | bytes 114720 | tf_op jit(solution)/shard_map/ppermute | solution.py:195
  77.8 1.5 %collective-permute-done.28 = f32[112,256]{1,0:T(8,128)S(1)} collective-permute-done((f32[112,256]{1,0:T(8,128)S(1)}, f32[112,256]{1,0:T(8,128)S(1)}, u32[]{:S(2)}, u32[]{:S(2)}) %collective-permute-start.28) | collective-permute-done | bytes 114720 | tf_op jit(solution)/shard_map/ppermute | solution.py:195
  (111 shorter events, 19.3 us)
Async XLA Ops:
  0.6 27.2 %copy-start.14 = (f32[1,1,15,15,256]{4,1,3,2,0:T(1,128)S(1)}, f32[1,1,15,15,256]{4,1,3,2,0:T(1,128)}, u32[]{:S(2)}) copy-start(f32[1,1,15,15,256]{4,1,3,2,0:T(1,128)} %param.10) | copy-start | bytes 691204
  0.6 9.6 %collective-permute-start = (f32[224,256]{1,0:T(8,128)}, f32[224,256]{1,0:T(8,128)S(1)}, u32[]{:S(2)}, u32[]{:S(2)}) collective-permute-start(f32[224,256]{1,0:T(8,128)} %bitcast.122), channel_id=1, source_target_pairs={{0,2},{1,3},{2,0},{3,1},{4,6},{5,7},{6,4},{7,5},{8,10},{9,11},{10,... | collective-permute-start | bytes 688136 | tf_op jit(solution)/shard_map/ppermute | solution.py:195
  3.6 8.8 %collective-permute-start.1 = (f32[224,256]{1,0:T(8,128)}, f32[224,256]{1,0:T(8,128)S(1)}, u32[]{:S(2)}, u32[]{:S(2)}) collective-permute-start(f32[224,256]{1,0:T(8,128)} %bitcast.123), channel_id=1, source_target_pairs={{0,4},{1,5},{2,6},{3,7},{4,0},{5,1},{6,2},{7,3},{8,12},{9,13},{10,... | collective-permute-start | bytes 688136 | tf_op jit(solution)/shard_map/ppermute | solution.py:195
  5.2 9.2 %collective-permute-start.9 = (f32[224,256]{1,0:T(8,128)}, f32[224,256]{1,0:T(8,128)S(1)}, u32[]{:S(2)}, u32[]{:S(2)}) collective-permute-start(f32[224,256]{1,0:T(8,128)} %bitcast.126), channel_id=1, source_target_pairs={{0,2},{1,3},{2,0},{3,1},{4,6},{5,7},{6,4},{7,5},{8,10},{9,11},{10,... | collective-permute-start | bytes 688136 | tf_op jit(solution)/shard_map/ppermute | solution.py:195
  5.7 8.7 %collective-permute-start.4 = (f32[224,256]{1,0:T(8,128)}, f32[224,256]{1,0:T(8,128)S(1)}, u32[]{:S(2)}, u32[]{:S(2)}) collective-permute-start(f32[224,256]{1,0:T(8,128)} %bitcast.124), channel_id=1, source_target_pairs={{0,1},{1,0},{2,3},{3,2},{4,5},{5,4},{6,7},{7,6},{8,9},{9,8},{10,11... | collective-permute-start | bytes 688136 | tf_op jit(solution)/shard_map/ppermute | solution.py:195
  5.7 11.4 %collective-permute-start.10 = (f32[224,256]{1,0:T(8,128)}, f32[224,256]{1,0:T(8,128)S(1)}, u32[]{:S(2)}, u32[]{:S(2)}) collective-permute-start(f32[224,256]{1,0:T(8,128)} %bitcast.127), channel_id=1, source_target_pairs={{0,4},{1,5},{2,6},{3,7},{4,0},{5,1},{6,2},{7,3},{8,12},{9,13},{10,... | collective-permute-start | bytes 688136 | tf_op jit(solution)/shard_map/ppermute | solution.py:195
  10.3 17.6 %copy-start.15 = (f32[1,1,15,15,256]{4,1,3,2,0:T(1,128)S(1)}, f32[1,1,15,15,256]{4,1,3,2,0:T(1,128)}, u32[]{:S(2)}) copy-start(f32[1,1,15,15,256]{4,1,3,2,0:T(1,128)} %param.11) | copy-start | bytes 691204
  10.3 8.3 %collective-permute-start.2 = (f32[112,256]{1,0:T(8,128)S(1)}, f32[112,256]{1,0:T(8,128)S(1)}, u32[]{:S(2)}, u32[]{:S(2)}) collective-permute-start(f32[112,256]{1,0:T(8,128)S(1)} %slice.168), channel_id=1, source_target_pairs={{0,4},{1,5},{2,6},{3,7},{4,0},{5,1},{6,2},{7,3},{8,12},{9,13},{10,... | collective-permute-start | bytes 344072 | tf_op jit(solution)/shard_map/ppermute | solution.py:195
  12.5 11.1 %collective-permute-start.5 = (f32[224,256]{1,0:T(8,128)S(1)}, f32[224,256]{1,0:T(8,128)S(1)}, u32[]{:S(2)}, u32[]{:S(2)}) collective-permute-start(f32[224,256]{1,0:T(8,128)S(1)} %collective-permute-done.refs_4_), channel_id=1, source_target_pairs={{0,1},{1,0},{2,3},{3,2},{4,5},{5,4},{6,7},{7,6},{8,9},{9,8},{10,11... | collective-permute-start | bytes 688136 | tf_op jit(solution)/shard_map/ppermute | solution.py:195
  14.4 9.7 %collective-permute-start.6 = (f32[224,256]{1,0:T(8,128)S(1)}, f32[224,256]{1,0:T(8,128)S(1)}, u32[]{:S(2)}, u32[]{:S(2)}) collective-permute-start(f32[224,256]{1,0:T(8,128)S(1)} %collective-permute-done.1.refs_5_), channel_id=1, source_target_pairs={{0,1},{1,0},{2,3},{3,2},{4,5},{5,4},{6,7},{7,6},{8,9},{9,8},{10,11... | collective-permute-start | bytes 688136 | tf_op jit(solution)/shard_map/ppermute | solution.py:195
  14.4 5.6 %collective-permute-start.3 = (f32[112,256]{1,0:T(8,128)S(1)}, f32[112,256]{1,0:T(8,128)S(1)}, u32[]{:S(2)}, u32[]{:S(2)}) collective-permute-start(f32[112,256]{1,0:T(8,128)S(1)} %slice.169), channel_id=1, source_target_pairs={{0,2},{1,3},{2,0},{3,1},{4,6},{5,7},{6,4},{7,5},{8,10},{9,11},{10,... | collective-permute-start | bytes 344072 | tf_op jit(solution)/shard_map/ppermute | solution.py:195
  17.1 4.9 %collective-permute-start.11 = (f32[112,256]{1,0:T(8,128)S(1)}, f32[112,256]{1,0:T(8,128)}, u32[]{:S(2)}, u32[]{:S(2)}) collective-permute-start(f32[112,256]{1,0:T(8,128)S(1)} %slice.170), channel_id=1, source_target_pairs={{0,4},{1,5},{2,6},{3,7},{4,0},{5,1},{6,2},{7,3},{8,12},{9,13},{10,... | collective-permute-start | bytes 344072 | tf_op jit(solution)/shard_map/ppermute | solution.py:195
  18.6 5.0 %collective-permute-start.12 = (f32[112,256]{1,0:T(8,128)S(1)}, f32[112,256]{1,0:T(8,128)}, u32[]{:S(2)}, u32[]{:S(2)}) collective-permute-start(f32[112,256]{1,0:T(8,128)S(1)} %slice.171), channel_id=1, source_target_pairs={{0,2},{1,3},{2,0},{3,1},{4,6},{5,7},{6,4},{7,5},{8,10},{9,11},{10,... | collective-permute-start | bytes 344072 | tf_op jit(solution)/shard_map/ppermute | solution.py:195
  20.0 5.4 %collective-permute-start.7 = (f32[112,256]{1,0:T(8,128)S(1)}, f32[112,256]{1,0:T(8,128)S(1)}, u32[]{:S(2)}, u32[]{:S(2)}) collective-permute-start(f32[112,256]{1,0:T(8,128)S(1)} %collective-permute-done.2.refs_6_), channel_id=1, source_target_pairs={{0,1},{1,0},{2,3},{3,2},{4,5},{5,4},{6,7},{7,6},{8,9},{9,8},{10,11... | collective-permute-start | bytes 344072 | tf_op jit(solution)/shard_map/ppermute | solution.py:195
  22.0 4.6 %collective-permute-start.8 = (f32[112,256]{1,0:T(8,128)S(1)}, f32[112,256]{1,0:T(8,128)S(1)}, u32[]{:S(2)}, u32[]{:S(2)}) collective-permute-start(f32[112,256]{1,0:T(8,128)S(1)} %collective-permute-done.3.refs_7_), channel_id=1, source_target_pairs={{0,1},{1,0},{2,3},{3,2},{4,5},{5,4},{6,7},{7,6},{8,9},{9,8},{10,11... | collective-permute-start | bytes 344072 | tf_op jit(solution)/shard_map/ppermute | solution.py:195
  23.6 13.8 %collective-permute-start.13 = (f32[224,256]{1,0:T(8,128)}, f32[224,256]{1,0:T(8,128)}, u32[]{:S(2)}, u32[]{:S(2)}) collective-permute-start(f32[224,256]{1,0:T(8,128)} %bitcast.128), channel_id=1, source_target_pairs={{0,1},{1,0},{2,3},{3,2},{4,5},{5,4},{6,7},{7,6},{8,9},{9,8},{10,11... | collective-permute-start | bytes 688136 | tf_op jit(solution)/shard_map/ppermute | solution.py:195
  23.6 13.8 %collective-permute-start.14 = (f32[224,256]{1,0:T(8,128)S(1)}, f32[224,256]{1,0:T(8,128)}, u32[]{:S(2)}, u32[]{:S(2)}) collective-permute-start(f32[224,256]{1,0:T(8,128)S(1)} %collective-permute-done.9.refs_3_), channel_id=1, source_target_pairs={{0,1},{1,0},{2,3},{3,2},{4,5},{5,4},{6,7},{7,6},{8,9},{9,8},{10,11... | collective-permute-start | bytes 688136 | tf_op jit(solution)/shard_map/ppermute | solution.py:195
  24.1 13.3 %collective-permute-start.15 = (f32[224,256]{1,0:T(8,128)S(1)}, f32[224,256]{1,0:T(8,128)}, u32[]{:S(2)}, u32[]{:S(2)}) collective-permute-start(f32[224,256]{1,0:T(8,128)S(1)} %collective-permute-done.10.refs_4_), channel_id=1, source_target_pairs={{0,1},{1,0},{2,3},{3,2},{4,5},{5,4},{6,7},{7,6},{8,9},{9,8},{10,11... | collective-permute-start | bytes 688136 | tf_op jit(solution)/shard_map/ppermute | solution.py:195
  26.1 11.3 %collective-permute-start.16 = (f32[112,256]{1,0:T(8,128)}, f32[112,256]{1,0:T(8,128)}, u32[]{:S(2)}, u32[]{:S(2)}) collective-permute-start(f32[112,256]{1,0:T(8,128)} %collective-permute-done.11.refs_5_), channel_id=1, source_target_pairs={{0,1},{1,0},{2,3},{3,2},{4,5},{5,4},{6,7},{7,6},{8,9},{9,8},{10,11... | collective-permute-start | bytes 344072 | tf_op jit(solution)/shard_map/ppermute | solution.py:195
  27.2 10.3 %collective-permute-start.17 = (f32[112,256]{1,0:T(8,128)}, f32[112,256]{1,0:T(8,128)}, u32[]{:S(2)}, u32[]{:S(2)}) collective-permute-start(f32[112,256]{1,0:T(8,128)} %collective-permute-done.12.refs_6_), channel_id=1, source_target_pairs={{0,1},{1,0},{2,3},{3,2},{4,5},{5,4},{6,7},{7,6},{8,9},{9,8},{10,11... | collective-permute-start | bytes 344072 | tf_op jit(solution)/shard_map/ppermute | solution.py:195
  40.1 10.3 %copy-start.12 = (f32[1,15,16,256]{3,2,0,1:T(8,128)S(1)}, f32[1,15,16,256]{3,2,0,1:T(8,128)}, u32[]{:S(2)}) copy-start(f32[1,15,16,256]{3,2,0,1:T(8,128)} %pad.21.clone) | copy-start | bytes 737284
  40.1 10.3 %collective-permute-start.18 = (f32[240,256]{1,0:T(8,128)S(1)}, f32[240,256]{1,0:T(8,128)S(1)}, u32[]{:S(2)}, u32[]{:S(2)}) collective-permute-start(f32[240,256]{1,0:T(8,128)S(1)} %get-tuple-element.14), channel_id=1, source_target_pairs={{8,0},{16,8},{24,16},{9,1},{17,9},{25,17},{10,2},{18,10},{26,18},{... | collective-permute-start | bytes 737288 | tf_op jit(solution)/shard_map/ppermute | solution.py:261
  52.6 5.9 %collective-permute-start.19 = (f32[4,224,256]{2,1,0:T(8,128)S(1)}, f32[4,224,256]{2,1,0:T(8,128)S(1)}, u32[]{:S(2)}, u32[]{:S(2)}) collective-permute-start(f32[4,224,256]{2,1,0:T(8,128)S(1)} %pad_maximum_fusion), channel_id=1, source_target_pairs={{0,1},{1,0},{2,3},{3,2},{4,5},{5,4},{6,7},{7,6},{8,9},{9,8},{10,11... | collective-permute-start | bytes 2752520 | tf_op jit(solution)/shard_map/ppermute | solution.py:195
  54.8 6.3 %collective-permute-start.24 = (f32[4,224,256]{2,1,0:T(8,128)S(1)}, f32[4,224,256]{2,1,0:T(8,128)S(1)}, u32[]{:S(2)}, u32[]{:S(2)}) collective-permute-start(f32[4,224,256]{2,1,0:T(8,128)S(1)} %pad_maximum_fusion.1), channel_id=1, source_target_pairs={{0,1},{1,0},{2,3},{3,2},{4,5},{5,4},{6,7},{7,6},{8,9},{9,8},{10,11... | collective-permute-start | bytes 2752520 | tf_op jit(solution)/shard_map/ppermute | solution.py:195
  58.7 8.5 %collective-permute-start.20 = (f32[2,112,256]{2,1,0:T(8,128)S(1)}, f32[2,112,256]{2,1,0:T(8,128)S(1)}, u32[]{:S(2)}, u32[]{:S(2)}) collective-permute-start(f32[2,112,256]{2,1,0:T(8,128)S(1)} %pad_maximum_fusion.3), channel_id=1, source_target_pairs={{0,2},{1,3},{2,0},{3,1},{4,6},{5,7},{6,4},{7,5},{8,10},{9,11},{10,... | collective-permute-start | bytes 688136 | tf_op jit(solution)/shard_map/ppermute | solution.py:195
  59.6 8.5 %collective-permute-start.22 = (f32[2,112,256]{2,1,0:T(8,128)S(1)}, f32[2,112,256]{2,1,0:T(8,128)S(1)}, u32[]{:S(2)}, u32[]{:S(2)}) collective-permute-start(f32[2,112,256]{2,1,0:T(8,128)S(1)} %stack.163), channel_id=1, source_target_pairs={{0,4},{1,5},{2,6},{3,7},{4,0},{5,1},{6,2},{7,3},{8,12},{9,13},{10,... | collective-permute-start | bytes 688136 | tf_op jit(solution)/shard_map/ppermute | solution.py:195
  61.3 10.9 %collective-permute-start.25 = (f32[2,112,256]{2,1,0:T(8,128)S(1)}, f32[2,112,256]{2,1,0:T(8,128)S(1)}, u32[]{:S(2)}, u32[]{:S(2)}) collective-permute-start(f32[2,112,256]{2,1,0:T(8,128)S(1)} %pad_maximum_fusion.4), channel_id=1, source_target_pairs={{0,2},{1,3},{2,0},{3,1},{4,6},{5,7},{6,4},{7,5},{8,10},{9,11},{10,... | collective-permute-start | bytes 688136 | tf_op jit(solution)/shard_map/ppermute | solution.py:195
  62.2 10.7 %collective-permute-start.27 = (f32[2,112,256]{2,1,0:T(8,128)S(1)}, f32[2,112,256]{2,1,0:T(8,128)S(1)}, u32[]{:S(2)}, u32[]{:S(2)}) collective-permute-start(f32[2,112,256]{2,1,0:T(8,128)S(1)} %stack.164), channel_id=1, source_target_pairs={{0,4},{1,5},{2,6},{3,7},{4,0},{5,1},{6,2},{7,3},{8,12},{9,13},{10,... | collective-permute-start | bytes 688136 | tf_op jit(solution)/shard_map/ppermute | solution.py:195
  68.1 7.3 %collective-permute-start.21 = (f32[112,256]{1,0:T(8,128)S(1)}, f32[112,256]{1,0:T(8,128)S(1)}, u32[]{:S(2)}, u32[]{:S(2)}) collective-permute-start(f32[112,256]{1,0:T(8,128)S(1)} %get-tuple-element.50), channel_id=1, source_target_pairs={{0,4},{1,5},{2,6},{3,7},{4,0},{5,1},{6,2},{7,3},{8,12},{9,13},{10,... | collective-permute-start | bytes 344072 | tf_op jit(solution)/shard_map/ppermute | solution.py:195
  69.7 5.8 %collective-permute-start.23 = (f32[112,256]{1,0:T(8,128)S(1)}, f32[112,256]{1,0:T(8,128)S(1)}, u32[]{:S(2)}, u32[]{:S(2)}) collective-permute-start(f32[112,256]{1,0:T(8,128)S(1)} %get-tuple-element.51), channel_id=1, source_target_pairs={{0,2},{1,3},{2,0},{3,1},{4,6},{5,7},{6,4},{7,5},{8,10},{9,11},{10,... | collective-permute-start | bytes 344072 | tf_op jit(solution)/shard_map/ppermute | solution.py:195
  73.0 4.9 %collective-permute-start.26 = (f32[112,256]{1,0:T(8,128)S(1)}, f32[112,256]{1,0:T(8,128)S(1)}, u32[]{:S(2)}, u32[]{:S(2)}) collective-permute-start(f32[112,256]{1,0:T(8,128)S(1)} %get-tuple-element.44), channel_id=1, source_target_pairs={{0,4},{1,5},{2,6},{3,7},{4,0},{5,1},{6,2},{7,3},{8,12},{9,13},{10,... | collective-permute-start | bytes 344072 | tf_op jit(solution)/shard_map/ppermute | solution.py:195
  74.6 4.8 %collective-permute-start.28 = (f32[112,256]{1,0:T(8,128)S(1)}, f32[112,256]{1,0:T(8,128)S(1)}, u32[]{:S(2)}, u32[]{:S(2)}) collective-permute-start(f32[112,256]{1,0:T(8,128)S(1)} %get-tuple-element.45), channel_id=1, source_target_pairs={{0,2},{1,3},{2,0},{3,1},{4,6},{5,7},{6,4},{7,5},{8,10},{9,11},{10,... | collective-permute-start | bytes 344072 | tf_op jit(solution)/shard_map/ppermute | solution.py:195
  (13 other events, 29.9 us)

commit v2 on v1

--- a/solution.py
+++ b/solution.py
@@ -195,58 +195,31 @@
     return lax.ppermute(shard, "dp", [(i, i ^ bit) for i in range(peers)])
 
 
-def four_chips():
-    return lax.axis_size("dp") == 8
-
-
-def gather(shards):
-    if not four_chips():
-        wholes = [lax.all_gather(shard, "dp", axis=0, tiled=True) for shard in shards]
-        return [(jnp.zeros((1,), jnp.int32), [whole]) for whole in wholes]
-    me = lax.axis_index("dp")
-    first = [(swap(shard, 2), swap(shard, 4)) for shard in shards]
-    result = []
-    for shard, (by_x, by_y) in zip(shards, first):
-        rows = shard.shape[0]
-        half = rows // 2
-        far_a = swap(by_x[:half], 4)
-        far_b = swap(by_y[half:], 2)
-        own = [(shard, 0, 0), (by_x, 2, 0), (by_y, 4, 0), (far_a, 6, 0), (far_b, 6, half)]
-        pieces = own + [(swap(piece, 1), bits ^ 1, offset) for piece, bits, offset in own]
-        starts = jnp.stack([(me ^ bits) * rows + offset for _, bits, offset in pieces])
-        result.append((starts.astype(jnp.int32), [piece for piece, _, _ in pieces]))
-    return result
-
-
-def scatter(partial):
-    if not four_chips():
-        return lax.psum_scatter(partial, "dp", scatter_dimension=0, tiled=True)
-    me = lax.axis_index("dp")
-    rows = partial.shape[0] // 8
-    half = rows // 2
-
-    def block(bits):
-        return lax.dynamic_slice_in_dim(partial, (me ^ bits) * rows, rows, axis=0)
-
-    sent = swap(jnp.stack([block(bits) for bits in (1, 3, 5, 7)]), 1)
-    kept = jnp.stack([block(bits) for bits in (0, 2, 4, 6)])
-    chip = kept + sent
-    a, b = chip[:, :half], chip[:, half:]
-    a_there = swap(jnp.stack([a[1], a[3]]), 2)
-    b_there = swap(jnp.stack([b[2], b[3]]), 4)
-    a_near, a_far = a[0] + a_there[0], a[2] + a_there[1]
-    b_near, b_far = b[0] + b_there[0], b[1] + b_there[1]
-    a_last = swap(a_far, 4)
-    b_last = swap(b_far, 2)
-    return jnp.concatenate([a_near + a_last, b_near + b_last], axis=0)
-
-
-def local(act_in, act_mid, relu_mask, arriving, loss_grad, w_first, w_second):
+def together(*values):
+    return lax.optimization_barrier(values)
+
+
+def starts_of(me, rows, pieces):
+    starts = jnp.stack([(me ^ bits) * rows + offset for _, bits, offset in pieces])
+    return starts.astype(jnp.int32), [piece for piece, _, _ in pieces]
+
+
+def with_sibling(pieces, sibling):
+    return pieces + [(piece, bits ^ 1, offset) for piece, (_, bits, offset) in zip(sibling, pieces)]
+
+
+def finish(outs, ticks, height, width):
+    return jnp.stack(outs).reshape(ticks, height, GROUP, -1)[:, :, :width][None, :, None]
+
+
+def local_any(act_in, act_mid, relu_mask, arriving, loss_grad, w_first, w_second):
     ticks, images, height, width = act_in.shape[1:5]
     sections = lax.axis_size("section")
     is_last = lax.axis_index("section") == sections - 1
     scale = 1.0 / (ticks * images * lax.axis_size("dp"))
-    second_pieces, first_pieces = gather([w_second[0], w_first[0]])
+    start = jnp.zeros((1,), jnp.int32)
+    first_pieces = (start, [lax.all_gather(w_first[0], "dp", axis=0, tiled=True)])
+    second_pieces = (start, [lax.all_gather(w_second[0], "dp", axis=0, tiled=True)])
     in_high, in_low, mid_high, mid_low = turned(by_column(act_in[0, :, 0]), by_row(act_mid[0, :, 0]))
     mask = by_row(relu_mask[0, :, 0])
     loss = by_row(loss_grad[:, 0])
@@ -257,17 +230,107 @@
     outs = [out]
     first = correlate(in_high[0], in_low[0], pre, scale)
     for tick in range(1, ticks):
-        pairs = [(i, i - 1) for i in range(1, sections)]
-        above = lax.ppermute(outs[-1], "section", pairs)
+        above = lax.ppermute(outs[-1], "section", [(i, i - 1) for i in range(1, sections)])
         incoming = jnp.where(is_last, loss[tick - 1], above)
         second = correlate(mid_high[tick], mid_low[tick], incoming, scale, second)
         pre = conv(incoming, mask[tick], width, weights=w_second_parts)
         first = correlate(in_high[tick], in_low[tick], pre, scale, first)
         outs.append(conv(pre, None, height, weights=w_first_parts))
-    second_grad = scatter(second)
-    first_grad = scatter(first)
-    data_grad = jnp.stack(outs).reshape(ticks, height, GROUP, -1)[:, :, :width]
-    return data_grad[None, :, None], first_grad[None], second_grad[None]
+    second_grad = lax.psum_scatter(second, "dp", scatter_dimension=0, tiled=True)
+    first_grad = lax.psum_scatter(first, "dp", scatter_dimension=0, tiled=True)
+    return finish(outs, ticks, height, width), first_grad[None], second_grad[None]
+
+
+def blocks(partial, me):
+    rows = partial.shape[0] // 8
+    kept, sent = (
+        jnp.stack([lax.dynamic_slice_in_dim(partial, (me ^ bits) * rows, rows, axis=0) for bits in group])
+        for group in ((0, 2, 4, 6), (1, 3, 5, 7))
+    )
+    return kept, sent
+
+
+def near_phase(chip):
+    half = chip.shape[1] // 2
+    a, b = chip[:, :half], chip[:, half:]
+    return a, b, swap(jnp.stack([a[1], a[3]]), 2), swap(jnp.stack([b[2], b[3]]), 4)
+
+
+def far_phase(a, b, a_there, b_there):
+    a_near, a_far = a[0] + a_there[0], a[2] + a_there[1]
+    b_near, b_far = b[0] + b_there[0], b[1] + b_there[1]
+    return a_near, b_near, swap(a_far, 4), swap(b_far, 2)
+
+
+def join(a_near, b_near, a_last, b_last):
+    return jnp.concatenate([a_near + a_last, b_near + b_last], axis=0)[None]
+
+
+def local_eight(act_in, act_mid, relu_mask, arriving, loss_grad, w_first, w_second):
+    ticks, images, height, width = act_in.shape[1:5]
+    sections = lax.axis_size("section")
+    is_last = lax.axis_index("section") == sections - 1
+    me = lax.axis_index("dp")
+    scale = 1.0 / (ticks * images * lax.axis_size("dp"))
+    one, two = w_first[0], w_second[0]
+    rows = one.shape[0]
+    half = rows // 2
+    x_two, y_two = swap(two, 2), swap(two, 4)
+    x_one, y_one = swap(one, 2), swap(one, 4)
+    s_two, s_one = swap(two, 1), swap(one, 1)
+    incoming = by_row(arriving[0, 0])
+    mid_rows = by_row(act_mid[0, :, 0])
+    in_rows = by_column(act_in[0, :, 0])
+    incoming, mid_rows, in_rows, x_two, y_two = together(incoming, mid_rows, in_rows, x_two, y_two)
+    ya_two, xb_two = swap(x_two[:half], 4), swap(y_two[half:], 2)
+    sx_two, sy_two = swap(x_two, 1), swap(y_two, 1)
+    in_high, in_low, mid_high, mid_low = turned(in_rows, mid_rows)
+    second = correlate(mid_high[0], mid_low[0], incoming, scale)
+    mask = by_row(relu_mask[0, :, 0])
+    loss = by_row(loss_grad[:, 0])
+    second, mask, loss, in_high, in_low, mid_high, mid_low, x_one, y_one = together(
+        second, mask, loss, in_high, in_low, mid_high, mid_low, x_one, y_one
+    )
+    ya_one, xb_one = swap(x_one[:half], 4), swap(y_one[half:], 2)
+    sx_one, sy_one = swap(x_one, 1), swap(y_one, 1)
+    sya_two, sxb_two = swap(ya_two, 1), swap(xb_two, 1)
+    own = [(two, 0, 0), (x_two, 2, 0), (y_two, 4, 0), (ya_two, 6, 0), (xb_two, 6, half)]
+    pieces = with_sibling(own, [s_two, sx_two, sy_two, sya_two, sxb_two])
+    pre, *w_second_parts = conv(incoming, mask[0], width, pieces=starts_of(me, rows, pieces))
+    sya_one, sxb_one = swap(ya_one, 1), swap(xb_one, 1)
+    own = [(one, 0, 0), (x_one, 2, 0), (y_one, 4, 0), (ya_one, 6, 0), (xb_one, 6, half)]
+    pieces = with_sibling(own, [s_one, sx_one, sy_one, sya_one, sxb_one])
+    out, *w_first_parts = conv(pre, None, height, pieces=starts_of(me, rows, pieces))
+    outs = [out]
+    first = correlate(in_high[0], in_low[0], pre, scale)
+    for tick in range(1, ticks):
+        above = lax.ppermute(outs[-1], "section", [(i, i - 1) for i in range(1, sections)])
+        above, first = together(above, first)
+        incoming = jnp.where(is_last, loss[tick - 1], above)
+        second = correlate(mid_high[tick], mid_low[tick], incoming, scale, second)
+        if tick < ticks - 1:
+            pre = conv(incoming, mask[tick], width, weights=w_second_parts)
+            first = correlate(in_high[tick], in_low[tick], pre, scale, first)
+            outs.append(conv(pre, None, height, weights=w_first_parts))
+    kept, sent = blocks(second, me)
+    other = swap(sent, 1)
+    pre = conv(incoming, mask[-1], width, weights=w_second_parts)
+    first = correlate(in_high[-1], in_low[-1], pre, scale, first)
+    first_kept, first_sent = blocks(first, me)
+    first_other = swap(first_sent, 1)
+    a, b, a_there, b_there = near_phase(kept + other)
+    first_a, first_b, first_a_there, first_b_there = near_phase(first_kept + first_other)
+    pre, a_there, b_there = together(pre, a_there, b_there)
+    last = far_phase(a, b, a_there, b_there)
+    outs.append(conv(pre, None, height, weights=w_first_parts))
+    data_grad = finish(outs, ticks, height, width)
+    data_grad, first_a_there, first_b_there = together(data_grad, first_a_there, first_b_there)
+    first_last = far_phase(first_a, first_b, first_a_there, first_b_there)
+    return data_grad, join(*first_last), join(*last)
+
+
+def local(*arguments):
+    return (local_eight if lax.axis_size("dp") == 8 else local_any)(*arguments)
 
 
 def solution(mesh):

time: 80.4 us -> 65.3 us (0.81)
  local copies, waits for them, and re-layouts: 12.6 us -> 6.04 us
  starting transfers between devices: 23.6 us -> 19.3 us
  waiting for transfers between devices: 30 us -> 26.6 us
    unnamed x42 -> x19, local copies, waits for them, and re-layouts: 10.1 us -> 4.73 us
    ppermute x28, starting transfers between devices: 22 us -> 17.8 us  [swap(): return lax.ppermute(shard, 'dp', [(i, i ^ bit) for i in range(peers)])]
    ppermute x28, waiting for transfers between devices: 22.2 us -> 18.8 us  [swap(): return lax.ppermute(shard, 'dp', [(i, i ^ bit) for i in range(peers)])]
  transfers between devices with their start and end apart: 29 -> 29, of which waited for: 13 -> 13; matrix products, arithmetic and copies ran while one was open for 10% -> 10% of each run, Pallas kernels for 7% -> 10%
where the time goes in v2:
time: 65.3 us; the launch traced here: 65.1 us
  waiting for transfers between devices  26.6 us (41%)
  starting transfers between devices  19.3 us (30%)
  Pallas kernels  9.52 us (15%)
  local copies, waits for them, and re-layouts  6.04 us (9%)
  other arithmetic  2.43 us (4%)
  between operations  1.19 us (2%)
    ppermute x28, waiting for transfers between devices, swap(): return lax.ppermute(shard, 'dp', [(i, i ^ bit) for i in range(peers)])  18.8 us
    ppermute x28, starting transfers between devices, swap(): return lax.ppermute(shard, 'dp', [(i, i ^ bit) for i in range(peers)])  17.8 us
    pallas_call x9, Pallas kernels, call(): pl.pallas_call(kernel, out_shape=out_shapes, in_specs=[SMEM] * scalars +...  9.52 us
    ppermute x1, waiting for transfers between devices, local_eight(): lax.ppermute(outs[-1], 'section', [(i, i - 1) for i in range(1, sections)])  7.81 us
    unnamed x19, local copies, waits for them, and re-layouts  4.73 us
    ppermute x1, starting transfers between devices, local_eight(): lax.ppermute(outs[-1], 'section', [(i, i - 1) for i in range(1, sections)])  1.47 us
    broadcast_in_dim x2, other arithmetic, join(): return jnp.concatenate([a_near + a_last, b_near + b_last], axis=0)[None]  1.41 us
  transfers between devices with their start and end apart: 29, of which 13 were waited for; matrix products, arithmetic and copies ran while one was open for 10% of the time, Pallas kernels for 10%

profile of v2, /device:TPU:0, one launch (start us, length us, event | category | flops | bytes accessed | tf_op | source)
XLA Modules:
  0.0 65.1 jit_solution(1339556038661541645)
XLA Ops:
  0.6 3.0 %collective-permute-start.1 = (f32[224,256]{1,0:T(8,128)}, f32[224,256]{1,0:T(8,128)S(1)}, u32[]{:S(2)}, u32[]{:S(2)}) collective-permute-start(f32[224,256]{1,0:T(8,128)} %bitcast.124), channel_id=1, source_target_pairs={{0,4},{1,5},{2,6},{3,7},{4,0},{5,1},{6,2},{7,3},{8,12},{9,13},{10,... | collective-permute-start | bytes 688136 | tf_op jit(solution)/shard_map/ppermute | solution.py:195
  3.7 1.5 %collective-permute-start = (f32[224,256]{1,0:T(8,128)}, f32[224,256]{1,0:T(8,128)S(1)}, u32[]{:S(2)}, u32[]{:S(2)}) collective-permute-start(f32[224,256]{1,0:T(8,128)} %bitcast.125), channel_id=1, source_target_pairs={{0,2},{1,3},{2,0},{3,1},{4,6},{5,7},{6,4},{7,5},{8,10},{9,11},{10,... | collective-permute-start | bytes 688136 | tf_op jit(solution)/shard_map/ppermute | solution.py:195
  5.8 1.0 %copy.33 = f32[1,1,15,15,256]{4,3,1,2,0:T(8,128)S(1)} copy(f32[1,1,15,15,256]{4,1,3,2,0:T(1,128)} %param.10) | data formatting | bytes 460800
  6.8 1.0 %copy.25 = f32[1,15,15,256]{3,2,0,1:T(8,128)S(1)} copy(f32[1,15,15,256]{3,0,2,1:T(1,128)} %bitcast.138) | data formatting | bytes 460800
  10.3 2.1 %collective-permute-done.refs_4_ = f32[224,256]{1,0:T(8,128)S(1)} collective-permute-done((f32[224,256]{1,0:T(8,128)}, f32[224,256]{1,0:T(8,128)S(1)}, u32[]{:S(2)}, u32[]{:S(2)}) %collective-permute-start) | collective-permute-done | bytes 229408 | tf_op jit(solution)/shard_map/ppermute | solution.py:195
  12.5 1.6 %collective-permute-start.5 = (f32[112,256]{1,0:T(8,128)S(1)}, f32[112,256]{1,0:T(8,128)S(1)}, u32[]{:S(2)}, u32[]{:S(2)}) collective-permute-start(f32[112,256]{1,0:T(8,128)S(1)} %slice.135), channel_id=1, source_target_pairs={{0,2},{1,3},{2,0},{3,1},{4,6},{5,7},{6,4},{7,5},{8,10},{9,11},{10,... | collective-permute-start | bytes 344072 | tf_op jit(solution)/shard_map/ppermute | solution.py:195
  14.5 0.9 %shard_map.95.refs_3_ = f32[1792,256]{1,0:T(8,128)S(1)} custom-call(bf16[256,240]{1,0:T(8,128)(2,1)S(1)} %get-tuple-element.105.refs_0_, bf16[256,240]{1,0:T(8,128)(2,1)S(1)} %get-tuple-element.104.refs_1_, f32[240,256]{1,0:T(8,128)S(1)} %bitcast.120), custom_call_target="tpu_custom_call" | custom-call | flops 660602880 | bytes 2326528 | tf_op jit(solution)/shard_map/pallas_call | solution.py:25
  15.4 0.8 %collective-permute-start.4 = (f32[112,256]{1,0:T(8,128)S(1)}, f32[112,256]{1,0:T(8,128)S(1)}, u32[]{:S(2)}, u32[]{:S(2)}) collective-permute-start(f32[112,256]{1,0:T(8,128)S(1)} %slice.134), channel_id=1, source_target_pairs={{0,4},{1,5},{2,6},{3,7},{4,0},{5,1},{6,2},{7,3},{8,12},{9,13},{10,... | collective-permute-start | bytes 344072 | tf_op jit(solution)/shard_map/ppermute | solution.py:195
  16.2 1.6 %collective-permute-start.12 = (f32[112,256]{1,0:T(8,128)S(1)}, f32[112,256]{1,0:T(8,128)S(1)}, u32[]{:S(2)}, u32[]{:S(2)}) collective-permute-start(f32[112,256]{1,0:T(8,128)S(1)} %slice.137), channel_id=1, source_target_pairs={{0,2},{1,3},{2,0},{3,1},{4,6},{5,7},{6,4},{7,5},{8,10},{9,11},{10,... | collective-permute-start | bytes 344072 | tf_op jit(solution)/shard_map/ppermute | solution.py:195
  18.7 2.0 %collective-permute-done.4.refs_6_ = f32[112,256]{1,0:T(8,128)S(1)} collective-permute-done((f32[112,256]{1,0:T(8,128)S(1)}, f32[112,256]{1,0:T(8,128)S(1)}, u32[]{:S(2)}, u32[]{:S(2)}) %collective-permute-start.4) | collective-permute-done | bytes 114720 | tf_op jit(solution)/shard_map/ppermute | solution.py:195
  21.2 2.2 %collective-permute-done.11.refs_5_ = f32[112,256]{1,0:T(8,128)S(1)} collective-permute-done((f32[112,256]{1,0:T(8,128)S(1)}, f32[112,256]{1,0:T(8,128)S(1)}, u32[]{:S(2)}, u32[]{:S(2)}) %collective-permute-start.11) | collective-permute-done | bytes 114720 | tf_op jit(solution)/shard_map/ppermute | solution.py:195
  24.6 1.8 %shard_map.96 = (f32[240,256]{1,0:T(8,128)S(1)}, bf16[1792,256]{1,0:T(8,128)(2,1)S(1)}, bf16[1792,256]{1,0:T(8,128)(2,1)S(1)}) custom-call(s32[10]{0:T(128)S(1)} %stack.135.refs_0_, f32[240,256]{1,0:T(8,128)S(1)} %bitcast.121, s32[240,256]{1,0:T(8,128)S(1)} %get-tuple-element.99.refs_2_, f32[224,256]{1,0:T(8,128)S(1)} %bitcast.127, ...), custom_call_target="tpu_custom_call" | custom-call | flops 660602880 | bytes 4407336 | tf_op jit(solution)/shard_map/pallas_call | solution.py:25
  26.5 1.8 %shard_map.97 = (f32[240,256]{1,0:T(8,128)S(1)}, bf16[1792,256]{1,0:T(8,128)(2,1)S(1)}, bf16[1792,256]{1,0:T(8,128)(2,1)S(1)}) custom-call(s32[10]{0:T(128)S(1)} %stack.135.refs_0_, f32[240,256]{1,0:T(8,128)S(1)} %get-tuple-element.45.refs_1_.refs_2_, f32[224,256]{1,0:T(8,128)S(1)} %bitcast.131, f32[224,256]{1,0:T(8,128)S(1)} %collective-permute-done.2.refs_3_, ...), custom_call_target="tpu_custom_call" | custom-call | flops 660602880 | bytes 4161576 | tf_op jit(solution)/shard_map/pallas_call | solution.py:25
  28.3 1.5 %collective-permute-start.18 = (f32[240,256]{1,0:T(8,128)S(1)}, f32[240,256]{1,0:T(8,128)S(1)}, u32[]{:S(2)}, u32[]{:S(2)}) collective-permute-start(f32[240,256]{1,0:T(8,128)S(1)} %get-tuple-element.48), channel_id=1, source_target_pairs={{8,0},{16,8},{24,16},{9,1},{17,9},{25,17},{10,2},{18,10},{26,18},{... | collective-permute-start | bytes 737288 | tf_op jit(solution)/shard_map/ppermute | solution.py:307
  29.8 0.9 %shard_map.98.refs_3_ = f32[1792,256]{1,0:T(8,128)S(1)} custom-call(bf16[256,240]{1,0:T(8,128)(2,1)S(1)} %get-tuple-element.103.refs_0_, bf16[256,240]{1,0:T(8,128)(2,1)S(1)} %get-tuple-element.101.refs_1_, f32[240,256]{1,0:T(8,128)S(1)} %get-tuple-element.45.refs_1_.refs_2_), custom_call_target="tpu_custom_call" | custom-call | flops 660602880 | bytes 2326528 | tf_op jit(solution)/shard_map/pallas_call | solution.py:25
  30.7 7.8 %collective-permute-done.18 = f32[240,256]{1,0:T(8,128)S(1)} collective-permute-done((f32[240,256]{1,0:T(8,128)S(1)}, f32[240,256]{1,0:T(8,128)S(1)}, u32[]{:S(2)}, u32[]{:S(2)}) %collective-permute-start.18) | collective-permute-done | bytes 245792 | tf_op jit(solution)/shard_map/ppermute | solution.py:307
  38.5 0.9 %shard_map.100 = f32[1792,256]{1,0:T(8,128)S(1)} custom-call(bf16[256,240]{1,0:T(8,128)(2,1)S(1)} %slice_bitcast_fusion.5.refs_0_, bf16[256,240]{1,0:T(8,128)(2,1)S(1)} %slice_bitcast_fusion.4.refs_1_, f32[240,256]{1,0:T(8,128)S(1)} %bitcast_select_fusion.refs_0_.refs_2_, f32[1792,256]{1,0:T(8,128)S(1)} %shard_map.95.refs_3_), custom_call_target="tpu_custom_call" | custom-call | flops 660602880 | bytes 4161536 | tf_op jit(solution)/shard_map/pallas_call | solution.py:25
  39.8 1.0 %shard_map.99.refs_0_.refs_2_ = f32[240,256]{1,0:T(8,128)S(1)} custom-call(f32[240,256]{1,0:T(8,128)S(1)} %bitcast_select_fusion.refs_0_.refs_2_, s32[240,256]{1,0:T(8,128)S(1)} %get-tuple-element.98.refs_1_, bf16[1792,256]{1,0:T(8,128)(2,1)S(1)} %get-tuple-element.53.refs_2_, bf16[1792,256]{1,0:T(8,128)(2,1)S(1)} %get-tuple-element.54.refs_3_), custom_call_target="tpu_custom_call" | custom-call | flops 660602880 | bytes 2572288 | tf_op jit(solution)/shard_map/pallas_call | solution.py:25
  40.8 0.9 %shard_map.102 = f32[1792,256]{1,0:T(8,128)S(1)} custom-call(bf16[256,240]{1,0:T(8,128)(2,1)S(1)} %get-tuple-element.102.refs_0_, bf16[256,240]{1,0:T(8,128)(2,1)S(1)} %get-tuple-element.100.refs_1_, f32[240,256]{1,0:T(8,128)S(1)} %shard_map.99.refs_0_.refs_2_, f32[1792,256]{1,0:T(8,128)S(1)} %shard_map.98.refs_3_), custom_call_target="tpu_custom_call" | custom-call | flops 660602880 | bytes 4161536 | tf_op jit(solution)/shard_map/pallas_call | solution.py:25
  43.0 1.5 %collective-permute-start.20 = (f32[2,112,256]{2,1,0:T(8,128)S(1)}, f32[2,112,256]{2,1,0:T(8,128)S(1)}, u32[]{:S(2)}, u32[]{:S(2)}) collective-permute-start(f32[2,112,256]{2,1,0:T(8,128)S(1)} %pad_maximum_fusion.3), channel_id=1, source_target_pairs={{0,2},{1,3},{2,0},{3,1},{4,6},{5,7},{6,4},{7,5},{8,10},{9,11},{10,... | collective-permute-start | bytes 688136 | tf_op jit(solution)/shard_map/ppermute | solution.py:195
  45.1 1.2 %collective-permute-start.23 = (f32[2,112,256]{2,1,0:T(8,128)S(1)}, f32[2,112,256]{2,1,0:T(8,128)S(1)}, u32[]{:S(2)}, u32[]{:S(2)}) collective-permute-start(f32[2,112,256]{2,1,0:T(8,128)S(1)} %pad_maximum_fusion.4), channel_id=1, source_target_pairs={{0,2},{1,3},{2,0},{3,1},{4,6},{5,7},{6,4},{7,5},{8,10},{9,11},{10,... | collective-permute-start | bytes 688136 | tf_op jit(solution)/shard_map/ppermute | solution.py:195
  46.3 1.0 %collective-permute-start.24 = (f32[2,112,256]{2,1,0:T(8,128)S(1)}, f32[2,112,256]{2,1,0:T(8,128)S(1)}, u32[]{:S(2)}, u32[]{:S(2)}) collective-permute-start(f32[2,112,256]{2,1,0:T(8,128)S(1)} %stack.164), channel_id=1, source_target_pairs={{0,4},{1,5},{2,6},{3,7},{4,0},{5,1},{6,2},{7,3},{8,12},{9,13},{10,... | collective-permute-start | bytes 688136 | tf_op jit(solution)/shard_map/ppermute | solution.py:195
  47.4 4.1 %collective-permute-done.20 = f32[2,112,256]{2,1,0:T(8,128)S(1)} collective-permute-done((f32[2,112,256]{2,1,0:T(8,128)S(1)}, f32[2,112,256]{2,1,0:T(8,128)S(1)}, u32[]{:S(2)}, u32[]{:S(2)}) %collective-permute-start.20) | collective-permute-done | bytes 229408 | tf_op jit(solution)/shard_map/ppermute | solution.py:195
  51.5 1.5 %collective-permute-done.21 = f32[2,112,256]{2,1,0:T(8,128)S(1)} collective-permute-done((f32[2,112,256]{2,1,0:T(8,128)S(1)}, f32[2,112,256]{2,1,0:T(8,128)S(1)}, u32[]{:S(2)}, u32[]{:S(2)}) %collective-permute-start.21) | collective-permute-done | bytes 229408 | tf_op jit(solution)/shard_map/ppermute | solution.py:195
  53.0 1.0 %shard_map.101 = f32[240,256]{1,0:T(8,128)S(1)} custom-call(f32[240,256]{1,0:T(8,128)S(1)} %shard_map.99.refs_0_.refs_2_, bf16[1792,256]{1,0:T(8,128)(2,1)S(1)} %get-tuple-element.59.refs_1_, bf16[1792,256]{1,0:T(8,128)(2,1)S(1)} %get-tuple-element.60.refs_2_), custom_call_target="tpu_custom_call" | custom-call | flops 660602880 | bytes 2326528 | tf_op jit(solution)/shard_map/pallas_call | solution.py:25
  54.7 0.7 %collective-permute-start.28 = (f32[112,256]{1,0:T(8,128)S(1)}, f32[112,256]{1,0:T(8,128)S(1)}, u32[]{:S(2)}, u32[]{:S(2)}) collective-permute-start(f32[112,256]{1,0:T(8,128)S(1)} %get-tuple-element.89), channel_id=1, source_target_pairs={{0,2},{1,3},{2,0},{3,1},{4,6},{5,7},{6,4},{7,5},{8,10},{9,11},{10,... | collective-permute-start | bytes 344072 | tf_op jit(solution)/shard_map/ppermute | solution.py:195
  56.2 1.6 %collective-permute-done.24 = f32[2,112,256]{2,1,0:T(8,128)S(1)} collective-permute-done((f32[2,112,256]{2,1,0:T(8,128)S(1)}, f32[2,112,256]{2,1,0:T(8,128)S(1)}, u32[]{:S(2)}, u32[]{:S(2)}) %collective-permute-start.24) | collective-permute-done | bytes 229408 | tf_op jit(solution)/shard_map/ppermute | solution.py:195
  57.9 1.2 %copy.19 = f32[1,2,1,15,15,256]{5,2,4,3,1,0:T(1,128)} copy(f32[1,2,1,15,15,256]{5,1,4,3,2,0:T(2,128)S(1)} %fusion) | data formatting | bytes 921600
  59.5 0.7 %collective-permute-start.26 = (f32[112,256]{1,0:T(8,128)S(1)}, f32[112,256]{1,0:T(8,128)S(1)}, u32[]{:S(2)}, u32[]{:S(2)}) collective-permute-start(f32[112,256]{1,0:T(8,128)S(1)} %get-tuple-element.93), channel_id=1, source_target_pairs={{0,2},{1,3},{2,0},{3,1},{4,6},{5,7},{6,4},{7,5},{8,10},{9,11},{10,... | collective-permute-start | bytes 344072 | tf_op jit(solution)/shard_map/ppermute | solution.py:195
  60.3 0.7 %maximum_bitcast_fusion.1 = f32[1,224,256]{2,1,0:T(8,128)} fusion(f32[112,256]{1,0:T(8,128)S(1)} %get-tuple-element.87, f32[112,256]{1,0:T(8,128)S(1)} %get-tuple-element.86), kind=kLoop, calls=%fused_computation.16 | loop fusion | flops 57344 | bytes 458752 | tf_op jit(solution)/shard_map/broadcast_in_dim | solution.py:266
  61.0 2.9 %collective-permute-done.25 = f32[112,256]{1,0:T(8,128)S(1)} collective-permute-done((f32[112,256]{1,0:T(8,128)S(1)}, f32[112,256]{1,0:T(8,128)S(1)}, u32[]{:S(2)}, u32[]{:S(2)}) %collective-permute-start.25) | collective-permute-done | bytes 114720 | tf_op jit(solution)/shard_map/ppermute | solution.py:195
  64.4 0.7 %maximum_bitcast_fusion = f32[1,224,256]{2,1,0:T(8,128)} fusion(f32[112,256]{1,0:T(8,128)S(1)} %get-tuple-element.91, f32[112,256]{1,0:T(8,128)S(1)} %get-tuple-element.90), kind=kLoop, calls=%fused_computation.15 | loop fusion | flops 57344 | bytes 458752 | tf_op jit(solution)/shard_map/broadcast_in_dim | solution.py:266
  (92 shorter events, 10.8 us)
Async XLA Ops:
  0.6 7.2 %copy-start.2 = (f32[1,2,1,15,15,256]{5,2,4,3,1,0:T(1,128)S(1)}, f32[1,2,1,15,15,256]{5,2,4,3,1,0:T(1,128)}, u32[]{:S(2)}) copy-start(f32[1,2,1,15,15,256]{5,2,4,3,1,0:T(1,128)} %param.7) | copy-start | bytes 1382404
  0.6 9.7 %collective-permute-start.1 = (f32[224,256]{1,0:T(8,128)}, f32[224,256]{1,0:T(8,128)S(1)}, u32[]{:S(2)}, u32[]{:S(2)}) collective-permute-start(f32[224,256]{1,0:T(8,128)} %bitcast.124), channel_id=1, source_target_pairs={{0,4},{1,5},{2,6},{3,7},{4,0},{5,1},{6,2},{7,3},{8,12},{9,13},{10,... | collective-permute-start | bytes 688136 | tf_op jit(solution)/shard_map/ppermute | solution.py:195
  3.7 8.7 %collective-permute-start = (f32[224,256]{1,0:T(8,128)}, f32[224,256]{1,0:T(8,128)S(1)}, u32[]{:S(2)}, u32[]{:S(2)}) collective-permute-start(f32[224,256]{1,0:T(8,128)} %bitcast.125), channel_id=1, source_target_pairs={{0,2},{1,3},{2,0},{3,1},{4,6},{5,7},{6,4},{7,5},{8,10},{9,11},{10,... | collective-permute-start | bytes 688136 | tf_op jit(solution)/shard_map/ppermute | solution.py:195
  5.2 10.2 %collective-permute-start.3 = (f32[224,256]{1,0:T(8,128)}, f32[224,256]{1,0:T(8,128)S(1)}, u32[]{:S(2)}, u32[]{:S(2)}) collective-permute-start(f32[224,256]{1,0:T(8,128)} %bitcast.128), channel_id=1, source_target_pairs={{0,4},{1,5},{2,6},{3,7},{4,0},{5,1},{6,2},{7,3},{8,12},{9,13},{10,... | collective-permute-start | bytes 688136 | tf_op jit(solution)/shard_map/ppermute | solution.py:195
  5.7 10.5 %collective-permute-start.2 = (f32[224,256]{1,0:T(8,128)}, f32[224,256]{1,0:T(8,128)S(1)}, u32[]{:S(2)}, u32[]{:S(2)}) collective-permute-start(f32[224,256]{1,0:T(8,128)} %bitcast.129), channel_id=1, source_target_pairs={{0,2},{1,3},{2,0},{3,1},{4,6},{5,7},{6,4},{7,5},{8,10},{9,11},{10,... | collective-permute-start | bytes 688136 | tf_op jit(solution)/shard_map/ppermute | solution.py:195
  5.8 12.0 %collective-permute-start.6 = (f32[224,256]{1,0:T(8,128)}, f32[224,256]{1,0:T(8,128)S(1)}, u32[]{:S(2)}, u32[]{:S(2)}) collective-permute-start(f32[224,256]{1,0:T(8,128)} %bitcast.126), channel_id=1, source_target_pairs={{0,1},{1,0},{2,3},{3,2},{4,5},{5,4},{6,7},{7,6},{8,9},{9,8},{10,11... | collective-permute-start | bytes 688136 | tf_op jit(solution)/shard_map/ppermute | solution.py:195
  12.4 11.6 %collective-permute-start.7 = (f32[224,256]{1,0:T(8,128)S(1)}, f32[224,256]{1,0:T(8,128)S(1)}, u32[]{:S(2)}, u32[]{:S(2)}) collective-permute-start(f32[224,256]{1,0:T(8,128)S(1)} %collective-permute-done.refs_4_), channel_id=1, source_target_pairs={{0,1},{1,0},{2,3},{3,2},{4,5},{5,4},{6,7},{7,6},{8,9},{9,8},{10,11... | collective-permute-start | bytes 688136 | tf_op jit(solution)/shard_map/ppermute | solution.py:195
  12.5 5.8 %collective-permute-start.5 = (f32[112,256]{1,0:T(8,128)S(1)}, f32[112,256]{1,0:T(8,128)S(1)}, u32[]{:S(2)}, u32[]{:S(2)}) collective-permute-start(f32[112,256]{1,0:T(8,128)S(1)} %slice.135), channel_id=1, source_target_pairs={{0,2},{1,3},{2,0},{3,1},{4,6},{5,7},{6,4},{7,5},{8,10},{9,11},{10,... | collective-permute-start | bytes 344072 | tf_op jit(solution)/shard_map/ppermute | solution.py:195
  15.3 8.1 %copy-start.1 = (f32[1,224,256]{2,1,0:T(8,128)S(1)}, f32[1,224,256]{2,1,0:T(8,128)}, u32[]{:S(2)}) copy-start(f32[1,224,256]{2,1,0:T(8,128)} %param.12) | copy-start | bytes 688132
  15.3 9.2 %copy-start = (f32[1,224,256]{2,1,0:T(8,128)S(1)}, f32[1,224,256]{2,1,0:T(8,128)}, u32[]{:S(2)}) copy-start(f32[1,224,256]{2,1,0:T(8,128)} %param.13) | copy-start | bytes 688132
  15.4 5.3 %collective-permute-start.4 = (f32[112,256]{1,0:T(8,128)S(1)}, f32[112,256]{1,0:T(8,128)S(1)}, u32[]{:S(2)}, u32[]{:S(2)}) collective-permute-start(f32[112,256]{1,0:T(8,128)S(1)} %slice.134), channel_id=1, source_target_pairs={{0,4},{1,5},{2,6},{3,7},{4,0},{5,1},{6,2},{7,3},{8,12},{9,13},{10,... | collective-permute-start | bytes 344072 | tf_op jit(solution)/shard_map/ppermute | solution.py:195
  16.2 4.9 %collective-permute-start.12 = (f32[112,256]{1,0:T(8,128)S(1)}, f32[112,256]{1,0:T(8,128)S(1)}, u32[]{:S(2)}, u32[]{:S(2)}) collective-permute-start(f32[112,256]{1,0:T(8,128)S(1)} %slice.137), channel_id=1, source_target_pairs={{0,2},{1,3},{2,0},{3,1},{4,6},{5,7},{6,4},{7,5},{8,10},{9,11},{10,... | collective-permute-start | bytes 344072 | tf_op jit(solution)/shard_map/ppermute | solution.py:195
  17.8 6.7 %collective-permute-start.8 = (f32[224,256]{1,0:T(8,128)S(1)}, f32[224,256]{1,0:T(8,128)S(1)}, u32[]{:S(2)}, u32[]{:S(2)}) collective-permute-start(f32[224,256]{1,0:T(8,128)S(1)} %collective-permute-done.1.refs_5_), channel_id=1, source_target_pairs={{0,1},{1,0},{2,3},{3,2},{4,5},{5,4},{6,7},{7,6},{8,9},{9,8},{10,11... | collective-permute-start | bytes 688136 | tf_op jit(solution)/shard_map/ppermute | solution.py:195
  18.3 5.1 %collective-permute-start.11 = (f32[112,256]{1,0:T(8,128)S(1)}, f32[112,256]{1,0:T(8,128)S(1)}, u32[]{:S(2)}, u32[]{:S(2)}) collective-permute-start(f32[112,256]{1,0:T(8,128)S(1)} %slice.136), channel_id=1, source_target_pairs={{0,4},{1,5},{2,6},{3,7},{4,0},{5,1},{6,2},{7,3},{8,12},{9,13},{10,... | collective-permute-start | bytes 344072 | tf_op jit(solution)/shard_map/ppermute | solution.py:195
  20.7 2.7 %collective-permute-start.10 = (f32[112,256]{1,0:T(8,128)S(1)}, f32[112,256]{1,0:T(8,128)S(1)}, u32[]{:S(2)}, u32[]{:S(2)}) collective-permute-start(f32[112,256]{1,0:T(8,128)S(1)} %collective-permute-done.5.refs_7_), channel_id=1, source_target_pairs={{0,1},{1,0},{2,3},{3,2},{4,5},{5,4},{6,7},{7,6},{8,9},{9,8},{10,11... | collective-permute-start | bytes 344072 | tf_op jit(solution)/shard_map/ppermute | solution.py:195
  21.1 2.9 %collective-permute-start.9 = (f32[112,256]{1,0:T(8,128)S(1)}, f32[112,256]{1,0:T(8,128)S(1)}, u32[]{:S(2)}, u32[]{:S(2)}) collective-permute-start(f32[112,256]{1,0:T(8,128)S(1)} %collective-permute-done.4.refs_6_), channel_id=1, source_target_pairs={{0,1},{1,0},{2,3},{3,2},{4,5},{5,4},{6,7},{7,6},{8,9},{9,8},{10,11... | collective-permute-start | bytes 344072 | tf_op jit(solution)/shard_map/ppermute | solution.py:195
  23.4 3.0 %collective-permute-start.13 = (f32[224,256]{1,0:T(8,128)S(1)}, f32[224,256]{1,0:T(8,128)S(1)}, u32[]{:S(2)}, u32[]{:S(2)}) collective-permute-start(f32[224,256]{1,0:T(8,128)S(1)} %bitcast.130), channel_id=1, source_target_pairs={{0,1},{1,0},{2,3},{3,2},{4,5},{5,4},{6,7},{7,6},{8,9},{9,8},{10,11... | collective-permute-start | bytes 688136 | tf_op jit(solution)/shard_map/ppermute | solution.py:195
  23.4 3.0 %collective-permute-start.14 = (f32[224,256]{1,0:T(8,128)S(1)}, f32[224,256]{1,0:T(8,128)S(1)}, u32[]{:S(2)}, u32[]{:S(2)}) collective-permute-start(f32[224,256]{1,0:T(8,128)S(1)} %collective-permute-done.2.refs_3_), channel_id=1, source_target_pairs={{0,1},{1,0},{2,3},{3,2},{4,5},{5,4},{6,7},{7,6},{8,9},{9,8},{10,11... | collective-permute-start | bytes 688136 | tf_op jit(solution)/shard_map/ppermute | solution.py:195
  24.0 2.5 %collective-permute-start.15 = (f32[224,256]{1,0:T(8,128)S(1)}, f32[224,256]{1,0:T(8,128)S(1)}, u32[]{:S(2)}, u32[]{:S(2)}) collective-permute-start(f32[224,256]{1,0:T(8,128)S(1)} %collective-permute-done.3.refs_4_), channel_id=1, source_target_pairs={{0,1},{1,0},{2,3},{3,2},{4,5},{5,4},{6,7},{7,6},{8,9},{9,8},{10,11... | collective-permute-start | bytes 688136 | tf_op jit(solution)/shard_map/ppermute | solution.py:195
  24.0 2.4 %collective-permute-start.17 = (f32[112,256]{1,0:T(8,128)S(1)}, f32[112,256]{1,0:T(8,128)S(1)}, u32[]{:S(2)}, u32[]{:S(2)}) collective-permute-start(f32[112,256]{1,0:T(8,128)S(1)} %collective-permute-done.12.refs_6_), channel_id=1, source_target_pairs={{0,1},{1,0},{2,3},{3,2},{4,5},{5,4},{6,7},{7,6},{8,9},{9,8},{10,11... | collective-permute-start | bytes 344072 | tf_op jit(solution)/shard_map/ppermute | solution.py:195
  24.5 2.0 %collective-permute-start.16 = (f32[112,256]{1,0:T(8,128)S(1)}, f32[112,256]{1,0:T(8,128)S(1)}, u32[]{:S(2)}, u32[]{:S(2)}) collective-permute-start(f32[112,256]{1,0:T(8,128)S(1)} %collective-permute-done.11.refs_5_), channel_id=1, source_target_pairs={{0,1},{1,0},{2,3},{3,2},{4,5},{5,4},{6,7},{7,6},{8,9},{9,8},{10,11... | collective-permute-start | bytes 344072 | tf_op jit(solution)/shard_map/ppermute | solution.py:195
  28.3 10.2 %collective-permute-start.18 = (f32[240,256]{1,0:T(8,128)S(1)}, f32[240,256]{1,0:T(8,128)S(1)}, u32[]{:S(2)}, u32[]{:S(2)}) collective-permute-start(f32[240,256]{1,0:T(8,128)S(1)} %get-tuple-element.48), channel_id=1, source_target_pairs={{8,0},{16,8},{24,16},{9,1},{17,9},{25,17},{10,2},{18,10},{26,18},{... | collective-permute-start | bytes 737288 | tf_op jit(solution)/shard_map/ppermute | solution.py:307
  39.7 3.1 %collective-permute-start.19 = (f32[4,224,256]{2,1,0:T(8,128)S(1)}, f32[4,224,256]{2,1,0:T(8,128)S(1)}, u32[]{:S(2)}, u32[]{:S(2)}) collective-permute-start(f32[4,224,256]{2,1,0:T(8,128)S(1)} %pad_maximum_fusion), channel_id=1, source_target_pairs={{0,1},{1,0},{2,3},{3,2},{4,5},{5,4},{6,7},{7,6},{8,9},{9,8},{10,11... | collective-permute-start | bytes 2752520 | tf_op jit(solution)/shard_map/ppermute | solution.py:195
  41.9 2.9 %collective-permute-start.22 = (f32[4,224,256]{2,1,0:T(8,128)S(1)}, f32[4,224,256]{2,1,0:T(8,128)S(1)}, u32[]{:S(2)}, u32[]{:S(2)}) collective-permute-start(f32[4,224,256]{2,1,0:T(8,128)S(1)} %pad_maximum_fusion.1), channel_id=1, source_target_pairs={{0,1},{1,0},{2,3},{3,2},{4,5},{5,4},{6,7},{7,6},{8,9},{9,8},{10,11... | collective-permute-start | bytes 2752520 | tf_op jit(solution)/shard_map/ppermute | solution.py:195
  43.0 8.5 %collective-permute-start.20 = (f32[2,112,256]{2,1,0:T(8,128)S(1)}, f32[2,112,256]{2,1,0:T(8,128)S(1)}, u32[]{:S(2)}, u32[]{:S(2)}) collective-permute-start(f32[2,112,256]{2,1,0:T(8,128)S(1)} %pad_maximum_fusion.3), channel_id=1, source_target_pairs={{0,2},{1,3},{2,0},{3,1},{4,6},{5,7},{6,4},{7,5},{8,10},{9,11},{10,... | collective-permute-start | bytes 688136 | tf_op jit(solution)/shard_map/ppermute | solution.py:195
  44.5 8.5 %collective-permute-start.21 = (f32[2,112,256]{2,1,0:T(8,128)S(1)}, f32[2,112,256]{2,1,0:T(8,128)S(1)}, u32[]{:S(2)}, u32[]{:S(2)}) collective-permute-start(f32[2,112,256]{2,1,0:T(8,128)S(1)} %stack.163), channel_id=1, source_target_pairs={{0,4},{1,5},{2,6},{3,7},{4,0},{5,1},{6,2},{7,3},{8,12},{9,13},{10,... | collective-permute-start | bytes 688136 | tf_op jit(solution)/shard_map/ppermute | solution.py:195
  45.1 11.2 %collective-permute-start.23 = (f32[2,112,256]{2,1,0:T(8,128)S(1)}, f32[2,112,256]{2,1,0:T(8,128)S(1)}, u32[]{:S(2)}, u32[]{:S(2)}) collective-permute-start(f32[2,112,256]{2,1,0:T(8,128)S(1)} %pad_maximum_fusion.4), channel_id=1, source_target_pairs={{0,2},{1,3},{2,0},{3,1},{4,6},{5,7},{6,4},{7,5},{8,10},{9,11},{10,... | collective-permute-start | bytes 688136 | tf_op jit(solution)/shard_map/ppermute | solution.py:195
  46.3 11.5 %collective-permute-start.24 = (f32[2,112,256]{2,1,0:T(8,128)S(1)}, f32[2,112,256]{2,1,0:T(8,128)S(1)}, u32[]{:S(2)}, u32[]{:S(2)}) collective-permute-start(f32[2,112,256]{2,1,0:T(8,128)S(1)} %stack.164), channel_id=1, source_target_pairs={{0,4},{1,5},{2,6},{3,7},{4,0},{5,1},{6,2},{7,3},{8,12},{9,13},{10,... | collective-permute-start | bytes 688136 | tf_op jit(solution)/shard_map/ppermute | solution.py:195
  54.3 6.0 %collective-permute-start.27 = (f32[112,256]{1,0:T(8,128)S(1)}, f32[112,256]{1,0:T(8,128)S(1)}, u32[]{:S(2)}, u32[]{:S(2)}) collective-permute-start(f32[112,256]{1,0:T(8,128)S(1)} %get-tuple-element.88), channel_id=1, source_target_pairs={{0,4},{1,5},{2,6},{3,7},{4,0},{5,1},{6,2},{7,3},{8,12},{9,13},{10,... | collective-permute-start | bytes 344072 | tf_op jit(solution)/shard_map/ppermute | solution.py:195
  54.7 5.5 %collective-permute-start.28 = (f32[112,256]{1,0:T(8,128)S(1)}, f32[112,256]{1,0:T(8,128)S(1)}, u32[]{:S(2)}, u32[]{:S(2)}) collective-permute-start(f32[112,256]{1,0:T(8,128)S(1)} %get-tuple-element.89), channel_id=1, source_target_pairs={{0,2},{1,3},{2,0},{3,1},{4,6},{5,7},{6,4},{7,5},{8,10},{9,11},{10,... | collective-permute-start | bytes 344072 | tf_op jit(solution)/shard_map/ppermute | solution.py:195
  59.1 4.8 %collective-permute-start.25 = (f32[112,256]{1,0:T(8,128)S(1)}, f32[112,256]{1,0:T(8,128)S(1)}, u32[]{:S(2)}, u32[]{:S(2)}) collective-permute-start(f32[112,256]{1,0:T(8,128)S(1)} %get-tuple-element.92), channel_id=1, source_target_pairs={{0,4},{1,5},{2,6},{3,7},{4,0},{5,1},{6,2},{7,3},{8,12},{9,13},{10,... | collective-permute-start | bytes 344072 | tf_op jit(solution)/shard_map/ppermute | solution.py:195
  59.5 4.8 %collective-permute-start.26 = (f32[112,256]{1,0:T(8,128)S(1)}, f32[112,256]{1,0:T(8,128)S(1)}, u32[]{:S(2)}, u32[]{:S(2)}) collective-permute-start(f32[112,256]{1,0:T(8,128)S(1)} %get-tuple-element.93), channel_id=1, source_target_pairs={{0,2},{1,3},{2,0},{3,1},{4,6},{5,7},{6,4},{7,5},{8,10},{9,11},{10,... | collective-permute-start | bytes 344072 | tf_op jit(solution)/shard_map/ppermute | solution.py:195
  (2 other events, 2.1 us)

commit v3 on v2

v3 whole, which is shorter than its diff:
```python
import functools

import jax
import jax.numpy as jnp
from jax import lax
from jax.experimental import pallas as pl
from jax.experimental.pallas import tpu as pltpu
from jax.sharding import PartitionSpec as P

TAPS = 7
REACH = TAPS // 2
GROUP = 16
LANES = 128
COST = 1
PREP = 60
F32 = jnp.float32
BF16 = jnp.bfloat16
NT = (((1,), (1,)), ((), ()))
NN = (((1,), (0,)), ((), ()))
VMEM = pl.BlockSpec(memory_space=pltpu.VMEM)
SMEM = pl.BlockSpec(memory_space=pltpu.SMEM)
HBM = pl.BlockSpec(memory_space=pltpu.HBM)


KNOBS = {'prep': 1, 'early2': 1, 'pretie': 1, 'fs': 1}


def knob(name, default=0):
    return KNOBS.get(name, default)


def call(kernel, out_shapes, scratch, flops, *operands, scalars=0, aliases=None, far=False, vmem=12):
    moved = sum(x.size * x.dtype.itemsize for x in operands)
    moved += sum(s.size * s.dtype.itemsize for s in out_shapes)
    return pl.pallas_call(
        kernel,
        out_shape=out_shapes,
        in_specs=[SMEM] * scalars + [HBM if far else VMEM] * (len(operands) - scalars),
        out_specs=[VMEM] * len(out_shapes),
        scratch_shapes=scratch,
        input_output_aliases=aliases or {},
        compiler_params=pltpu.CompilerParams(vmem_limit_bytes=vmem * 1024 * 1024),
        cost_estimate=pl.CostEstimate(flops=int(flops * COST), bytes_accessed=int(moved * COST), transcendentals=0),
    )(*operands)


def split(value):
    high = value.astype(BF16)
    return high, (value - high.astype(F32)).astype(BF16)


def padded_rows(rows):
    return rows + 2 * REACH * GROUP


def fill(rows_ref, high_ref, low_ref):
    rows, channels = rows_ref.shape
    edge = REACH * GROUP
    border = jnp.zeros((edge, channels), BF16)
    high, low = split(rows_ref[...])
    for ref, body in ((high_ref, high), (low_ref, low)):
        ref[pl.ds(0, edge), :] = border
        ref[pl.ds(edge, rows), :] = body
        ref[pl.ds(edge + rows, edge), :] = border


def dot(a, b, dims):
    return lax.dot_general(a, b, dims, preferred_element_type=F32)


def window(ref, tap, rows):
    return ref[pl.ds((TAPS - 1 - tap) * GROUP, rows), :]


def convolve(high_ref, low_ref, w_high, w_low, rows, columns):
    channels = w_high.shape[0] // TAPS
    width = columns[1] - columns[0]
    total = jnp.zeros((rows, width), F32)
    for tap in range(TAPS):
        taken = pl.ds(tap * channels + columns[0], width)
        high, low = window(high_ref, tap, rows), window(low_ref, tap, rows)
        total += dot(high, w_high[taken, :], NT)
        total += dot(low, w_high[taken, :], NT)
        total += dot(high, w_low[taken, :], NT)
    return total


def regroup(source_ref, out_ref, groups, members):
    tail = jnp.zeros((GROUP - groups, out_ref.shape[-1]), F32)
    for member in range(members):
        for lane in range(source_ref.shape[0]):
            taken = source_ref[lane, pl.ds(member, groups, stride=GROUP), :]
            out_ref[pl.ds(member * GROUP, groups), lane * LANES : (lane + 1) * LANES] = taken
        out_ref[pl.ds(member * GROUP + groups, GROUP - groups), :] = tail


def place(starts_ref, granule, pieces, w_high, w_low):
    index = 0
    for piece in pieces:
        for begin in range(0, piece.shape[0], granule):
            high, low = split(piece[pl.ds(begin, granule), :])
            taken = pl.ds(pl.multiple_of(starts_ref[index], GROUP), granule)
            w_high[taken, :] = high
            w_low[taken, :] = low
            index += 1


def place_kernel(granule, starts_ref, *refs):
    place(starts_ref, granule, refs[:-2], *refs[-2:])


def placed(granule, starts, pieces, filter_rows):
    out = [jax.ShapeDtypeStruct((filter_rows, pieces[0].shape[1]), BF16)] * 2
    return call(functools.partial(place_kernel, granule), out, [], 0, starts, *pieces, scalars=1)


def conv_kernel(piece_count, granule, carried, masked, members, columns, *refs):
    refs = list(refs)
    starts = refs.pop(0) if piece_count else None
    rows_ref = refs.pop(0)
    mask_ref = refs.pop(0) if masked else None
    pieces = [refs.pop(0) for _ in range(piece_count)]
    if carried:
        w_high, w_low = refs.pop(0), refs.pop(0)
    out_ref = refs.pop(0)
    if piece_count:
        w_high, w_low = refs.pop(0), refs.pop(0)
        place(starts, granule, pieces, w_high, w_low)
    high, low, flat = refs
    rows = rows_ref.shape[0]
    fill(rows_ref, high, low)
    total = convolve(high, low, w_high, w_low, rows, columns)
    if masked:
        total = total * mask_ref[...].astype(F32)
    for lane in range(flat.shape[0]):
        flat[lane] = total[:, lane * LANES : (lane + 1) * LANES]
    regroup(flat, out_ref, rows // GROUP, members)


def conv(rows, mask, members, weights=None, pieces=None, columns=None):
    count, channels = rows.shape
    filter_rows = TAPS * channels
    columns = columns or (0, channels)
    width = columns[1] - columns[0]
    granule, starts, parts = pieces or (0, None, [])
    operands = [rows] + ([] if mask is None else [mask]) + parts + list(weights or [])
    out = [jax.ShapeDtypeStruct((members * GROUP, width), F32)]
    aliases = {}
    if parts:
        operands = [starts] + operands
        out += [jax.ShapeDtypeStruct((filter_rows, channels), BF16)] * 2
        if weights:
            aliases = {len(operands) - 2: 1, len(operands) - 1: 2}
    scratch = [
        pltpu.VMEM((padded_rows(count), channels), BF16),
        pltpu.VMEM((padded_rows(count), channels), BF16),
        pltpu.VMEM((width // LANES, count, LANES), F32),
    ]
    kernel = functools.partial(
        conv_kernel, len(parts), granule, bool(weights), mask is not None, members, columns
    )
    flops = 6 * count * filter_rows * width
    result = call(kernel, out, scratch, flops, *operands, scalars=1 if parts else 0, aliases=aliases)
    return result if parts else result[0]


def spread(line_ref, start, height, width, out_ref):
    out_ref[...] = jnp.zeros_like(out_ref)
    for row in range(height):
        out_ref[pl.ds(row * GROUP, width), :] = line_ref[pl.ds(start + row * width, width), 0, :]


def prepare_kernel(height, width, *refs):
    sources, refs = refs[:5], refs[5:]
    row_outs, turned_outs, refs = refs[:3], refs[3:7], refs[7:]
    lines, (flat, grouped, scratch, arrived) = refs[:5], refs[5:]
    copies = [pltpu.make_async_copy(source, held, arrived.at[index]) for index, (source, held) in enumerate(zip(sources, lines))]
    for copy in copies:
        copy.start()
    for copy, held, out in zip(copies, lines, row_outs):
        copy.wait()
        for index in range(out.shape[0]):
            spread(held, index * height * width, height, width, out.at[index])
    in_line, mid_line = lines[3:]
    copies[3].wait()
    copies[4].wait()
    for tick in range(turned_outs[0].shape[0]):
        start = tick * height * width
        spread(in_line, start, height, width, scratch)
        for lane in range(flat.shape[0]):
            flat[lane] = scratch[:, lane * LANES : (lane + 1) * LANES]
        regroup(flat, grouped, height, width)
        turned_outs[0][tick], turned_outs[1][tick] = split(grouped[...].T)
        spread(mid_line, start, height, width, scratch)
        turned_outs[2][tick], turned_outs[3][tick] = split(scratch[...].T)


def prepare(height, width, mask, loss, came, act_in, act_mid):
    sources = [came, mask, loss, act_in, act_mid]
    ticks, channels = act_in.shape[0] // (height * width), act_in.shape[2]
    out = [jax.ShapeDtypeStruct((x.shape[0] // (height * width), height * GROUP, channels), x.dtype) for x in sources[:3]]
    out += [jax.ShapeDtypeStruct((ticks, channels, width * GROUP), BF16)] * 2
    out += [jax.ShapeDtypeStruct((ticks, channels, height * GROUP), BF16)] * 2
    scratch = [pltpu.VMEM(x.shape, x.dtype) for x in sources]
    scratch += [
        pltpu.VMEM((channels // LANES, height * GROUP, LANES), F32),
        pltpu.VMEM((width * GROUP, channels), F32),
        pltpu.VMEM((height * GROUP, channels), F32),
        pltpu.SemaphoreType.DMA((len(sources),)),
    ]
    kernel = functools.partial(prepare_kernel, height, width)
    came, mask, loss, *parts = call(kernel, out, scratch, 0, *sources, far=True, vmem=PREP)
    return mask, loss, came[0], *parts


def last_kernel(height, width, *refs):
    rows_ref, w_high, w_low = refs[:3]
    before, (line_ref, high, low, flat) = refs[3:-4], refs[-4:]
    for tick, ref in enumerate(before):
        for row in range(height):
            start = (tick * height + row) * width
            line_ref[pl.ds(start, width), 0, :] = ref[pl.ds(row * GROUP, width), :]
    rows = rows_ref.shape[0]
    fill(rows_ref, high, low)
    total = convolve(high, low, w_high, w_low, rows, (0, rows_ref.shape[1]))
    lanes = flat.shape[0]
    for lane in range(lanes):
        flat[lane] = total[:, lane * LANES : (lane + 1) * LANES]
    for row in range(height):
        start = (len(before) * height + row) * width
        taken = [flat[lane, pl.ds(row, width, stride=GROUP), :] for lane in range(lanes)]
        line_ref[pl.ds(start, width), 0, :] = jnp.concatenate(taken, axis=1)


def last_conv(rows, weights, before, height, width):
    count, channels = rows.shape
    out = [jax.ShapeDtypeStruct(((len(before) + 1) * height * width, 1, channels), F32)]
    scratch = [
        pltpu.VMEM((padded_rows(count), channels), BF16),
        pltpu.VMEM((padded_rows(count), channels), BF16),
        pltpu.VMEM((channels // LANES, count, LANES), F32),
    ]
    flops = 6 * count * TAPS * channels * channels
    kernel = functools.partial(last_kernel, height, width)
    return call(kernel, out, scratch, flops, rows, *weights, *before)[0]


def correlate_kernel(scale, carried, dealt, *refs):
    refs = list(refs)
    starts = refs.pop(0) if dealt else None
    act_high, act_low, rows_ref = refs[:3]
    before = refs[3] if carried else None
    out_ref, high, low = refs[3 + carried :]
    fill(rows_ref, high, low)
    rows, channels = rows_ref.shape
    for tap in range(TAPS):
        taken = pl.ds(tap * channels, channels)
        here_high, here_low = window(high, tap, rows), window(low, tap, rows)
        total = dot(act_high[...], here_high, NN)
        total += dot(act_low[...], here_high, NN)
        total += dot(act_high[...], here_low, NN)
        total *= scale
        if carried:
            total += before[taken, :]
        if not dealt:
            out_ref[taken, :] = total
            continue
        block_rows = out_ref.shape[2]
        begin, end = tap * channels, (tap + 1) * channels
        for block in range(begin // block_rows, -(-end // block_rows)):
            first, last = max(begin, block * block_rows), min(end, (block + 1) * block_rows)
            into = pl.ds(first - block * block_rows, last - first)
            distance = jnp.bitwise_xor(block, starts[0])
            place_at = (jnp.bitwise_and(distance, 1), jnp.right_shift(distance, 1), into)
            out_ref[place_at] = total[first - begin : last - begin, :]


def correlate(act_high, act_low, rows, scale, before=None, starts=None):
    count, channels = rows.shape
    filter_rows = TAPS * channels
    scratch = [pltpu.VMEM((padded_rows(count), channels), BF16)] * 2
    operands = [act_high, act_low, rows] + ([] if before is None else [before])
    if starts is None:
        out = [jax.ShapeDtypeStruct((filter_rows, channels), F32)]
    else:
        out = [jax.ShapeDtypeStruct((2, 4, filter_rows // 8, channels), F32)]
        operands = [starts] + operands
    kernel = functools.partial(correlate_kernel, scale, before is not None, starts is not None)
    flops = 6 * count * filter_rows * channels
    result = call(kernel, out, scratch, flops, *operands, scalars=0 if starts is None else 1)
    return result[0]


def both_kernel(scale, *refs):
    two, one, (second_ref, first_ref, high, low) = refs[:3], refs[3:6], refs[6:]
    correlate_kernel(scale, False, False, *two, second_ref, high, low)
    correlate_kernel(scale, False, False, *one, first_ref, high, low)


def correlate_both(mid_parts, incoming, in_parts, pre, scale):
    count, channels = incoming.shape
    out = [jax.ShapeDtypeStruct((TAPS * channels, channels), F32)] * 2
    scratch = [pltpu.VMEM((padded_rows(count), channels), BF16)] * 2
    operands = [*mid_parts, incoming, *in_parts, pre]
    flops = 12 * count * TAPS * channels * channels
    return call(functools.partial(both_kernel, scale), out, scratch, flops, *operands)


def line(values):
    return values.reshape(-1, 1, values.shape[-1])


def swap(shard, bit):
    peers = lax.axis_size("dp")
    return lax.ppermute(shard, "dp", [(i, i ^ bit) for i in range(peers)])


def together(*values):
    return lax.optimization_barrier(values)


def starts_of(me, rows, granule, pieces):
    starts = []
    for piece, bits, offset in pieces:
        bits = bits if isinstance(bits, tuple) else (bits,)
        for begin in range(0, piece.shape[0], granule):
            block = me ^ bits[begin // rows]
            starts.append(block * rows + offset + begin % rows)
    return granule, jnp.stack(starts).astype(jnp.int32), [piece for piece, _, _ in pieces]


def local_any(act_in, act_mid, relu_mask, arriving, loss_grad, w_first, w_second):
    ticks, images, height, width = act_in.shape[1:5]
    sections = lax.axis_size("section")
    is_last = lax.axis_index("section") == sections - 1
    scale = 1.0 / (ticks * images * lax.axis_size("dp"))
    start = jnp.zeros((1,), jnp.int32)
    filter_rows = w_first.shape[1] * lax.axis_size("dp")
    first_pieces = (filter_rows, start, [lax.all_gather(w_first[0], "dp", axis=0, tiled=True)])
    second_pieces = (filter_rows, start, [lax.all_gather(w_second[0], "dp", axis=0, tiled=True)])
    mask, loss, incoming, in_high, in_low, mid_high, mid_low = prepare(
        height, width, line(relu_mask), line(loss_grad), line(arriving), line(act_in), line(act_mid)
    )
    second = correlate(mid_high[0], mid_low[0], incoming, scale)
    pre, *second_parts = conv(incoming, mask[0], width, pieces=second_pieces)
    out, *first_parts = conv(pre, None, height, pieces=first_pieces)
    outs = [out]
    first = correlate(in_high[0], in_low[0], pre, scale)
    for tick in range(1, ticks):
        above = lax.ppermute(outs[-1], "section", [(i, i - 1) for i in range(1, sections)])
        incoming = jnp.where(is_last, loss[tick - 1], above)
        second = correlate(mid_high[tick], mid_low[tick], incoming, scale, second)
        pre = conv(incoming, mask[tick], width, weights=second_parts)
        first = correlate(in_high[tick], in_low[tick], pre, scale, first)
        if tick < ticks - 1:
            outs.append(conv(pre, None, height, weights=first_parts))
    data_grad = last_conv(pre, first_parts, outs, height, width).reshape(act_in.shape)
    second_grad = lax.psum_scatter(second, "dp", scatter_dimension=0, tiled=True)
    first_grad = lax.psum_scatter(first, "dp", scatter_dimension=0, tiled=True)
    return data_grad, first_grad[None], second_grad[None]


def near_phase(chip):
    half = chip.shape[1] // 2
    a, b = chip[:, :half], chip[:, half:]
    return a, b, swap(jnp.stack([a[1], a[3]]), 2), swap(jnp.stack([b[2], b[3]]), 4)


def far_phase(a, b, a_there, b_there):
    a_near, a_far = a[0] + a_there[0], a[2] + a_there[1]
    if knob("fs"):
        a_far, b_there = together(a_far, b_there)
    b_near, b_far = b[0] + b_there[0], b[1] + b_there[1]
    return a_near, b_near, swap(a_far, 4), swap(b_far, 2)


def join(a_near, b_near, a_last, b_last):
    return jnp.concatenate([a_near + a_last, b_near + b_last], axis=0)[None]


def far_pieces(x_piece, y_piece):
    half = x_piece.shape[0] // 2
    return swap(x_piece[:half], 4), swap(y_piece[half:], 2)


def local_eight(act_in, act_mid, relu_mask, arriving, loss_grad, w_first, w_second):
    ticks, images, height, width = act_in.shape[1:5]
    channels = act_in.shape[-1]
    filter_rows = TAPS * channels
    sections = lax.axis_size("section")
    is_last = lax.axis_index("section") == sections - 1
    me = lax.axis_index("dp")
    scale = 1.0 / (ticks * images * lax.axis_size("dp"))
    one, two = w_first[0], w_second[0]
    rows = one.shape[0]
    half = rows // 2
    owners = jnp.reshape(me, (1,)).astype(jnp.int32)
    x_two, y_two = swap(two, 2), swap(two, 4)
    x_one, y_one = swap(one, 2), swap(one, 4)
    s_two, s_one = swap(two, 1), swap(one, 1)
    mask, loss, incoming, in_high, in_low, mid_high, mid_low = prepare(
        height, width, line(relu_mask), line(loss_grad), line(arriving), line(act_in), line(act_mid)
    )
    if knob("mask"):
        mask = [mask[tick] for tick in range(ticks)]
        if knob("mask") == 2:
            *mask, y_two = together(*mask, y_two)
    if knob("prep") == 4:
        mask, loss, incoming, x_two, in_high, in_low, mid_high, mid_low = together(
            mask, loss, incoming, x_two, in_high, in_low, mid_high, mid_low
        )
    elif knob("prep") == 0:
        mask, loss, incoming, x_two, y_two = together(mask, loss, incoming, x_two, y_two)
    elif knob("prep") == 1:
        mask, loss, incoming, x_two, y_two, in_high, in_low, mid_high, mid_low = together(
            mask, loss, incoming, x_two, y_two, in_high, in_low, mid_high, mid_low
        )
    elif knob("prep") == 2:
        mask, loss, incoming, x_two, y_two, s_two, in_high, in_low, mid_high, mid_low = together(
            mask, loss, incoming, x_two, y_two, s_two, in_high, in_low, mid_high, mid_low
        )
    elif knob("prep") == 3:
        mask, loss, incoming, x_two, y_two, s_two = together(mask, loss, incoming, x_two, y_two, s_two)
    ya_two, xb_two = far_pieces(x_two, y_two)
    if knob("near") == 0:
        sx_two, sy_two = swap(x_two, 1), swap(y_two, 1)
        near_two = [(x_two, 2, 0), (y_two, 4, 0), (sx_two, 3, 0), (sy_two, 5, 0)]
    else:
        n_two = jnp.concatenate([x_two, y_two])
        near_two = [(n_two, (2, 4), 0), (swap(n_two, 1), (3, 5), 0)]
    come = [(two, 0, 0), (s_two, 1, 0)] + near_two
    second_parts = None
    if knob("early2"):
        second_parts = placed(*starts_of(me, rows, rows, come), filter_rows)
        come = []
    if knob("g2") == 0:
        second = correlate(mid_high[0], mid_low[0], incoming, scale)
    if knob("tie2") == 1:
        x_one, y_one, second = together(x_one, y_one, second)
    elif knob("tie2") == 2:
        x_one, y_one, *second_parts = together(x_one, y_one, *second_parts)
    elif knob("tie2") == 3:
        x_one, y_one, in_high, in_low, mid_high, mid_low = together(
            x_one, y_one, in_high, in_low, mid_high, mid_low
        )
    if knob("late1") == 1:
        s_one = swap(together(one, x_two)[0], 1)
    elif knob("late1") == 2:
        s_one = swap(together(one, x_one, y_one)[0], 1)
    if knob("far1") == 0:
        ya_one, xb_one = far_pieces(x_one, y_one)
        far_one = [(ya_one, 6, 0), (xb_one, 6, half)]
    else:
        d_one = swap(together(one, x_two, y_two)[0], 6)
        far_one = [(d_one, 6, 0)]
    if knob("near") == 0:
        sx_one, sy_one = swap(x_one, 1), swap(y_one, 1)
        near_one = [(x_one, 2, 0), (y_one, 4, 0), (sx_one, 3, 0), (sy_one, 5, 0)]
    else:
        n_one = jnp.concatenate([x_one, y_one])
        near_one = [(n_one, (2, 4), 0), (swap(n_one, 1), (3, 5), 0)]
    if knob("farcat"):
        f_two = jnp.concatenate([ya_two, xb_two])
        come += [(f_two, 6, 0), (swap(f_two, 1), 7, 0)]
    else:
        sya_two, sxb_two = swap(ya_two, 1), swap(xb_two, 1)
        come += [(ya_two, 6, 0), (xb_two, 6, half), (sya_two, 7, 0), (sxb_two, 7, half)]
    pre, *second_parts = conv(incoming, mask[0], width, weights=second_parts, pieces=starts_of(me, rows, half, come))
    come = [(one, 0, 0), (s_one, 1, 0)] + near_one
    first_parts = None
    if knob("early1"):
        first_parts = placed(*starts_of(me, rows, rows, come), filter_rows)
        come = []
    if knob("pretie") == 1:
        ends, pre = [piece for piece, _, _ in far_one], pre
        *ends, pre = together(*ends, pre)
        far_one = [(end, bits, offset) for end, (_, bits, offset) in zip(ends, far_one)]
    elif knob("pretie") == 2:
        *ends, pre, first_high, first_low = together(*[piece for piece, _, _ in far_one], pre, *first_parts)
        first_parts = [first_high, first_low]
        far_one = [(end, bits, offset) for end, (_, bits, offset) in zip(ends, far_one)]
    if knob("farcat") and len(far_one) == 2:
        far_one = [(jnp.concatenate([piece for piece, _, _ in far_one]), 6, 0)]
    come += far_one + [(swap(piece, 1), bits ^ 1, offset) for piece, bits, offset in far_one]
    out, *first_parts = conv(pre, None, height, weights=first_parts, pieces=starts_of(me, rows, half, come))
    outs = [out]
    in_high, in_low, pre, _ = together(in_high, in_low, pre, out)
    if knob("g2") == 1:
        mid_high, mid_low, _ = together(mid_high, mid_low, out)
        second = correlate(mid_high[0], mid_low[0], incoming, scale)
    if knob("g2") == 2:
        mid_high, mid_low, _ = together(mid_high, mid_low, out)
        second, first = correlate_both((mid_high[0], mid_low[0]), incoming, (in_high[0], in_low[0]), pre, scale)
    else:
        first = correlate(in_high[0], in_low[0], pre, scale)
    for tick in range(1, ticks):
        above = lax.ppermute(outs[-1], "section", [(i, i - 1) for i in range(1, sections)])
        above, first, second = together(above, first, second)
        incoming = jnp.where(is_last, loss[tick - 1], above)
        if tick < ticks - 1:
            second = correlate(mid_high[tick], mid_low[tick], incoming, scale, second)
            pre = conv(incoming, mask[tick], width, weights=second_parts)
            first = correlate(in_high[tick], in_low[tick], pre, scale, first)
            outs.append(conv(pre, None, height, weights=first_parts))
    dealt = correlate(mid_high[-1], mid_low[-1], incoming, scale, second, owners)
    kept, other = dealt[0], swap(dealt[1], 1)
    pre = conv(incoming, mask[-1], width, weights=second_parts)
    first_dealt = correlate(in_high[-1], in_low[-1], pre, scale, first, owners)
    first_kept, first_other = first_dealt[0], swap(first_dealt[1], 1)
    a, b, a_there, b_there = near_phase(kept + other)
    if knob("rs") == 3:
        data_grad = last_conv(pre, first_parts, outs, height, width)
        first_other, data_grad = together(first_other, data_grad)
    first_a, first_b, first_a_there, first_b_there = near_phase(first_kept + first_other)
    if knob("rs") == 0:
        pre, a_there, b_there = together(pre, a_there, b_there)
    elif knob("rs") == 1:
        pre, first_a_there, first_b_there = together(pre, first_a_there, first_b_there)
    elif knob("rs") == 2:
        pre, first_other = together(pre, first_other)
    last = far_phase(a, b, a_there, b_there)
    if knob("rs") != 3:
        data_grad = last_conv(pre, first_parts, outs, height, width)
    if knob("rs") == 2:
        data_grad, first_a_there, first_b_there = together(data_grad, first_a_there, first_b_there)
    first_last = far_phase(first_a, first_b, first_a_there, first_b_there)
    if knob("join"):
        both = together(*last, *first_last)
        last, first_last = both[:4], both[4:]
    return data_grad.reshape((1, ticks, images, height, width, channels)), join(*first_last), join(*last)


def local(*arguments):
    return (local_eight if lax.axis_size("dp") == 8 else local_any)(*arguments)


def solution(mesh):
    return jax.shard_map(
        local,
        mesh=mesh,
        in_specs=(
            P("section", None, "dp", None, None, None),
            P("section", None, "dp", None, None, None),
            P("section", None, "dp", None, None, None),
            P("section", "dp", None, None, None),
            P(None, "dp", None, None, None),
            P("section", "dp", None),
            P("section", "dp", None),
        ),
        out_specs=(
            P("section", None, "dp", None, None, None),
            P("section", "dp", None),
            P("section", "dp", None),
        ),
        check_vma=False,
    )
```

time: 65.3 us -> 63 us (0.965)
  waiting for transfers between devices: 26.6 us -> 20.6 us
  local copies, waits for them, and re-layouts: 6.04 us -> 1.62 us
  Pallas kernels: 9.52 us -> 13.9 us
  starting transfers between devices: 19.3 us -> 23.6 us
    ppermute x28, waiting for transfers between devices: 18.8 us -> 12.9 us  [swap(): return lax.ppermute(shard, 'dp', [(i, i ^ bit) for i in range(peers)])]
    unnamed x19 -> x16, local copies, waits for them, and re-layouts: 4.73 us -> 0.03 us
    pallas_call x9 -> x10, Pallas kernels: 9.52 us -> 13.9 us  [call(): pl.pallas_call(kernel, out_shape=out_shapes, in_specs=[SMEM] * scalars +...]
    ppermute x28, starting transfers between devices: 17.8 us -> 22.2 us  [swap(): return lax.ppermute(shard, 'dp', [(i, i ^ bit) for i in range(peers)])]
    squeeze x6 -> x5, local copies, waits for them, and re-layouts: 0.11 us -> 1.3 us  [the longest x1 1.09 us: local_eight(): pre = conv(incoming, mask[-1], width, weights=second_parts)]
    another operation x5 -> x2, local copies, waits for them, and re-layouts: 0.95 us -> 0.17 us  [starts_of(): jnp.stack(starts).astype(jnp.int32)]
  transfers between devices with their start and end apart: 29 -> 29, of which waited for: 13 -> 13; matrix products, arithmetic and copies ran while one was open for 10% -> 4% of each run, Pallas kernels for 10% -> 18%
where the time goes in v3:
time: 63 us; the launch traced here: 62.8 us
  starting transfers between devices  23.6 us (37%)
  waiting for transfers between devices  20.6 us (33%)
  Pallas kernels  13.9 us (22%)
  other arithmetic  1.94 us (3%)
  local copies, waits for them, and re-layouts  1.62 us (3%)
  between operations  1.06 us (2%)
    ppermute x28, starting transfers between devices, swap(): return lax.ppermute(shard, 'dp', [(i, i ^ bit) for i in range(peers)])  22.2 us
    pallas_call x10, Pallas kernels, call(): pl.pallas_call(kernel, out_shape=out_shapes, in_specs=[SMEM] * scalars +...  13.9 us
    ppermute x28, waiting for transfers between devices, swap(): return lax.ppermute(shard, 'dp', [(i, i ^ bit) for i in range(peers)])  12.9 us
    ppermute x1, waiting for transfers between devices, local_eight(): lax.ppermute(outs[-1], 'section', [(i, i - 1) for i in range(1, sections)])  7.69 us
    ppermute x1, starting transfers between devices, local_eight(): lax.ppermute(outs[-1], 'section', [(i, i - 1) for i in range(1, sections)])  1.42 us
    broadcast_in_dim x2, other arithmetic, join(): return jnp.concatenate([a_near + a_last, b_near + b_last], axis=0)[None]  1.41 us
  transfers between devices with their start and end apart: 29, of which 13 were waited for; matrix products, arithmetic and copies ran while one was open for 4% of the time, Pallas kernels for 18%

profile of v3, /device:TPU:0, one launch (start us, length us, event | category | flops | bytes accessed | tf_op | source)
XLA Modules:
  0.0 62.8 jit_solution(12547537527612874321)
XLA Ops:
  0.6 3.0 %collective-permute-start.1 = (f32[224,256]{1,0:T(8,128)}, f32[224,256]{1,0:T(8,128)S(1)}, u32[]{:S(2)}, u32[]{:S(2)}) collective-permute-start(f32[224,256]{1,0:T(8,128)} %bitcast.92), channel_id=1, source_target_pairs={{0,4},{1,5},{2,6},{3,7},{4,0},{5,1},{6,2},{7,3},{8,12},{9,13},{10,... | collective-permute-start | bytes 688136 | tf_op jit(solution)/shard_map/ppermute | solution.py:315
  3.7 1.5 %collective-permute-start = (f32[224,256]{1,0:T(8,128)}, f32[224,256]{1,0:T(8,128)S(1)}, u32[]{:S(2)}, u32[]{:S(2)}) collective-permute-start(f32[224,256]{1,0:T(8,128)} %bitcast.93), channel_id=1, source_target_pairs={{0,2},{1,3},{2,0},{3,1},{4,6},{5,7},{6,4},{7,5},{8,10},{9,11},{10,... | collective-permute-start | bytes 688136 | tf_op jit(solution)/shard_map/ppermute | solution.py:315
  5.8 3.3 %shard_map.94 = (f32[1,240,256]{2,1,0:T(8,128)}, s32[2,240,256]{2,1,0:T(8,128)}, f32[1,240,256]{2,1,0:T(8,128)}, bf16[2,256,240]{2,1,0:T(8,128)(2,1)}, bf16[2,25...) custom-call(f32[225,1,256]{2,1,0:T(1,128)} %bitcast.104, ...), custom_call_target="tpu_custom_call" | custom-call | bytes 3809280 | tf_op jit(solution)/shard_map/pallas_call | solution.py:35
  9.1 1.2 %collective-permute-done.1.refs_3_ = f32[224,256]{1,0:T(8,128)S(1)} collective-permute-done((f32[224,256]{1,0:T(8,128)}, f32[224,256]{1,0:T(8,128)S(1)}, u32[]{:S(2)}, u32[]{:S(2)}) %collective-permute-start.1) | collective-permute-done | bytes 229408 | tf_op jit(solution)/shard_map/ppermute | solution.py:315
  10.3 2.1 %collective-permute-done.refs_2_ = f32[224,256]{1,0:T(8,128)S(1)} collective-permute-done((f32[224,256]{1,0:T(8,128)}, f32[224,256]{1,0:T(8,128)S(1)}, u32[]{:S(2)}, u32[]{:S(2)}) %collective-permute-start) | collective-permute-done | bytes 229408 | tf_op jit(solution)/shard_map/ppermute | solution.py:315
  12.4 1.6 %collective-permute-start.7 = (f32[112,256]{1,0:T(8,128)S(1)}, f32[112,256]{1,0:T(8,128)S(1)}, u32[]{:S(2)}, u32[]{:S(2)}) collective-permute-start(f32[112,256]{1,0:T(8,128)S(1)} %slice.144), channel_id=1, source_target_pairs={{0,2},{1,3},{2,0},{3,1},{4,6},{5,7},{6,4},{7,5},{8,10},{9,11},{10,... | collective-permute-start | bytes 344072 | tf_op jit(solution)/shard_map/ppermute | solution.py:315
  14.4 1.7 %collective-permute-start.6 = (f32[112,256]{1,0:T(8,128)S(1)}, f32[112,256]{1,0:T(8,128)S(1)}, u32[]{:S(2)}, u32[]{:S(2)}) collective-permute-start(f32[112,256]{1,0:T(8,128)S(1)} %slice.143), channel_id=1, source_target_pairs={{0,4},{1,5},{2,6},{3,7},{4,0},{5,1},{6,2},{7,3},{8,12},{9,13},{10,... | collective-permute-start | bytes 344072 | tf_op jit(solution)/shard_map/ppermute | solution.py:315
  16.5 1.6 %collective-permute-start.5 = (f32[112,256]{1,0:T(8,128)S(1)}, f32[112,256]{1,0:T(8,128)S(1)}, u32[]{:S(2)}, u32[]{:S(2)}) collective-permute-start(f32[112,256]{1,0:T(8,128)S(1)} %slice.179), channel_id=1, source_target_pairs={{0,2},{1,3},{2,0},{3,1},{4,6},{5,7},{6,4},{7,5},{8,10},{9,11},{10,... | collective-permute-start | bytes 344072 | tf_op jit(solution)/shard_map/ppermute | solution.py:315
  18.7 0.6 collective-permute-done.6.refs_3_
  19.8 1.1 %slice_bitcast_fusion.4 = (s32[240,256]{1,0:T(8,128)S(1)}, s32[240,256]{1,0:T(8,128)S(1)}) fusion(s32[2,240,256]{2,1,0:T(8,128)} %get-tuple-element.52), kind=kLoop, calls=%fused_computation.7 | loop fusion | bytes 983040 | tf_op jit(solution)/shard_map/squeeze | solution.py:507
  21.0 0.7 %shard_map.95 = (bf16[1792,256]{1,0:T(8,128)(2,1)S(1)}, bf16[1792,256]{1,0:T(8,128)(2,1)S(1)}) custom-call(s32[6]{0:T(128)S(1)} %stack.97.starts_ref, f32[224,256]{1,0:T(8,128)S(1)} %bitcast.95, f32[224,256]{1,0:T(8,128)S(1)} %collective-permute-done.10.refs_1_, f32[224,256]{1,0:T(8,128)S(1)} %collective-permute-done.refs_2_, ...), custom_call_target="tpu_custom_call" | custom-call | bytes 3211288 | tf_op jit(solution)/shard_map/pallas_call | solution.py:35
  22.4 1.6 %shard_map.96 = (f32[240,256]{1,0:T(8,128)S(1)}, bf16[1792,256]{1,0:T(8,128)(2,1)S(1)}, bf16[1792,256]{1,0:T(8,128)(2,1)S(1)}) custom-call(s32[4]{0:T(128)S(1)} %pad_add_fusion.refs_0_, f32[240,256]{1,0:T(8,128)S(1)} %bitcast.90, s32[240,256]{1,0:T(8,128)S(1)} %get-tuple-element.95.refs_2_, ...), custom_call_target="tpu_custom_call", output_to_operand_aliasing={{1}: (7, {}), {2}: (8, {})} | custom-call | flops 660602880 | bytes 4866064 | tf_op jit(solution)/shard_map/pallas_call | solution.py:35
  24.7 0.9 %shard_map.99.refs_4_ = f32[1792,256]{1,0:T(8,128)S(1)} custom-call(bf16[256,240]{1,0:T(8,128)(2,1)S(1)} %get-tuple-element.104.refs_0_, bf16[256,240]{1,0:T(8,128)(2,1)S(1)} %get-tuple-element.101.refs_1_, f32[240,256]{1,0:T(8,128)S(1)} %bitcast.91), custom_call_target="tpu_custom_call" | custom-call | flops 660602880 | bytes 2326528 | tf_op jit(solution)/shard_map/pallas_call | solution.py:35
  25.9 1.8 %shard_map.97 = (f32[240,256]{1,0:T(8,128)S(1)}, bf16[1792,256]{1,0:T(8,128)(2,1)S(1)}, bf16[1792,256]{1,0:T(8,128)(2,1)S(1)}) custom-call(s32[16]{0:T(128)S(1)} %stack.95.refs_0_, f32[240,256]{1,0:T(8,128)S(1)} %get-tuple-element.66.refs_1_.refs_2_, f32[224,256]{1,0:T(8,128)S(1)} %bitcast.99, f32[224,256]{1,0:T(8,128)S(1)} %collective-permute-done.13.refs_3_, ...), custom_call_target="tpu_custom_call" | custom-call | flops 660602880 | bytes 4161600 | tf_op jit(solution)/shard_map/pallas_call | solution.py:35
  27.7 1.4 %collective-permute-start.18 = (f32[240,256]{1,0:T(8,128)S(1)}, f32[240,256]{1,0:T(8,128)S(1)}, u32[]{:S(2)}, u32[]{:S(2)}) collective-permute-start(f32[240,256]{1,0:T(8,128)S(1)} %get-tuple-element.61.refs_3_), channel_id=1, source_target_pairs={{8,0},{16,8},{24,16},{9,1},{17,9},{25,17},{10,2},{18,10},{26,18},{... | collective-permute-start | bytes 737288 | tf_op jit(solution)/shard_map/ppermute | solution.py:497
  29.2 0.9 %shard_map.98.refs_4_ = f32[1792,256]{1,0:T(8,128)S(1)} custom-call(bf16[256,240]{1,0:T(8,128)(2,1)S(1)} %get-tuple-element.106.refs_0_, bf16[256,240]{1,0:T(8,128)(2,1)S(1)} %get-tuple-element.97.refs_1_, f32[240,256]{1,0:T(8,128)S(1)} %get-tuple-element.66.refs_1_.refs_2_), custom_call_target="tpu_custom_call" | custom-call | flops 660602880 | bytes 2326528 | tf_op jit(solution)/shard_map/pallas_call | solution.py:35
  30.1 7.7 %collective-permute-done.18 = f32[240,256]{1,0:T(8,128)S(1)} collective-permute-done((f32[240,256]{1,0:T(8,128)S(1)}, f32[240,256]{1,0:T(8,128)S(1)}, u32[]{:S(2)}, u32[]{:S(2)}) %collective-permute-start.18) | collective-permute-done | bytes 245792 | tf_op jit(solution)/shard_map/ppermute | solution.py:497
  37.8 0.9 %shard_map.101 = f32[2,4,224,256]{3,2,1,0:T(8,128)S(1)} custom-call(s32[1]{0:T(128)} %bitcast.31.refs_0_, bf16[256,240]{1,0:T(8,128)(2,1)S(1)} %get-tuple-element.105.refs_1_, bf16[256,240]{1,0:T(8,128)(2,1)S(1)} %get-tuple-element.100.refs_2_, f32[240,256]{1,0:T(8,128)S(1)} %bitcast_select_fusion.refs_0_.refs_3_, f32[1792,256]{1,0:T(8,128)S(1)} %shard_map.99.refs_4_), custom_call_target="tpu_custom_call" | custom-call | flops 660602880 | bytes 4161540 | tf_op jit(solution)/shard_map/pallas_call | solution.py:35
  38.9 1.0 %shard_map.100.refs_0_.refs_3_ = f32[240,256]{1,0:T(8,128)S(1)} custom-call(f32[240,256]{1,0:T(8,128)S(1)} %bitcast_select_fusion.refs_0_.refs_3_, s32[240,256]{1,0:T(8,128)S(1)} %get-tuple-element.94.refs_1_, bf16[1792,256]{1,0:T(8,128)(2,1)S(1)} %get-tuple-element.70.refs_2_, bf16[1792,256]{1,0:T(8,128)(2,1)S(1)} %get-tuple-element.71.refs_3_), custom_call_target="tpu_custom_call" | custom-call | flops 660602880 | bytes 2572288 | tf_op jit(solution)/shard_map/pallas_call | solution.py:35
  39.9 0.9 %shard_map.103 = f32[2,4,224,256]{3,2,1,0:T(8,128)S(1)} custom-call(s32[1]{0:T(128)} %bitcast.31.refs_0_, bf16[256,240]{1,0:T(8,128)(2,1)S(1)} %get-tuple-element.107.refs_1_, bf16[256,240]{1,0:T(8,128)(2,1)S(1)} %get-tuple-element.96.refs_2_, f32[240,256]{1,0:T(8,128)S(1)} %shard_map.100.refs_0_.refs_3_, f32[1792,256]{1,0:T(8,128)S(1)} %shard_map.98.refs_4_), custom_call_target="tpu_custom_call" | custom-call | flops 660602880 | bytes 4161540 | tf_op jit(solution)/shard_map/pallas_call | solution.py:35
  41.7 1.7 %collective-permute-start.20 = (f32[2,112,256]{2,1,0:T(8,128)S(1)}, f32[2,112,256]{2,1,0:T(8,128)S(1)}, u32[]{:S(2)}, u32[]{:S(2)}) collective-permute-start(f32[2,112,256]{2,1,0:T(8,128)S(1)} %pad_maximum_fusion), channel_id=1, source_target_pairs={{0,2},{1,3},{2,0},{3,1},{4,6},{5,7},{6,4},{7,5},{8,10},{9,11},{10,... | collective-permute-start | bytes 688136 | tf_op jit(solution)/shard_map/ppermute | solution.py:315
  43.4 1.5 %collective-permute-start.21 = (f32[2,112,256]{2,1,0:T(8,128)S(1)}, f32[2,112,256]{2,1,0:T(8,128)S(1)}, u32[]{:S(2)}, u32[]{:S(2)}) collective-permute-start(f32[2,112,256]{2,1,0:T(8,128)S(1)} %stack.102), channel_id=1, source_target_pairs={{0,4},{1,5},{2,6},{3,7},{4,0},{5,1},{6,2},{7,3},{8,12},{9,13},{10,... | collective-permute-start | bytes 688136 | tf_op jit(solution)/shard_map/ppermute | solution.py:315
  45.7 1.3 %collective-permute-start.24 = (f32[2,112,256]{2,1,0:T(8,128)S(1)}, f32[2,112,256]{2,1,0:T(8,128)S(1)}, u32[]{:S(2)}, u32[]{:S(2)}) collective-permute-start(f32[2,112,256]{2,1,0:T(8,128)S(1)} %stack.103), channel_id=1, source_target_pairs={{0,4},{1,5},{2,6},{3,7},{4,0},{5,1},{6,2},{7,3},{8,12},{9,13},{10,... | collective-permute-start | bytes 688136 | tf_op jit(solution)/shard_map/ppermute | solution.py:315
  47.0 3.2 %collective-permute-done.20 = f32[2,112,256]{2,1,0:T(8,128)S(1)} collective-permute-done((f32[2,112,256]{2,1,0:T(8,128)S(1)}, f32[2,112,256]{2,1,0:T(8,128)S(1)}, u32[]{:S(2)}, u32[]{:S(2)}) %collective-permute-start.20) | collective-permute-done | bytes 229408 | tf_op jit(solution)/shard_map/ppermute | solution.py:315
  50.2 1.7 %collective-permute-done.21 = f32[2,112,256]{2,1,0:T(8,128)S(1)} collective-permute-done((f32[2,112,256]{2,1,0:T(8,128)S(1)}, f32[2,112,256]{2,1,0:T(8,128)S(1)}, u32[]{:S(2)}, u32[]{:S(2)}) %collective-permute-start.21) | collective-permute-done | bytes 229408 | tf_op jit(solution)/shard_map/ppermute | solution.py:315
  52.4 1.6 %collective-permute-start.27 = (f32[112,256]{1,0:T(8,128)S(1)}, f32[112,256]{1,0:T(8,128)S(1)}, u32[]{:S(2)}, u32[]{:S(2)}) collective-permute-start(f32[112,256]{1,0:T(8,128)S(1)} %fusion.5), channel_id=1, source_target_pairs={{0,4},{1,5},{2,6},{3,7},{4,0},{5,1},{6,2},{7,3},{8,12},{9,13},{10,... | collective-permute-start | bytes 344072 | tf_op jit(solution)/shard_map/ppermute | solution.py:315
  54.0 1.1 %collective-permute-done.23 = f32[2,112,256]{2,1,0:T(8,128)S(1)} collective-permute-done((f32[2,112,256]{2,1,0:T(8,128)S(1)}, f32[2,112,256]{2,1,0:T(8,128)S(1)}, u32[]{:S(2)}, u32[]{:S(2)}) %collective-permute-start.23) | collective-permute-done | bytes 229408 | tf_op jit(solution)/shard_map/ppermute | solution.py:315
  55.1 1.6 %collective-permute-done.24 = f32[2,112,256]{2,1,0:T(8,128)S(1)} collective-permute-done((f32[2,112,256]{2,1,0:T(8,128)S(1)}, f32[2,112,256]{2,1,0:T(8,128)S(1)}, u32[]{:S(2)}, u32[]{:S(2)}) %collective-permute-start.24) | collective-permute-done | bytes 229408 | tf_op jit(solution)/shard_map/ppermute | solution.py:315
  57.3 1.6 %collective-permute-start.25 = (f32[112,256]{1,0:T(8,128)S(1)}, f32[112,256]{1,0:T(8,128)S(1)}, u32[]{:S(2)}, u32[]{:S(2)}) collective-permute-start(f32[112,256]{1,0:T(8,128)S(1)} %fusion.11), channel_id=1, source_target_pairs={{0,4},{1,5},{2,6},{3,7},{4,0},{5,1},{6,2},{7,3},{8,12},{9,13},{10,... | collective-permute-start | bytes 344072 | tf_op jit(solution)/shard_map/ppermute | solution.py:315
  58.9 1.9 %shard_map.102 = f32[450,1,256]{2,1,0:T(1,128)} custom-call(f32[240,256]{1,0:T(8,128)S(1)} %shard_map.100.refs_0_.refs_3_, bf16[1792,256]{1,0:T(8,128)(2,1)S(1)} %get-tuple-element.74.refs_1_, bf16[1792,256]{1,0:T(8,128)(2,1)S(1)} %get-tuple-element.75.refs_2_, f32[240,256]{1,0:T(8,128)S(1)} %get-tuple-element.61.refs_3_), custom_call_target="tpu_custom_call" | custom-call | flops 660602880 | bytes 2787328 | tf_op jit(solution)/shard_map/pallas_call | solution.py:35
  60.8 0.7 %maximum_bitcast_fusion.1 = f32[1,224,256]{2,1,0:T(8,128)} fusion(f32[112,256]{1,0:T(8,128)S(1)} %get-tuple-element.87, f32[112,256]{1,0:T(8,128)S(1)} %get-tuple-element.86), kind=kLoop, calls=%fused_computation.12 | loop fusion | flops 57344 | bytes 458752 | tf_op jit(solution)/shard_map/broadcast_in_dim | solution.py:378
  62.1 0.7 %maximum_bitcast_fusion = f32[1,224,256]{2,1,0:T(8,128)} fusion(f32[112,256]{1,0:T(8,128)S(1)} %get-tuple-element.89, f32[112,256]{1,0:T(8,128)S(1)} %get-tuple-element.88), kind=kLoop, calls=%fused_computation.11 | loop fusion | flops 57344 | bytes 458752 | tf_op jit(solution)/shard_map/broadcast_in_dim | solution.py:378
  (81 shorter events, 7.5 us)
Async XLA Ops:
  0.6 9.7 %collective-permute-start.1 = (f32[224,256]{1,0:T(8,128)}, f32[224,256]{1,0:T(8,128)S(1)}, u32[]{:S(2)}, u32[]{:S(2)}) collective-permute-start(f32[224,256]{1,0:T(8,128)} %bitcast.92), channel_id=1, source_target_pairs={{0,4},{1,5},{2,6},{3,7},{4,0},{5,1},{6,2},{7,3},{8,12},{9,13},{10,... | collective-permute-start | bytes 688136 | tf_op jit(solution)/shard_map/ppermute | solution.py:315
  3.7 8.7 %collective-permute-start = (f32[224,256]{1,0:T(8,128)}, f32[224,256]{1,0:T(8,128)S(1)}, u32[]{:S(2)}, u32[]{:S(2)}) collective-permute-start(f32[224,256]{1,0:T(8,128)} %bitcast.93), channel_id=1, source_target_pairs={{0,2},{1,3},{2,0},{3,1},{4,6},{5,7},{6,4},{7,5},{8,10},{9,11},{10,... | collective-permute-start | bytes 688136 | tf_op jit(solution)/shard_map/ppermute | solution.py:315
  5.2 9.2 %collective-permute-start.4 = (f32[224,256]{1,0:T(8,128)}, f32[224,256]{1,0:T(8,128)S(1)}, u32[]{:S(2)}, u32[]{:S(2)}) collective-permute-start(f32[224,256]{1,0:T(8,128)} %bitcast.96), channel_id=1, source_target_pairs={{0,4},{1,5},{2,6},{3,7},{4,0},{5,1},{6,2},{7,3},{8,12},{9,13},{10,... | collective-permute-start | bytes 688136 | tf_op jit(solution)/shard_map/ppermute | solution.py:315
  5.7 10.7 %collective-permute-start.2 = (f32[224,256]{1,0:T(8,128)}, f32[224,256]{1,0:T(8,128)S(1)}, u32[]{:S(2)}, u32[]{:S(2)}) collective-permute-start(f32[224,256]{1,0:T(8,128)} %bitcast.97), channel_id=1, source_target_pairs={{0,2},{1,3},{2,0},{3,1},{4,6},{5,7},{6,4},{7,5},{8,10},{9,11},{10,... | collective-permute-start | bytes 688136 | tf_op jit(solution)/shard_map/ppermute | solution.py:315
  5.8 10.7 %collective-permute-start.10 = (f32[224,256]{1,0:T(8,128)}, f32[224,256]{1,0:T(8,128)S(1)}, u32[]{:S(2)}, u32[]{:S(2)}) collective-permute-start(f32[224,256]{1,0:T(8,128)} %bitcast.94), channel_id=1, source_target_pairs={{0,1},{1,0},{2,3},{3,2},{4,5},{5,4},{6,7},{7,6},{8,9},{9,8},{10,11... | collective-permute-start | bytes 688136 | tf_op jit(solution)/shard_map/ppermute | solution.py:315
  5.8 15.1 %copy-start.2 = (f32[1,224,256]{2,1,0:T(8,128)S(1)}, f32[1,224,256]{2,1,0:T(8,128)}, u32[]{:S(2)}) copy-start(f32[1,224,256]{2,1,0:T(8,128)} %param.12) | copy-start | bytes 688132
  5.8 15.2 %copy-start.1 = (f32[1,224,256]{2,1,0:T(8,128)S(1)}, f32[1,224,256]{2,1,0:T(8,128)}, u32[]{:S(2)}) copy-start(f32[1,224,256]{2,1,0:T(8,128)} %param.13) | copy-start | bytes 688132
  9.1 13.4 %copy-start = (f32[1,240,256]{2,1,0:T(8,128)S(1)}, f32[1,240,256]{2,1,0:T(8,128)}, u32[]{:S(2)}) copy-start(f32[1,240,256]{2,1,0:T(8,128)} %get-tuple-element.45) | copy-start | bytes 737284
  12.4 6.9 %collective-permute-start.11 = (f32[224,256]{1,0:T(8,128)S(1)}, f32[224,256]{1,0:T(8,128)S(1)}, u32[]{:S(2)}, u32[]{:S(2)}) collective-permute-start(f32[224,256]{1,0:T(8,128)S(1)} %collective-permute-done.refs_2_), channel_id=1, source_target_pairs={{0,1},{1,0},{2,3},{3,2},{4,5},{5,4},{6,7},{7,6},{8,9},{9,8},{10,11... | collective-permute-start | bytes 688136 | tf_op jit(solution)/shard_map/ppermute | solution.py:315
  12.4 5.9 %collective-permute-start.7 = (f32[112,256]{1,0:T(8,128)S(1)}, f32[112,256]{1,0:T(8,128)S(1)}, u32[]{:S(2)}, u32[]{:S(2)}) collective-permute-start(f32[112,256]{1,0:T(8,128)S(1)} %slice.144), channel_id=1, source_target_pairs={{0,2},{1,3},{2,0},{3,1},{4,6},{5,7},{6,4},{7,5},{8,10},{9,11},{10,... | collective-permute-start | bytes 344072 | tf_op jit(solution)/shard_map/ppermute | solution.py:315
  14.4 4.9 %collective-permute-start.6 = (f32[112,256]{1,0:T(8,128)S(1)}, f32[112,256]{1,0:T(8,128)S(1)}, u32[]{:S(2)}, u32[]{:S(2)}) collective-permute-start(f32[112,256]{1,0:T(8,128)S(1)} %slice.143), channel_id=1, source_target_pairs={{0,4},{1,5},{2,6},{3,7},{4,0},{5,1},{6,2},{7,3},{8,12},{9,13},{10,... | collective-permute-start | bytes 344072 | tf_op jit(solution)/shard_map/ppermute | solution.py:315
  16.4 4.5 %collective-permute-start.12 = (f32[224,256]{1,0:T(8,128)S(1)}, f32[224,256]{1,0:T(8,128)S(1)}, u32[]{:S(2)}, u32[]{:S(2)}) collective-permute-start(f32[224,256]{1,0:T(8,128)S(1)} %collective-permute-done.1.refs_3_), channel_id=1, source_target_pairs={{0,1},{1,0},{2,3},{3,2},{4,5},{5,4},{6,7},{7,6},{8,9},{9,8},{10,11... | collective-permute-start | bytes 688136 | tf_op jit(solution)/shard_map/ppermute | solution.py:315
  16.5 7.5 %collective-permute-start.5 = (f32[112,256]{1,0:T(8,128)S(1)}, f32[112,256]{1,0:T(8,128)S(1)}, u32[]{:S(2)}, u32[]{:S(2)}) collective-permute-start(f32[112,256]{1,0:T(8,128)S(1)} %slice.179), channel_id=1, source_target_pairs={{0,2},{1,3},{2,0},{3,1},{4,6},{5,7},{6,4},{7,5},{8,10},{9,11},{10,... | collective-permute-start | bytes 344072 | tf_op jit(solution)/shard_map/ppermute | solution.py:315
  18.3 5.7 %collective-permute-start.3 = (f32[112,256]{1,0:T(8,128)S(1)}, f32[112,256]{1,0:T(8,128)S(1)}, u32[]{:S(2)}, u32[]{:S(2)}) collective-permute-start(f32[112,256]{1,0:T(8,128)S(1)} %slice.178), channel_id=1, source_target_pairs={{0,4},{1,5},{2,6},{3,7},{4,0},{5,1},{6,2},{7,3},{8,12},{9,13},{10,... | collective-permute-start | bytes 344072 | tf_op jit(solution)/shard_map/ppermute | solution.py:315
  19.3 2.5 %collective-permute-start.9 = (f32[112,256]{1,0:T(8,128)S(1)}, f32[112,256]{1,0:T(8,128)S(1)}, u32[]{:S(2)}, u32[]{:S(2)}) collective-permute-start(f32[112,256]{1,0:T(8,128)S(1)} %collective-permute-done.7.refs_4_), channel_id=1, source_target_pairs={{0,1},{1,0},{2,3},{3,2},{4,5},{5,4},{6,7},{7,6},{8,9},{9,8},{10,11... | collective-permute-start | bytes 344072 | tf_op jit(solution)/shard_map/ppermute | solution.py:315
  19.3 3.1 %collective-permute-start.8 = (f32[112,256]{1,0:T(8,128)S(1)}, f32[112,256]{1,0:T(8,128)S(1)}, u32[]{:S(2)}, u32[]{:S(2)}) collective-permute-start(f32[112,256]{1,0:T(8,128)S(1)} %collective-permute-done.6.refs_3_), channel_id=1, source_target_pairs={{0,1},{1,0},{2,3},{3,2},{4,5},{5,4},{6,7},{7,6},{8,9},{9,8},{10,11... | collective-permute-start | bytes 344072 | tf_op jit(solution)/shard_map/ppermute | solution.py:315
  20.9 4.7 %collective-permute-start.13 = (f32[224,256]{1,0:T(8,128)S(1)}, f32[224,256]{1,0:T(8,128)S(1)}, u32[]{:S(2)}, u32[]{:S(2)}) collective-permute-start(f32[224,256]{1,0:T(8,128)S(1)} %bitcast.98), channel_id=1, source_target_pairs={{0,1},{1,0},{2,3},{3,2},{4,5},{5,4},{6,7},{7,6},{8,9},{9,8},{10,11... | collective-permute-start | bytes 688136 | tf_op jit(solution)/shard_map/ppermute | solution.py:315
  21.8 3.8 %collective-permute-start.15 = (f32[224,256]{1,0:T(8,128)S(1)}, f32[224,256]{1,0:T(8,128)S(1)}, u32[]{:S(2)}, u32[]{:S(2)}) collective-permute-start(f32[224,256]{1,0:T(8,128)S(1)} %collective-permute-done.4.refs_5_), channel_id=1, source_target_pairs={{0,1},{1,0},{2,3},{3,2},{4,5},{5,4},{6,7},{7,6},{8,9},{9,8},{10,11... | collective-permute-start | bytes 688136 | tf_op jit(solution)/shard_map/ppermute | solution.py:315
  22.3 3.3 %collective-permute-start.14 = (f32[224,256]{1,0:T(8,128)S(1)}, f32[224,256]{1,0:T(8,128)S(1)}, u32[]{:S(2)}, u32[]{:S(2)}) collective-permute-start(f32[224,256]{1,0:T(8,128)S(1)} %collective-permute-done.2.refs_4_), channel_id=1, source_target_pairs={{0,1},{1,0},{2,3},{3,2},{4,5},{5,4},{6,7},{7,6},{8,9},{9,8},{10,11... | collective-permute-start | bytes 688136 | tf_op jit(solution)/shard_map/ppermute | solution.py:315
  24.0 1.6 %collective-permute-start.16 = (f32[112,256]{1,0:T(8,128)S(1)}, f32[112,256]{1,0:T(8,128)S(1)}, u32[]{:S(2)}, u32[]{:S(2)}) collective-permute-start(f32[112,256]{1,0:T(8,128)S(1)} %collective-permute-done.3.refs_8_), channel_id=1, source_target_pairs={{0,1},{1,0},{2,3},{3,2},{4,5},{5,4},{6,7},{7,6},{8,9},{9,8},{10,11... | collective-permute-start | bytes 344072 | tf_op jit(solution)/shard_map/ppermute | solution.py:315
  24.5 1.3 %collective-permute-start.17 = (f32[112,256]{1,0:T(8,128)S(1)}, f32[112,256]{1,0:T(8,128)S(1)}, u32[]{:S(2)}, u32[]{:S(2)}) collective-permute-start(f32[112,256]{1,0:T(8,128)S(1)} %collective-permute-done.5.refs_9_), channel_id=1, source_target_pairs={{0,1},{1,0},{2,3},{3,2},{4,5},{5,4},{6,7},{7,6},{8,9},{9,8},{10,11... | collective-permute-start | bytes 344072 | tf_op jit(solution)/shard_map/ppermute | solution.py:315
  27.7 10.1 %collective-permute-start.18 = (f32[240,256]{1,0:T(8,128)S(1)}, f32[240,256]{1,0:T(8,128)S(1)}, u32[]{:S(2)}, u32[]{:S(2)}) collective-permute-start(f32[240,256]{1,0:T(8,128)S(1)} %get-tuple-element.61.refs_3_), channel_id=1, source_target_pairs={{8,0},{16,8},{24,16},{9,1},{17,9},{25,17},{10,2},{18,10},{26,18},{... | collective-permute-start | bytes 737288 | tf_op jit(solution)/shard_map/ppermute | solution.py:497
  38.8 2.6 %collective-permute-start.19 = (f32[4,224,256]{2,1,0:T(8,128)S(1)}, f32[4,224,256]{2,1,0:T(8,128)S(1)}, u32[]{:S(2)}, u32[]{:S(2)}) collective-permute-start(f32[4,224,256]{2,1,0:T(8,128)S(1)} %slice_bitcast_fusion.2), channel_id=1, source_target_pairs={{0,1},{1,0},{2,3},{3,2},{4,5},{5,4},{6,7},{7,6},{8,9},{9,8},{10,11... | collective-permute-start | bytes 2752520 | tf_op jit(solution)/shard_map/ppermute | solution.py:315
  40.9 4.0 %collective-permute-start.22 = (f32[4,224,256]{2,1,0:T(8,128)S(1)}, f32[4,224,256]{2,1,0:T(8,128)S(1)}, u32[]{:S(2)}, u32[]{:S(2)}) collective-permute-start(f32[4,224,256]{2,1,0:T(8,128)S(1)} %slice_bitcast_fusion), channel_id=1, source_target_pairs={{0,1},{1,0},{2,3},{3,2},{4,5},{5,4},{6,7},{7,6},{8,9},{9,8},{10,11... | collective-permute-start | bytes 2752520 | tf_op jit(solution)/shard_map/ppermute | solution.py:315
  41.7 8.5 %collective-permute-start.20 = (f32[2,112,256]{2,1,0:T(8,128)S(1)}, f32[2,112,256]{2,1,0:T(8,128)S(1)}, u32[]{:S(2)}, u32[]{:S(2)}) collective-permute-start(f32[2,112,256]{2,1,0:T(8,128)S(1)} %pad_maximum_fusion), channel_id=1, source_target_pairs={{0,2},{1,3},{2,0},{3,1},{4,6},{5,7},{6,4},{7,5},{8,10},{9,11},{10,... | collective-permute-start | bytes 688136 | tf_op jit(solution)/shard_map/ppermute | solution.py:315
  43.4 8.5 %collective-permute-start.21 = (f32[2,112,256]{2,1,0:T(8,128)S(1)}, f32[2,112,256]{2,1,0:T(8,128)S(1)}, u32[]{:S(2)}, u32[]{:S(2)}) collective-permute-start(f32[2,112,256]{2,1,0:T(8,128)S(1)} %stack.102), channel_id=1, source_target_pairs={{0,4},{1,5},{2,6},{3,7},{4,0},{5,1},{6,2},{7,3},{8,12},{9,13},{10,... | collective-permute-start | bytes 688136 | tf_op jit(solution)/shard_map/ppermute | solution.py:315
  45.1 10.0 %collective-permute-start.23 = (f32[2,112,256]{2,1,0:T(8,128)S(1)}, f32[2,112,256]{2,1,0:T(8,128)S(1)}, u32[]{:S(2)}, u32[]{:S(2)}) collective-permute-start(f32[2,112,256]{2,1,0:T(8,128)S(1)} %pad_maximum_fusion.1), channel_id=1, source_target_pairs={{0,2},{1,3},{2,0},{3,1},{4,6},{5,7},{6,4},{7,5},{8,10},{9,11},{10,... | collective-permute-start | bytes 688136 | tf_op jit(solution)/shard_map/ppermute | solution.py:315
  45.7 11.1 %collective-permute-start.24 = (f32[2,112,256]{2,1,0:T(8,128)S(1)}, f32[2,112,256]{2,1,0:T(8,128)S(1)}, u32[]{:S(2)}, u32[]{:S(2)}) collective-permute-start(f32[2,112,256]{2,1,0:T(8,128)S(1)} %stack.103), channel_id=1, source_target_pairs={{0,4},{1,5},{2,6},{3,7},{4,0},{5,1},{6,2},{7,3},{8,12},{9,13},{10,... | collective-permute-start | bytes 688136 | tf_op jit(solution)/shard_map/ppermute | solution.py:315
  51.9 8.9 %collective-permute-start.28 = (f32[112,256]{1,0:T(8,128)S(1)}, f32[112,256]{1,0:T(8,128)S(1)}, u32[]{:S(2)}, u32[]{:S(2)}) collective-permute-start(f32[112,256]{1,0:T(8,128)S(1)} %fusion.2), channel_id=1, source_target_pairs={{0,2},{1,3},{2,0},{3,1},{4,6},{5,7},{6,4},{7,5},{8,10},{9,11},{10,... | collective-permute-start | bytes 344072 | tf_op jit(solution)/shard_map/ppermute | solution.py:315
  52.4 8.4 %collective-permute-start.27 = (f32[112,256]{1,0:T(8,128)S(1)}, f32[112,256]{1,0:T(8,128)S(1)}, u32[]{:S(2)}, u32[]{:S(2)}) collective-permute-start(f32[112,256]{1,0:T(8,128)S(1)} %fusion.5), channel_id=1, source_target_pairs={{0,4},{1,5},{2,6},{3,7},{4,0},{5,1},{6,2},{7,3},{8,12},{9,13},{10,... | collective-permute-start | bytes 344072 | tf_op jit(solution)/shard_map/ppermute | solution.py:315
  56.8 4.9 %collective-permute-start.26 = (f32[112,256]{1,0:T(8,128)S(1)}, f32[112,256]{1,0:T(8,128)S(1)}, u32[]{:S(2)}, u32[]{:S(2)}) collective-permute-start(f32[112,256]{1,0:T(8,128)S(1)} %fusion.8), channel_id=1, source_target_pairs={{0,2},{1,3},{2,0},{3,1},{4,6},{5,7},{6,4},{7,5},{8,10},{9,11},{10,... | collective-permute-start | bytes 344072 | tf_op jit(solution)/shard_map/ppermute | solution.py:315
  57.3 4.8 %collective-permute-start.25 = (f32[112,256]{1,0:T(8,128)S(1)}, f32[112,256]{1,0:T(8,128)S(1)}, u32[]{:S(2)}, u32[]{:S(2)}) collective-permute-start(f32[112,256]{1,0:T(8,128)S(1)} %fusion.11), channel_id=1, source_target_pairs={{0,4},{1,5},{2,6},{3,7},{4,0},{5,1},{6,2},{7,3},{8,12},{9,13},{10,... | collective-permute-start | bytes 344072 | tf_op jit(solution)/shard_map/ppermute | solution.py:315
  (5 other events, 26.5 us)

commit v4 on v3

--- a/solution.py
+++ b/solution.py
@@ -11,8 +11,6 @@
 REACH = TAPS // 2
 GROUP = 16
 LANES = 128
-COST = 1
-PREP = 60
 F32 = jnp.float32
 BF16 = jnp.bfloat16
 NT = (((1,), (1,)), ((), ()))
@@ -20,13 +18,6 @@
 VMEM = pl.BlockSpec(memory_space=pltpu.VMEM)
 SMEM = pl.BlockSpec(memory_space=pltpu.SMEM)
 HBM = pl.BlockSpec(memory_space=pltpu.HBM)
-
-
-KNOBS = {'prep': 1, 'early2': 1, 'pretie': 1, 'fs': 1}
-
-
-def knob(name, default=0):
-    return KNOBS.get(name, default)
 
 
 def call(kernel, out_shapes, scratch, flops, *operands, scalars=0, aliases=None, far=False, vmem=12):
@@ -40,7 +31,7 @@
         scratch_shapes=scratch,
         input_output_aliases=aliases or {},
         compiler_params=pltpu.CompilerParams(vmem_limit_bytes=vmem * 1024 * 1024),
-        cost_estimate=pl.CostEstimate(flops=int(flops * COST), bytes_accessed=int(moved * COST), transcendentals=0),
+        cost_estimate=pl.CostEstimate(flops=flops, bytes_accessed=moved, transcendentals=0),
     )(*operands)
 
 
@@ -165,9 +156,10 @@
 
 
 def spread(line_ref, start, height, width, out_ref):
-    out_ref[...] = jnp.zeros_like(out_ref)
+    tail = jnp.zeros((GROUP - width, out_ref.shape[-1]), line_ref.dtype)
     for row in range(height):
-        out_ref[pl.ds(row * GROUP, width), :] = line_ref[pl.ds(start + row * width, width), 0, :]
+        taken = jnp.concatenate([line_ref[pl.ds(start + row * width, width), 0, :], tail])
+        out_ref[pl.ds(row * GROUP, GROUP), :] = taken.astype(out_ref.dtype)
 
 
 def prepare_kernel(height, width, *refs):
@@ -199,6 +191,7 @@
     sources = [came, mask, loss, act_in, act_mid]
     ticks, channels = act_in.shape[0] // (height * width), act_in.shape[2]
     out = [jax.ShapeDtypeStruct((x.shape[0] // (height * width), height * GROUP, channels), x.dtype) for x in sources[:3]]
+    out[1] = jax.ShapeDtypeStruct(out[1].shape, BF16)
     out += [jax.ShapeDtypeStruct((ticks, channels, width * GROUP), BF16)] * 2
     out += [jax.ShapeDtypeStruct((ticks, channels, height * GROUP), BF16)] * 2
     scratch = [pltpu.VMEM(x.shape, x.dtype) for x in sources]
@@ -209,7 +202,7 @@
         pltpu.SemaphoreType.DMA((len(sources),)),
     ]
     kernel = functools.partial(prepare_kernel, height, width)
-    came, mask, loss, *parts = call(kernel, out, scratch, 0, *sources, far=True, vmem=PREP)
+    came, mask, loss, *parts = call(kernel, out, scratch, 0, *sources, far=True, vmem=60)
     return mask, loss, came[0], *parts
 
 
@@ -368,8 +361,7 @@
 
 def far_phase(a, b, a_there, b_there):
     a_near, a_far = a[0] + a_there[0], a[2] + a_there[1]
-    if knob("fs"):
-        a_far, b_there = together(a_far, b_there)
+    a_far, b_there = together(a_far, b_there)
     b_near, b_far = b[0] + b_there[0], b[1] + b_there[1]
     return a_near, b_near, swap(a_far, 4), swap(b_far, 2)
 
@@ -394,105 +386,33 @@
     one, two = w_first[0], w_second[0]
     rows = one.shape[0]
     half = rows // 2
-    owners = jnp.reshape(me, (1,)).astype(jnp.int32)
+    number = jnp.reshape(me, (1,)).astype(jnp.int32)
     x_two, y_two = swap(two, 2), swap(two, 4)
     x_one, y_one = swap(one, 2), swap(one, 4)
     s_two, s_one = swap(two, 1), swap(one, 1)
     mask, loss, incoming, in_high, in_low, mid_high, mid_low = prepare(
         height, width, line(relu_mask), line(loss_grad), line(arriving), line(act_in), line(act_mid)
     )
-    if knob("mask"):
-        mask = [mask[tick] for tick in range(ticks)]
-        if knob("mask") == 2:
-            *mask, y_two = together(*mask, y_two)
-    if knob("prep") == 4:
-        mask, loss, incoming, x_two, in_high, in_low, mid_high, mid_low = together(
-            mask, loss, incoming, x_two, in_high, in_low, mid_high, mid_low
-        )
-    elif knob("prep") == 0:
-        mask, loss, incoming, x_two, y_two = together(mask, loss, incoming, x_two, y_two)
-    elif knob("prep") == 1:
-        mask, loss, incoming, x_two, y_two, in_high, in_low, mid_high, mid_low = together(
-            mask, loss, incoming, x_two, y_two, in_high, in_low, mid_high, mid_low
-        )
-    elif knob("prep") == 2:
-        mask, loss, incoming, x_two, y_two, s_two, in_high, in_low, mid_high, mid_low = together(
-            mask, loss, incoming, x_two, y_two, s_two, in_high, in_low, mid_high, mid_low
-        )
-    elif knob("prep") == 3:
-        mask, loss, incoming, x_two, y_two, s_two = together(mask, loss, incoming, x_two, y_two, s_two)
+    mask, loss, incoming, x_two, y_two, in_high, in_low, mid_high, mid_low = together(
+        mask, loss, incoming, x_two, y_two, in_high, in_low, mid_high, mid_low
+    )
     ya_two, xb_two = far_pieces(x_two, y_two)
-    if knob("near") == 0:
-        sx_two, sy_two = swap(x_two, 1), swap(y_two, 1)
-        near_two = [(x_two, 2, 0), (y_two, 4, 0), (sx_two, 3, 0), (sy_two, 5, 0)]
-    else:
-        n_two = jnp.concatenate([x_two, y_two])
-        near_two = [(n_two, (2, 4), 0), (swap(n_two, 1), (3, 5), 0)]
-    come = [(two, 0, 0), (s_two, 1, 0)] + near_two
-    second_parts = None
-    if knob("early2"):
-        second_parts = placed(*starts_of(me, rows, rows, come), filter_rows)
-        come = []
-    if knob("g2") == 0:
-        second = correlate(mid_high[0], mid_low[0], incoming, scale)
-    if knob("tie2") == 1:
-        x_one, y_one, second = together(x_one, y_one, second)
-    elif knob("tie2") == 2:
-        x_one, y_one, *second_parts = together(x_one, y_one, *second_parts)
-    elif knob("tie2") == 3:
-        x_one, y_one, in_high, in_low, mid_high, mid_low = together(
-            x_one, y_one, in_high, in_low, mid_high, mid_low
-        )
-    if knob("late1") == 1:
-        s_one = swap(together(one, x_two)[0], 1)
-    elif knob("late1") == 2:
-        s_one = swap(together(one, x_one, y_one)[0], 1)
-    if knob("far1") == 0:
-        ya_one, xb_one = far_pieces(x_one, y_one)
-        far_one = [(ya_one, 6, 0), (xb_one, 6, half)]
-    else:
-        d_one = swap(together(one, x_two, y_two)[0], 6)
-        far_one = [(d_one, 6, 0)]
-    if knob("near") == 0:
-        sx_one, sy_one = swap(x_one, 1), swap(y_one, 1)
-        near_one = [(x_one, 2, 0), (y_one, 4, 0), (sx_one, 3, 0), (sy_one, 5, 0)]
-    else:
-        n_one = jnp.concatenate([x_one, y_one])
-        near_one = [(n_one, (2, 4), 0), (swap(n_one, 1), (3, 5), 0)]
-    if knob("farcat"):
-        f_two = jnp.concatenate([ya_two, xb_two])
-        come += [(f_two, 6, 0), (swap(f_two, 1), 7, 0)]
-    else:
-        sya_two, sxb_two = swap(ya_two, 1), swap(xb_two, 1)
-        come += [(ya_two, 6, 0), (xb_two, 6, half), (sya_two, 7, 0), (sxb_two, 7, half)]
+    sx_two, sy_two = swap(x_two, 1), swap(y_two, 1)
+    come = [(two, 0, 0), (s_two, 1, 0), (x_two, 2, 0), (y_two, 4, 0), (sx_two, 3, 0), (sy_two, 5, 0)]
+    second_parts = placed(*starts_of(me, rows, rows, come), filter_rows)
+    ya_one, xb_one = far_pieces(x_one, y_one)
+    sx_one, sy_one = swap(x_one, 1), swap(y_one, 1)
+    sya_two, sxb_two = swap(ya_two, 1), swap(xb_two, 1)
+    come = [(ya_two, 6, 0), (xb_two, 6, half), (sya_two, 7, 0), (sxb_two, 7, half)]
     pre, *second_parts = conv(incoming, mask[0], width, weights=second_parts, pieces=starts_of(me, rows, half, come))
-    come = [(one, 0, 0), (s_one, 1, 0)] + near_one
-    first_parts = None
-    if knob("early1"):
-        first_parts = placed(*starts_of(me, rows, rows, come), filter_rows)
-        come = []
-    if knob("pretie") == 1:
-        ends, pre = [piece for piece, _, _ in far_one], pre
-        *ends, pre = together(*ends, pre)
-        far_one = [(end, bits, offset) for end, (_, bits, offset) in zip(ends, far_one)]
-    elif knob("pretie") == 2:
-        *ends, pre, first_high, first_low = together(*[piece for piece, _, _ in far_one], pre, *first_parts)
-        first_parts = [first_high, first_low]
-        far_one = [(end, bits, offset) for end, (_, bits, offset) in zip(ends, far_one)]
-    if knob("farcat") and len(far_one) == 2:
-        far_one = [(jnp.concatenate([piece for piece, _, _ in far_one]), 6, 0)]
-    come += far_one + [(swap(piece, 1), bits ^ 1, offset) for piece, bits, offset in far_one]
+    come = [(one, 0, 0), (s_one, 1, 0), (x_one, 2, 0), (y_one, 4, 0), (sx_one, 3, 0), (sy_one, 5, 0)]
+    first_parts = placed(*starts_of(me, rows, rows, come), filter_rows)
+    ya_one, xb_one, pre = together(ya_one, xb_one, pre)
+    come = [(ya_one, 6, 0), (xb_one, 6, half), (swap(ya_one, 1), 7, 0), (swap(xb_one, 1), 7, half)]
     out, *first_parts = conv(pre, None, height, weights=first_parts, pieces=starts_of(me, rows, half, come))
     outs = [out]
     in_high, in_low, pre, _ = together(in_high, in_low, pre, out)
-    if knob("g2") == 1:
-        mid_high, mid_low, _ = together(mid_high, mid_low, out)
-        second = correlate(mid_high[0], mid_low[0], incoming, scale)
-    if knob("g2") == 2:
-        mid_high, mid_low, _ = together(mid_high, mid_low, out)
-        second, first = correlate_both((mid_high[0], mid_low[0]), incoming, (in_high[0], in_low[0]), pre, scale)
-    else:
-        first = correlate(in_high[0], in_low[0], pre, scale)
+    second, first = correlate_both((mid_high[0], mid_low[0]), incoming, (in_high[0], in_low[0]), pre, scale)
     for tick in range(1, ticks):
         above = lax.ppermute(outs[-1], "section", [(i, i - 1) for i in range(1, sections)])
         above, first, second = together(above, first, second)
@@ -502,31 +422,17 @@
             pre = conv(incoming, mask[tick], width, weights=second_parts)
             first = correlate(in_high[tick], in_low[tick], pre, scale, first)
             outs.append(conv(pre, None, height, weights=first_parts))
-    dealt = correlate(mid_high[-1], mid_low[-1], incoming, scale, second, owners)
+    dealt = correlate(mid_high[-1], mid_low[-1], incoming, scale, second, number)
     kept, other = dealt[0], swap(dealt[1], 1)
     pre = conv(incoming, mask[-1], width, weights=second_parts)
-    first_dealt = correlate(in_high[-1], in_low[-1], pre, scale, first, owners)
+    first_dealt = correlate(in_high[-1], in_low[-1], pre, scale, first, number)
     first_kept, first_other = first_dealt[0], swap(first_dealt[1], 1)
     a, b, a_there, b_there = near_phase(kept + other)
-    if knob("rs") == 3:
-        data_grad = last_conv(pre, first_parts, outs, height, width)
-        first_other, data_grad = together(first_other, data_grad)
     first_a, first_b, first_a_there, first_b_there = near_phase(first_kept + first_other)
-    if knob("rs") == 0:
-        pre, a_there, b_there = together(pre, a_there, b_there)
-    elif knob("rs") == 1:
-        pre, first_a_there, first_b_there = together(pre, first_a_there, first_b_there)
-    elif knob("rs") == 2:
-        pre, first_other = together(pre, first_other)
+    pre, a_there, b_there = together(pre, a_there, b_there)
     last = far_phase(a, b, a_there, b_there)
-    if knob("rs") != 3:
-        data_grad = last_conv(pre, first_parts, outs, height, width)
-    if knob("rs") == 2:
-        data_grad, first_a_there, first_b_there = together(data_grad, first_a_there, first_b_there)
+    data_grad = last_conv(pre, first_parts, outs, height, width)
     first_last = far_phase(first_a, first_b, first_a_there, first_b_there)
-    if knob("join"):
-        both = together(*last, *first_last)
-        last, first_last = both[:4], both[4:]
     return data_grad.reshape((1, ticks, images, height, width, channels)), join(*first_last), join(*last)
 
 

time: 63 us -> 62.4 us (level)
    ppermute x1, waiting for transfers between devices: 7.69 us -> 6.94 us  [local_eight(): lax.ppermute(outs[-1], 'section', [(i, i - 1) for i in range(1, sections)])]
  transfers between devices with their start and end apart: 29 -> 29, of which waited for: 13 -> 13; matrix products, arithmetic and copies ran while one was open for 4% -> 4% of each run, Pallas kernels for 18% -> 19%
where the time goes in v4:
time: 62.4 us; the launch traced here: 62.3 us
  starting transfers between devices  23.5 us (38%)
  waiting for transfers between devices  20.2 us (32%)
  Pallas kernels  14.2 us (23%)
  other arithmetic  1.94 us (3%)
  local copies, waits for them, and re-layouts  1.42 us (2%)
  between operations  1.06 us (2%)
    ppermute x28, starting transfers between devices, swap(): return lax.ppermute(shard, 'dp', [(i, i ^ bit) for i in range(peers)])  22.2 us
    pallas_call x10, Pallas kernels, call(): pl.pallas_call(kernel, out_shape=out_shapes, in_specs=[SMEM] * scalars +...  14.2 us
    ppermute x28, waiting for transfers between devices, swap(): return lax.ppermute(shard, 'dp', [(i, i ^ bit) for i in range(peers)])  13.2 us
    ppermute x1, waiting for transfers between devices, local_eight(): lax.ppermute(outs[-1], 'section', [(i, i - 1) for i in range(1, sections)])  6.94 us
    broadcast_in_dim x2, other arithmetic, join(): return jnp.concatenate([a_near + a_last, b_near + b_last], axis=0)[None]  1.41 us
    ppermute x1, starting transfers between devices, local_eight(): lax.ppermute(outs[-1], 'section', [(i, i - 1) for i in range(1, sections)])  1.29 us
  transfers between devices with their start and end apart: 29, of which 13 were waited for; matrix products, arithmetic and copies ran while one was open for 4% of the time, Pallas kernels for 19%

profile of v4, /device:TPU:0, one launch (start us, length us, event | category | flops | bytes accessed | tf_op | source)
XLA Modules:
  0.0 62.3 jit_solution(9791624141587782692)
XLA Ops:
  0.7 3.0 %collective-permute-start.1 = (f32[224,256]{1,0:T(8,128)}, f32[224,256]{1,0:T(8,128)S(1)}, u32[]{:S(2)}, u32[]{:S(2)}) collective-permute-start(f32[224,256]{1,0:T(8,128)} %bitcast.86), channel_id=1, source_target_pairs={{0,4},{1,5},{2,6},{3,7},{4,0},{5,1},{6,2},{7,3},{8,12},{9,13},{10,... | collective-permute-start | bytes 688136 | tf_op jit(solution)/shard_map/ppermute | solution.py:308
  3.7 1.5 %collective-permute-start = (f32[224,256]{1,0:T(8,128)}, f32[224,256]{1,0:T(8,128)S(1)}, u32[]{:S(2)}, u32[]{:S(2)}) collective-permute-start(f32[224,256]{1,0:T(8,128)} %bitcast.87), channel_id=1, source_target_pairs={{0,2},{1,3},{2,0},{3,1},{4,6},{5,7},{6,4},{7,5},{8,10},{9,11},{10,... | collective-permute-start | bytes 688136 | tf_op jit(solution)/shard_map/ppermute | solution.py:308
  5.8 3.2 %shard_map.94 = (f32[1,240,256]{2,1,0:T(8,128)}, bf16[2,240,256]{2,1,0:T(8,128)(2,1)}, f32[1,240,256]{2,1,0:T(8,128)}, bf16[2,256,240]{2,1,0:T(8,128)(2,1)}, bf1...) custom-call(f32[225,1,256]{2,1,0:T(1,128)} %bitcast.98, ...), custom_call_target="tpu_custom_call" | custom-call | bytes 3563520 | tf_op jit(solution)/shard_map/pallas_call | solution.py:26
  9.0 1.3 %collective-permute-done.1.refs_3_ = f32[224,256]{1,0:T(8,128)S(1)} collective-permute-done((f32[224,256]{1,0:T(8,128)}, f32[224,256]{1,0:T(8,128)S(1)}, u32[]{:S(2)}, u32[]{:S(2)}) %collective-permute-start.1) | collective-permute-done | bytes 229408 | tf_op jit(solution)/shard_map/ppermute | solution.py:308
  10.3 2.1 %collective-permute-done.refs_2_ = f32[224,256]{1,0:T(8,128)S(1)} collective-permute-done((f32[224,256]{1,0:T(8,128)}, f32[224,256]{1,0:T(8,128)S(1)}, u32[]{:S(2)}, u32[]{:S(2)}) %collective-permute-start) | collective-permute-done | bytes 229408 | tf_op jit(solution)/shard_map/ppermute | solution.py:308
  12.5 1.6 %collective-permute-start.7 = (f32[112,256]{1,0:T(8,128)S(1)}, f32[112,256]{1,0:T(8,128)S(1)}, u32[]{:S(2)}, u32[]{:S(2)}) collective-permute-start(f32[112,256]{1,0:T(8,128)S(1)} %slice.144), channel_id=1, source_target_pairs={{0,2},{1,3},{2,0},{3,1},{4,6},{5,7},{6,4},{7,5},{8,10},{9,11},{10,... | collective-permute-start | bytes 344072 | tf_op jit(solution)/shard_map/ppermute | solution.py:308
  14.4 1.7 %collective-permute-start.6 = (f32[112,256]{1,0:T(8,128)S(1)}, f32[112,256]{1,0:T(8,128)S(1)}, u32[]{:S(2)}, u32[]{:S(2)}) collective-permute-start(f32[112,256]{1,0:T(8,128)S(1)} %slice.143), channel_id=1, source_target_pairs={{0,4},{1,5},{2,6},{3,7},{4,0},{5,1},{6,2},{7,3},{8,12},{9,13},{10,... | collective-permute-start | bytes 344072 | tf_op jit(solution)/shard_map/ppermute | solution.py:308
  16.4 1.6 %collective-permute-start.5 = (f32[112,256]{1,0:T(8,128)S(1)}, f32[112,256]{1,0:T(8,128)S(1)}, u32[]{:S(2)}, u32[]{:S(2)}) collective-permute-start(f32[112,256]{1,0:T(8,128)S(1)} %slice.179), channel_id=1, source_target_pairs={{0,2},{1,3},{2,0},{3,1},{4,6},{5,7},{6,4},{7,5},{8,10},{9,11},{10,... | collective-permute-start | bytes 344072 | tf_op jit(solution)/shard_map/ppermute | solution.py:308
  18.7 0.6 collective-permute-done.6.refs_3_
  19.8 1.0 %slice_bitcast_fusion.12 = (bf16[240,256]{1,0:T(8,128)(2,1)S(1)}, bf16[240,256]{1,0:T(8,128)(2,1)S(1)}) fusion(bf16[2,240,256]{2,1,0:T(8,128)(2,1)} %get-tuple-element.56), kind=kLoop, calls=%fused_computation.19 | loop fusion | bytes 491520 | tf_op jit(solution)/shard_map/squeeze | solution.py:427
  20.9 0.7 %shard_map.95 = (bf16[1792,256]{1,0:T(8,128)(2,1)S(1)}, bf16[1792,256]{1,0:T(8,128)(2,1)S(1)}) custom-call(s32[6]{0:T(128)S(1)} %stack.71.starts_ref, f32[224,256]{1,0:T(8,128)S(1)} %bitcast.89, f32[224,256]{1,0:T(8,128)S(1)} %collective-permute-done.10.refs_1_, f32[224,256]{1,0:T(8,128)S(1)} %collective-permute-done.refs_2_, ...), custom_call_target="tpu_custom_call" | custom-call | bytes 3211288 | tf_op jit(solution)/shard_map/pallas_call | solution.py:26
  22.3 1.6 %shard_map.96 = (f32[240,256]{1,0:T(8,128)S(1)}, bf16[1792,256]{1,0:T(8,128)(2,1)S(1)}, bf16[1792,256]{1,0:T(8,128)(2,1)S(1)}) custom-call(s32[4]{0:T(128)S(1)} %pad_add_fusion.refs_0_, f32[240,256]{1,0:T(8,128)S(1)} %bitcast.84, bf16[240,256]{1,0:T(8,128)(2,1)S(1)} %get-tuple-element.111.refs_2_, ...), custom_call_target="tpu_custom_call", output_to_operand_aliasing={{1}: (7, {}), {2}: (8, {})} | custom-call | flops 660602880 | bytes 4743184 | tf_op jit(solution)/shard_map/pallas_call | solution.py:26
  24.6 0.8 %shard_map.97 = (bf16[1792,256]{1,0:T(8,128)(2,1)S(1)}, bf16[1792,256]{1,0:T(8,128)(2,1)S(1)}) custom-call(s32[6]{0:T(128)S(1)} %stack.71.starts_ref, f32[224,256]{1,0:T(8,128)S(1)} %bitcast.93, f32[224,256]{1,0:T(8,128)S(1)} %collective-permute-done.15.refs_1_, f32[224,256]{1,0:T(8,128)S(1)} %collective-permute-done.2.refs_2_, ...), custom_call_target="tpu_custom_call" | custom-call | bytes 3211288 | tf_op jit(solution)/shard_map/pallas_call | solution.py:26
  25.8 1.6 %shard_map.98 = (f32[240,256]{1,0:T(8,128)S(1)}, bf16[1792,256]{1,0:T(8,128)(2,1)S(1)}, bf16[1792,256]{1,0:T(8,128)(2,1)S(1)}) custom-call(s32[4]{0:T(128)S(1)} %pad_add_fusion.refs_0_, f32[240,256]{1,0:T(8,128)S(1)} %get-tuple-element.74.refs_1_.refs_5_, ...), custom_call_target="tpu_custom_call", output_to_operand_aliasing={{1}: (6, {}), {2}: (7, {})} | custom-call | flops 660602880 | bytes 4620304 | tf_op jit(solution)/shard_map/pallas_call | solution.py:26
  27.3 1.3 %collective-permute-start.18 = (f32[240,256]{1,0:T(8,128)S(1)}, f32[240,256]{1,0:T(8,128)S(1)}, u32[]{:S(2)}, u32[]{:S(2)}) collective-permute-start(f32[240,256]{1,0:T(8,128)S(1)} %get-tuple-element.67.refs_3_), channel_id=1, source_target_pairs={{8,0},{16,8},{24,16},{9,1},{17,9},{25,17},{10,2},{18,10},{26,18},{... | collective-permute-start | bytes 737288 | tf_op jit(solution)/shard_map/ppermute | solution.py:417
  28.7 1.6 %shard_map.99 = (f32[1792,256]{1,0:T(8,128)S(1)}, f32[1792,256]{1,0:T(8,128)S(1)}) custom-call(bf16[256,240]{1,0:T(8,128)(2,1)S(1)} %get-tuple-element.112.refs_0_, bf16[256,240]{1,0:T(8,128)(2,1)S(1)} %get-tuple-element.107.refs_1_, f32[240,256]{1,0:T(8,128)S(1)} %bitcast.85, bf16[256,240]{1,0:T(8,128)(2,1)S(1)} %get-tuple-element.114.refs_3_, ...), custom_call_target="tpu_custom_call" | custom-call | flops 1321205760 | bytes 4653056 | tf_op jit(solution)/shard_map/pallas_call | solution.py:26
  30.3 6.9 %collective-permute-done.18 = f32[240,256]{1,0:T(8,128)S(1)} collective-permute-done((f32[240,256]{1,0:T(8,128)S(1)}, f32[240,256]{1,0:T(8,128)S(1)}, u32[]{:S(2)}, u32[]{:S(2)}) %collective-permute-start.18) | collective-permute-done | bytes 245792 | tf_op jit(solution)/shard_map/ppermute | solution.py:417
  37.3 0.9 %shard_map.101 = f32[2,4,224,256]{3,2,1,0:T(8,128)S(1)} custom-call(s32[1]{0:T(128)} %bitcast.25.refs_0_, bf16[256,240]{1,0:T(8,128)(2,1)S(1)} %get-tuple-element.113.refs_1_, bf16[256,240]{1,0:T(8,128)(2,1)S(1)} %get-tuple-element.106.refs_2_, f32[240,256]{1,0:T(8,128)S(1)} %bitcast_select_fusion.refs_0_.refs_3_, f32[1792,256]{1,0:T(8,128)S(1)} %get-tuple-element.80.refs_4_), custom_call_target="tpu_custom_call" | custom-call | flops 660602880 | bytes 4161540 | tf_op jit(solution)/shard_map/pallas_call | solution.py:26
  38.4 1.0 %shard_map.100.refs_0_.refs_3_ = f32[240,256]{1,0:T(8,128)S(1)} custom-call(f32[240,256]{1,0:T(8,128)S(1)} %bitcast_select_fusion.refs_0_.refs_3_, bf16[240,256]{1,0:T(8,128)(2,1)S(1)} %get-tuple-element.110.refs_1_, bf16[1792,256]{1,0:T(8,128)(2,1)S(1)} %get-tuple-element.78.refs_2_, bf16[1792,256]{1,0:T(8,128)(2,1)S(1)} %get-tuple-element.79.refs_3_), custom_call_target="tpu_custom_call" | custom-call | flops 660602880 | bytes 2449408 | tf_op jit(solution)/shard_map/pallas_call | solution.py:26
  39.4 0.9 %shard_map.103 = f32[2,4,224,256]{3,2,1,0:T(8,128)S(1)} custom-call(s32[1]{0:T(128)} %bitcast.25.refs_0_, bf16[256,240]{1,0:T(8,128)(2,1)S(1)} %get-tuple-element.115.refs_1_, bf16[256,240]{1,0:T(8,128)(2,1)S(1)} %get-tuple-element.102.refs_2_, f32[240,256]{1,0:T(8,128)S(1)} %shard_map.100.refs_0_.refs_3_, f32[1792,256]{1,0:T(8,128)S(1)} %get-tuple-element.84.refs_4_), custom_call_target="tpu_custom_call" | custom-call | flops 660602880 | bytes 4161540 | tf_op jit(solution)/shard_map/pallas_call | solution.py:26
  41.1 1.7 %collective-permute-start.20 = (f32[2,112,256]{2,1,0:T(8,128)S(1)}, f32[2,112,256]{2,1,0:T(8,128)S(1)}, u32[]{:S(2)}, u32[]{:S(2)}) collective-permute-start(f32[2,112,256]{2,1,0:T(8,128)S(1)} %pad_maximum_fusion), channel_id=1, source_target_pairs={{0,2},{1,3},{2,0},{3,1},{4,6},{5,7},{6,4},{7,5},{8,10},{9,11},{10,... | collective-permute-start | bytes 688136 | tf_op jit(solution)/shard_map/ppermute | solution.py:308
  42.8 1.5 %collective-permute-start.21 = (f32[2,112,256]{2,1,0:T(8,128)S(1)}, f32[2,112,256]{2,1,0:T(8,128)S(1)}, u32[]{:S(2)}, u32[]{:S(2)}) collective-permute-start(f32[2,112,256]{2,1,0:T(8,128)S(1)} %stack.76), channel_id=1, source_target_pairs={{0,4},{1,5},{2,6},{3,7},{4,0},{5,1},{6,2},{7,3},{8,12},{9,13},{10,... | collective-permute-start | bytes 688136 | tf_op jit(solution)/shard_map/ppermute | solution.py:308
  45.1 1.3 %collective-permute-start.24 = (f32[2,112,256]{2,1,0:T(8,128)S(1)}, f32[2,112,256]{2,1,0:T(8,128)S(1)}, u32[]{:S(2)}, u32[]{:S(2)}) collective-permute-start(f32[2,112,256]{2,1,0:T(8,128)S(1)} %stack.77), channel_id=1, source_target_pairs={{0,4},{1,5},{2,6},{3,7},{4,0},{5,1},{6,2},{7,3},{8,12},{9,13},{10,... | collective-permute-start | bytes 688136 | tf_op jit(solution)/shard_map/ppermute | solution.py:308
  46.4 3.2 %collective-permute-done.20 = f32[2,112,256]{2,1,0:T(8,128)S(1)} collective-permute-done((f32[2,112,256]{2,1,0:T(8,128)S(1)}, f32[2,112,256]{2,1,0:T(8,128)S(1)}, u32[]{:S(2)}, u32[]{:S(2)}) %collective-permute-start.20) | collective-permute-done | bytes 229408 | tf_op jit(solution)/shard_map/ppermute | solution.py:308
  49.7 1.7 %collective-permute-done.21 = f32[2,112,256]{2,1,0:T(8,128)S(1)} collective-permute-done((f32[2,112,256]{2,1,0:T(8,128)S(1)}, f32[2,112,256]{2,1,0:T(8,128)S(1)}, u32[]{:S(2)}, u32[]{:S(2)}) %collective-permute-start.21) | collective-permute-done | bytes 229408 | tf_op jit(solution)/shard_map/ppermute | solution.py:308
  51.8 1.7 %collective-permute-start.27 = (f32[112,256]{1,0:T(8,128)S(1)}, f32[112,256]{1,0:T(8,128)S(1)}, u32[]{:S(2)}, u32[]{:S(2)}) collective-permute-start(f32[112,256]{1,0:T(8,128)S(1)} %fusion.5), channel_id=1, source_target_pairs={{0,4},{1,5},{2,6},{3,7},{4,0},{5,1},{6,2},{7,3},{8,12},{9,13},{10,... | collective-permute-start | bytes 344072 | tf_op jit(solution)/shard_map/ppermute | solution.py:308
  53.5 1.1 %collective-permute-done.23 = f32[2,112,256]{2,1,0:T(8,128)S(1)} collective-permute-done((f32[2,112,256]{2,1,0:T(8,128)S(1)}, f32[2,112,256]{2,1,0:T(8,128)S(1)}, u32[]{:S(2)}, u32[]{:S(2)}) %collective-permute-start.23) | collective-permute-done | bytes 229408 | tf_op jit(solution)/shard_map/ppermute | solution.py:308
  54.6 1.6 %collective-permute-done.24 = f32[2,112,256]{2,1,0:T(8,128)S(1)} collective-permute-done((f32[2,112,256]{2,1,0:T(8,128)S(1)}, f32[2,112,256]{2,1,0:T(8,128)S(1)}, u32[]{:S(2)}, u32[]{:S(2)}) %collective-permute-start.24) | collective-permute-done | bytes 229408 | tf_op jit(solution)/shard_map/ppermute | solution.py:308
  56.7 1.7 %collective-permute-start.25 = (f32[112,256]{1,0:T(8,128)S(1)}, f32[112,256]{1,0:T(8,128)S(1)}, u32[]{:S(2)}, u32[]{:S(2)}) collective-permute-start(f32[112,256]{1,0:T(8,128)S(1)} %fusion.11), channel_id=1, source_target_pairs={{0,4},{1,5},{2,6},{3,7},{4,0},{5,1},{6,2},{7,3},{8,12},{9,13},{10,... | collective-permute-start | bytes 344072 | tf_op jit(solution)/shard_map/ppermute | solution.py:308
  58.4 1.9 %shard_map.102 = f32[450,1,256]{2,1,0:T(1,128)} custom-call(f32[240,256]{1,0:T(8,128)S(1)} %shard_map.100.refs_0_.refs_3_, bf16[1792,256]{1,0:T(8,128)(2,1)S(1)} %get-tuple-element.82.refs_1_, bf16[1792,256]{1,0:T(8,128)(2,1)S(1)} %get-tuple-element.83.refs_2_, f32[240,256]{1,0:T(8,128)S(1)} %get-tuple-element.67.refs_3_), custom_call_target="tpu_custom_call" | custom-call | flops 660602880 | bytes 2787328 | tf_op jit(solution)/shard_map/pallas_call | solution.py:26
  60.3 0.7 %maximum_bitcast_fusion.1 = f32[1,224,256]{2,1,0:T(8,128)} fusion(f32[112,256]{1,0:T(8,128)S(1)} %get-tuple-element.95, f32[112,256]{1,0:T(8,128)S(1)} %get-tuple-element.94), kind=kLoop, calls=%fused_computation.10 | loop fusion | flops 57344 | bytes 458752 | tf_op jit(solution)/shard_map/broadcast_in_dim | solution.py:370
  61.6 0.7 %maximum_bitcast_fusion = f32[1,224,256]{2,1,0:T(8,128)} fusion(f32[112,256]{1,0:T(8,128)S(1)} %get-tuple-element.97, f32[112,256]{1,0:T(8,128)S(1)} %get-tuple-element.96), kind=kLoop, calls=%fused_computation.9 | loop fusion | flops 57344 | bytes 458752 | tf_op jit(solution)/shard_map/broadcast_in_dim | solution.py:370
  (80 shorter events, 7.6 us)
Async XLA Ops:
  0.6 20.3 %copy-start.1 = (f32[1,224,256]{2,1,0:T(8,128)S(1)}, f32[1,224,256]{2,1,0:T(8,128)}, u32[]{:S(2)}) copy-start(f32[1,224,256]{2,1,0:T(8,128)} %param.13) | copy-start | bytes 688132
  0.6 20.2 %copy-start.2 = (f32[1,224,256]{2,1,0:T(8,128)S(1)}, f32[1,224,256]{2,1,0:T(8,128)}, u32[]{:S(2)}) copy-start(f32[1,224,256]{2,1,0:T(8,128)} %param.12) | copy-start | bytes 688132
  0.7 9.7 %collective-permute-start.1 = (f32[224,256]{1,0:T(8,128)}, f32[224,256]{1,0:T(8,128)S(1)}, u32[]{:S(2)}, u32[]{:S(2)}) collective-permute-start(f32[224,256]{1,0:T(8,128)} %bitcast.86), channel_id=1, source_target_pairs={{0,4},{1,5},{2,6},{3,7},{4,0},{5,1},{6,2},{7,3},{8,12},{9,13},{10,... | collective-permute-start | bytes 688136 | tf_op jit(solution)/shard_map/ppermute | solution.py:308
  3.7 8.7 %collective-permute-start = (f32[224,256]{1,0:T(8,128)}, f32[224,256]{1,0:T(8,128)S(1)}, u32[]{:S(2)}, u32[]{:S(2)}) collective-permute-start(f32[224,256]{1,0:T(8,128)} %bitcast.87), channel_id=1, source_target_pairs={{0,2},{1,3},{2,0},{3,1},{4,6},{5,7},{6,4},{7,5},{8,10},{9,11},{10,... | collective-permute-start | bytes 688136 | tf_op jit(solution)/shard_map/ppermute | solution.py:308
  5.2 9.2 %collective-permute-start.4 = (f32[224,256]{1,0:T(8,128)}, f32[224,256]{1,0:T(8,128)S(1)}, u32[]{:S(2)}, u32[]{:S(2)}) collective-permute-start(f32[224,256]{1,0:T(8,128)} %bitcast.90), channel_id=1, source_target_pairs={{0,4},{1,5},{2,6},{3,7},{4,0},{5,1},{6,2},{7,3},{8,12},{9,13},{10,... | collective-permute-start | bytes 688136 | tf_op jit(solution)/shard_map/ppermute | solution.py:308
  5.7 10.6 %collective-permute-start.2 = (f32[224,256]{1,0:T(8,128)}, f32[224,256]{1,0:T(8,128)S(1)}, u32[]{:S(2)}, u32[]{:S(2)}) collective-permute-start(f32[224,256]{1,0:T(8,128)} %bitcast.91), channel_id=1, source_target_pairs={{0,2},{1,3},{2,0},{3,1},{4,6},{5,7},{6,4},{7,5},{8,10},{9,11},{10,... | collective-permute-start | bytes 688136 | tf_op jit(solution)/shard_map/ppermute | solution.py:308
  5.8 10.6 %collective-permute-start.10 = (f32[224,256]{1,0:T(8,128)}, f32[224,256]{1,0:T(8,128)S(1)}, u32[]{:S(2)}, u32[]{:S(2)}) collective-permute-start(f32[224,256]{1,0:T(8,128)} %bitcast.88), channel_id=1, source_target_pairs={{0,1},{1,0},{2,3},{3,2},{4,5},{5,4},{6,7},{7,6},{8,9},{9,8},{10,11... | collective-permute-start | bytes 688136 | tf_op jit(solution)/shard_map/ppermute | solution.py:308
  9.0 13.3 %copy-start = (f32[1,240,256]{2,1,0:T(8,128)S(1)}, f32[1,240,256]{2,1,0:T(8,128)}, u32[]{:S(2)}) copy-start(f32[1,240,256]{2,1,0:T(8,128)} %get-tuple-element.49) | copy-start | bytes 737284
  12.4 6.9 %collective-permute-start.11 = (f32[224,256]{1,0:T(8,128)S(1)}, f32[224,256]{1,0:T(8,128)S(1)}, u32[]{:S(2)}, u32[]{:S(2)}) collective-permute-start(f32[224,256]{1,0:T(8,128)S(1)} %collective-permute-done.refs_2_), channel_id=1, source_target_pairs={{0,1},{1,0},{2,3},{3,2},{4,5},{5,4},{6,7},{7,6},{8,9},{9,8},{10,11... | collective-permute-start | bytes 688136 | tf_op jit(solution)/shard_map/ppermute | solution.py:308
  12.5 5.9 %collective-permute-start.7 = (f32[112,256]{1,0:T(8,128)S(1)}, f32[112,256]{1,0:T(8,128)S(1)}, u32[]{:S(2)}, u32[]{:S(2)}) collective-permute-start(f32[112,256]{1,0:T(8,128)S(1)} %slice.144), channel_id=1, source_target_pairs={{0,2},{1,3},{2,0},{3,1},{4,6},{5,7},{6,4},{7,5},{8,10},{9,11},{10,... | collective-permute-start | bytes 344072 | tf_op jit(solution)/shard_map/ppermute | solution.py:308
  14.4 4.9 %collective-permute-start.6 = (f32[112,256]{1,0:T(8,128)S(1)}, f32[112,256]{1,0:T(8,128)S(1)}, u32[]{:S(2)}, u32[]{:S(2)}) collective-permute-start(f32[112,256]{1,0:T(8,128)S(1)} %slice.143), channel_id=1, source_target_pairs={{0,4},{1,5},{2,6},{3,7},{4,0},{5,1},{6,2},{7,3},{8,12},{9,13},{10,... | collective-permute-start | bytes 344072 | tf_op jit(solution)/shard_map/ppermute | solution.py:308
  16.3 4.5 %collective-permute-start.12 = (f32[224,256]{1,0:T(8,128)S(1)}, f32[224,256]{1,0:T(8,128)S(1)}, u32[]{:S(2)}, u32[]{:S(2)}) collective-permute-start(f32[224,256]{1,0:T(8,128)S(1)} %collective-permute-done.1.refs_3_), channel_id=1, source_target_pairs={{0,1},{1,0},{2,3},{3,2},{4,5},{5,4},{6,7},{7,6},{8,9},{9,8},{10,11... | collective-permute-start | bytes 688136 | tf_op jit(solution)/shard_map/ppermute | solution.py:308
  16.4 7.5 %collective-permute-start.5 = (f32[112,256]{1,0:T(8,128)S(1)}, f32[112,256]{1,0:T(8,128)S(1)}, u32[]{:S(2)}, u32[]{:S(2)}) collective-permute-start(f32[112,256]{1,0:T(8,128)S(1)} %slice.179), channel_id=1, source_target_pairs={{0,2},{1,3},{2,0},{3,1},{4,6},{5,7},{6,4},{7,5},{8,10},{9,11},{10,... | collective-permute-start | bytes 344072 | tf_op jit(solution)/shard_map/ppermute | solution.py:308
  18.3 5.6 %collective-permute-start.3 = (f32[112,256]{1,0:T(8,128)S(1)}, f32[112,256]{1,0:T(8,128)S(1)}, u32[]{:S(2)}, u32[]{:S(2)}) collective-permute-start(f32[112,256]{1,0:T(8,128)S(1)} %slice.178), channel_id=1, source_target_pairs={{0,4},{1,5},{2,6},{3,7},{4,0},{5,1},{6,2},{7,3},{8,12},{9,13},{10,... | collective-permute-start | bytes 344072 | tf_op jit(solution)/shard_map/ppermute | solution.py:308
  19.3 2.4 %collective-permute-start.9 = (f32[112,256]{1,0:T(8,128)S(1)}, f32[112,256]{1,0:T(8,128)S(1)}, u32[]{:S(2)}, u32[]{:S(2)}) collective-permute-start(f32[112,256]{1,0:T(8,128)S(1)} %collective-permute-done.7.refs_4_), channel_id=1, source_target_pairs={{0,1},{1,0},{2,3},{3,2},{4,5},{5,4},{6,7},{7,6},{8,9},{9,8},{10,11... | collective-permute-start | bytes 344072 | tf_op jit(solution)/shard_map/ppermute | solution.py:308
  19.3 2.9 %collective-permute-start.8 = (f32[112,256]{1,0:T(8,128)S(1)}, f32[112,256]{1,0:T(8,128)S(1)}, u32[]{:S(2)}, u32[]{:S(2)}) collective-permute-start(f32[112,256]{1,0:T(8,128)S(1)} %collective-permute-done.6.refs_3_), channel_id=1, source_target_pairs={{0,1},{1,0},{2,3},{3,2},{4,5},{5,4},{6,7},{7,6},{8,9},{9,8},{10,11... | collective-permute-start | bytes 344072 | tf_op jit(solution)/shard_map/ppermute | solution.py:308
  20.8 3.8 %collective-permute-start.15 = (f32[224,256]{1,0:T(8,128)S(1)}, f32[224,256]{1,0:T(8,128)S(1)}, u32[]{:S(2)}, u32[]{:S(2)}) collective-permute-start(f32[224,256]{1,0:T(8,128)S(1)} %bitcast.92), channel_id=1, source_target_pairs={{0,1},{1,0},{2,3},{3,2},{4,5},{5,4},{6,7},{7,6},{8,9},{9,8},{10,11... | collective-permute-start | bytes 688136 | tf_op jit(solution)/shard_map/ppermute | solution.py:308
  21.7 2.9 %collective-permute-start.17 = (f32[224,256]{1,0:T(8,128)S(1)}, f32[224,256]{1,0:T(8,128)S(1)}, u32[]{:S(2)}, u32[]{:S(2)}) collective-permute-start(f32[224,256]{1,0:T(8,128)S(1)} %collective-permute-done.4.refs_3_), channel_id=1, source_target_pairs={{0,1},{1,0},{2,3},{3,2},{4,5},{5,4},{6,7},{7,6},{8,9},{9,8},{10,11... | collective-permute-start | bytes 688136 | tf_op jit(solution)/shard_map/ppermute | solution.py:308
  22.2 2.4 %collective-permute-start.16 = (f32[224,256]{1,0:T(8,128)S(1)}, f32[224,256]{1,0:T(8,128)S(1)}, u32[]{:S(2)}, u32[]{:S(2)}) collective-permute-start(f32[224,256]{1,0:T(8,128)S(1)} %collective-permute-done.2.refs_2_), channel_id=1, source_target_pairs={{0,1},{1,0},{2,3},{3,2},{4,5},{5,4},{6,7},{7,6},{8,9},{9,8},{10,11... | collective-permute-start | bytes 688136 | tf_op jit(solution)/shard_map/ppermute | solution.py:308
  23.9 1.5 %collective-permute-start.13 = (f32[112,256]{1,0:T(8,128)S(1)}, f32[112,256]{1,0:T(8,128)S(1)}, u32[]{:S(2)}, u32[]{:S(2)}) collective-permute-start(f32[112,256]{1,0:T(8,128)S(1)} %collective-permute-done.3.refs_2_), channel_id=1, source_target_pairs={{0,1},{1,0},{2,3},{3,2},{4,5},{5,4},{6,7},{7,6},{8,9},{9,8},{10,11... | collective-permute-start | bytes 344072 | tf_op jit(solution)/shard_map/ppermute | solution.py:308
  24.4 1.3 %collective-permute-start.14 = (f32[112,256]{1,0:T(8,128)S(1)}, f32[112,256]{1,0:T(8,128)S(1)}, u32[]{:S(2)}, u32[]{:S(2)}) collective-permute-start(f32[112,256]{1,0:T(8,128)S(1)} %collective-permute-done.5.refs_3_), channel_id=1, source_target_pairs={{0,1},{1,0},{2,3},{3,2},{4,5},{5,4},{6,7},{7,6},{8,9},{9,8},{10,11... | collective-permute-start | bytes 344072 | tf_op jit(solution)/shard_map/ppermute | solution.py:308
  27.3 9.9 %collective-permute-start.18 = (f32[240,256]{1,0:T(8,128)S(1)}, f32[240,256]{1,0:T(8,128)S(1)}, u32[]{:S(2)}, u32[]{:S(2)}) collective-permute-start(f32[240,256]{1,0:T(8,128)S(1)} %get-tuple-element.67.refs_3_), channel_id=1, source_target_pairs={{8,0},{16,8},{24,16},{9,1},{17,9},{25,17},{10,2},{18,10},{26,18},{... | collective-permute-start | bytes 737288 | tf_op jit(solution)/shard_map/ppermute | solution.py:417
  38.3 2.6 %collective-permute-start.19 = (f32[4,224,256]{2,1,0:T(8,128)S(1)}, f32[4,224,256]{2,1,0:T(8,128)S(1)}, u32[]{:S(2)}, u32[]{:S(2)}) collective-permute-start(f32[4,224,256]{2,1,0:T(8,128)S(1)} %slice_bitcast_fusion.2), channel_id=1, source_target_pairs={{0,1},{1,0},{2,3},{3,2},{4,5},{5,4},{6,7},{7,6},{8,9},{9,8},{10,11... | collective-permute-start | bytes 2752520 | tf_op jit(solution)/shard_map/ppermute | solution.py:308
  40.4 4.0 %collective-permute-start.22 = (f32[4,224,256]{2,1,0:T(8,128)S(1)}, f32[4,224,256]{2,1,0:T(8,128)S(1)}, u32[]{:S(2)}, u32[]{:S(2)}) collective-permute-start(f32[4,224,256]{2,1,0:T(8,128)S(1)} %slice_bitcast_fusion), channel_id=1, source_target_pairs={{0,1},{1,0},{2,3},{3,2},{4,5},{5,4},{6,7},{7,6},{8,9},{9,8},{10,11... | collective-permute-start | bytes 2752520 | tf_op jit(solution)/shard_map/ppermute | solution.py:308
  41.1 8.5 %collective-permute-start.20 = (f32[2,112,256]{2,1,0:T(8,128)S(1)}, f32[2,112,256]{2,1,0:T(8,128)S(1)}, u32[]{:S(2)}, u32[]{:S(2)}) collective-permute-start(f32[2,112,256]{2,1,0:T(8,128)S(1)} %pad_maximum_fusion), channel_id=1, source_target_pairs={{0,2},{1,3},{2,0},{3,1},{4,6},{5,7},{6,4},{7,5},{8,10},{9,11},{10,... | collective-permute-start | bytes 688136 | tf_op jit(solution)/shard_map/ppermute | solution.py:308
  42.8 8.5 %collective-permute-start.21 = (f32[2,112,256]{2,1,0:T(8,128)S(1)}, f32[2,112,256]{2,1,0:T(8,128)S(1)}, u32[]{:S(2)}, u32[]{:S(2)}) collective-permute-start(f32[2,112,256]{2,1,0:T(8,128)S(1)} %stack.76), channel_id=1, source_target_pairs={{0,4},{1,5},{2,6},{3,7},{4,0},{5,1},{6,2},{7,3},{8,12},{9,13},{10,... | collective-permute-start | bytes 688136 | tf_op jit(solution)/shard_map/ppermute | solution.py:308
  44.5 10.0 %collective-permute-start.23 = (f32[2,112,256]{2,1,0:T(8,128)S(1)}, f32[2,112,256]{2,1,0:T(8,128)S(1)}, u32[]{:S(2)}, u32[]{:S(2)}) collective-permute-start(f32[2,112,256]{2,1,0:T(8,128)S(1)} %pad_maximum_fusion.1), channel_id=1, source_target_pairs={{0,2},{1,3},{2,0},{3,1},{4,6},{5,7},{6,4},{7,5},{8,10},{9,11},{10,... | collective-permute-start | bytes 688136 | tf_op jit(solution)/shard_map/ppermute | solution.py:308
  45.1 11.1 %collective-permute-start.24 = (f32[2,112,256]{2,1,0:T(8,128)S(1)}, f32[2,112,256]{2,1,0:T(8,128)S(1)}, u32[]{:S(2)}, u32[]{:S(2)}) collective-permute-start(f32[2,112,256]{2,1,0:T(8,128)S(1)} %stack.77), channel_id=1, source_target_pairs={{0,4},{1,5},{2,6},{3,7},{4,0},{5,1},{6,2},{7,3},{8,12},{9,13},{10,... | collective-permute-start | bytes 688136 | tf_op jit(solution)/shard_map/ppermute | solution.py:308
  51.4 8.9 %collective-permute-start.28 = (f32[112,256]{1,0:T(8,128)S(1)}, f32[112,256]{1,0:T(8,128)S(1)}, u32[]{:S(2)}, u32[]{:S(2)}) collective-permute-start(f32[112,256]{1,0:T(8,128)S(1)} %fusion.2), channel_id=1, source_target_pairs={{0,2},{1,3},{2,0},{3,1},{4,6},{5,7},{6,4},{7,5},{8,10},{9,11},{10,... | collective-permute-start | bytes 344072 | tf_op jit(solution)/shard_map/ppermute | solution.py:308
  51.8 8.4 %collective-permute-start.27 = (f32[112,256]{1,0:T(8,128)S(1)}, f32[112,256]{1,0:T(8,128)S(1)}, u32[]{:S(2)}, u32[]{:S(2)}) collective-permute-start(f32[112,256]{1,0:T(8,128)S(1)} %fusion.5), channel_id=1, source_target_pairs={{0,4},{1,5},{2,6},{3,7},{4,0},{5,1},{6,2},{7,3},{8,12},{9,13},{10,... | collective-permute-start | bytes 344072 | tf_op jit(solution)/shard_map/ppermute | solution.py:308
  56.3 4.9 %collective-permute-start.26 = (f32[112,256]{1,0:T(8,128)S(1)}, f32[112,256]{1,0:T(8,128)S(1)}, u32[]{:S(2)}, u32[]{:S(2)}) collective-permute-start(f32[112,256]{1,0:T(8,128)S(1)} %fusion.8), channel_id=1, source_target_pairs={{0,2},{1,3},{2,0},{3,1},{4,6},{5,7},{6,4},{7,5},{8,10},{9,11},{10,... | collective-permute-start | bytes 344072 | tf_op jit(solution)/shard_map/ppermute | solution.py:308
  56.7 4.8 %collective-permute-start.25 = (f32[112,256]{1,0:T(8,128)S(1)}, f32[112,256]{1,0:T(8,128)S(1)}, u32[]{:S(2)}, u32[]{:S(2)}) collective-permute-start(f32[112,256]{1,0:T(8,128)S(1)} %fusion.11), channel_id=1, source_target_pairs={{0,4},{1,5},{2,6},{3,7},{4,0},{5,1},{6,2},{7,3},{8,12},{9,13},{10,... | collective-permute-start | bytes 344072 | tf_op jit(solution)/shard_map/ppermute | solution.py:308
  (5 other events, 24.2 us)

commit v5 on v4

--- a/solution.py
+++ b/solution.py
@@ -405,10 +405,11 @@
     sya_two, sxb_two = swap(ya_two, 1), swap(xb_two, 1)
     come = [(ya_two, 6, 0), (xb_two, 6, half), (sya_two, 7, 0), (sxb_two, 7, half)]
     pre, *second_parts = conv(incoming, mask[0], width, weights=second_parts, pieces=starts_of(me, rows, half, come))
+    ya_one, xb_one, pre = together(ya_one, xb_one, pre)
     come = [(one, 0, 0), (s_one, 1, 0), (x_one, 2, 0), (y_one, 4, 0), (sx_one, 3, 0), (sy_one, 5, 0)]
-    first_parts = placed(*starts_of(me, rows, rows, come), filter_rows)
-    ya_one, xb_one, pre = together(ya_one, xb_one, pre)
-    come = [(ya_one, 6, 0), (xb_one, 6, half), (swap(ya_one, 1), 7, 0), (swap(xb_one, 1), 7, half)]
+    come += [(ya_one, 6, 0), (xb_one, 6, half)]
+    first_parts = placed(*starts_of(me, rows, half, come), filter_rows)
+    come = [(swap(ya_one, 1), 7, 0), (swap(xb_one, 1), 7, half)]
     out, *first_parts = conv(pre, None, height, weights=first_parts, pieces=starts_of(me, rows, half, come))
     outs = [out]
     in_high, in_low, pre, _ = together(in_high, in_low, pre, out)

time: 62.4 us -> 62.4 us (level)
  no operation moved by 1% of the time
where the time goes in v5:
time: 62.4 us; the launch traced here: 62.2 us
  starting transfers between devices  23.5 us (38%)
  waiting for transfers between devices  20 us (32%)
  Pallas kernels  14.2 us (23%)
  other arithmetic  2.02 us (3%)
  local copies, waits for them, and re-layouts  1.48 us (2%)
  between operations  1.07 us (2%)
    ppermute x28, starting transfers between devices, swap(): return lax.ppermute(shard, 'dp', [(i, i ^ bit) for i in range(peers)])  22.2 us
    pallas_call x10, Pallas kernels, call(): pl.pallas_call(kernel, out_shape=out_shapes, in_specs=[SMEM] * scalars +...  14.2 us
    ppermute x28, waiting for transfers between devices, swap(): return lax.ppermute(shard, 'dp', [(i, i ^ bit) for i in range(peers)])  13.1 us
    ppermute x1, waiting for transfers between devices, local_eight(): lax.ppermute(outs[-1], 'section', [(i, i - 1) for i in range(1, sections)])  6.93 us
    broadcast_in_dim x2, other arithmetic, join(): return jnp.concatenate([a_near + a_last, b_near + b_last], axis=0)[None]  1.41 us
    ppermute x1, starting transfers between devices, local_eight(): lax.ppermute(outs[-1], 'section', [(i, i - 1) for i in range(1, sections)])  1.29 us
  transfers between devices with their start and end apart: 29, of which 13 were waited for; matrix products, arithmetic and copies ran while one was open for 4% of the time, Pallas kernels for 19%

profile of v5, /device:TPU:0, one launch (start us, length us, event | category | flops | bytes accessed | tf_op | source)
XLA Modules:
  0.0 62.2 jit_solution(268171019625260928)
XLA Ops:
  0.7 3.0 %collective-permute-start.1 = (f32[224,256]{1,0:T(8,128)}, f32[224,256]{1,0:T(8,128)S(1)}, u32[]{:S(2)}, u32[]{:S(2)}) collective-permute-start(f32[224,256]{1,0:T(8,128)} %bitcast.92), channel_id=1, source_target_pairs={{0,4},{1,5},{2,6},{3,7},{4,0},{5,1},{6,2},{7,3},{8,12},{9,13},{10,... | collective-permute-start | bytes 688136 | tf_op jit(solution)/shard_map/ppermute | solution.py:308
  3.7 1.5 %collective-permute-start = (f32[224,256]{1,0:T(8,128)}, f32[224,256]{1,0:T(8,128)S(1)}, u32[]{:S(2)}, u32[]{:S(2)}) collective-permute-start(f32[224,256]{1,0:T(8,128)} %bitcast.93), channel_id=1, source_target_pairs={{0,2},{1,3},{2,0},{3,1},{4,6},{5,7},{6,4},{7,5},{8,10},{9,11},{10,... | collective-permute-start | bytes 688136 | tf_op jit(solution)/shard_map/ppermute | solution.py:308
  5.8 3.2 %shard_map.94 = (f32[1,240,256]{2,1,0:T(8,128)}, bf16[2,240,256]{2,1,0:T(8,128)(2,1)}, f32[1,240,256]{2,1,0:T(8,128)}, bf16[2,256,240]{2,1,0:T(8,128)(2,1)}, bf1...) custom-call(f32[225,1,256]{2,1,0:T(1,128)} %bitcast.104, ...), custom_call_target="tpu_custom_call" | custom-call | bytes 3563520 | tf_op jit(solution)/shard_map/pallas_call | solution.py:26
  9.0 1.3 %collective-permute-done.1.refs_3_ = f32[224,256]{1,0:T(8,128)S(1)} collective-permute-done((f32[224,256]{1,0:T(8,128)}, f32[224,256]{1,0:T(8,128)S(1)}, u32[]{:S(2)}, u32[]{:S(2)}) %collective-permute-start.1) | collective-permute-done | bytes 229408 | tf_op jit(solution)/shard_map/ppermute | solution.py:308
  10.3 2.1 %collective-permute-done.refs_2_ = f32[224,256]{1,0:T(8,128)S(1)} collective-permute-done((f32[224,256]{1,0:T(8,128)}, f32[224,256]{1,0:T(8,128)S(1)}, u32[]{:S(2)}, u32[]{:S(2)}) %collective-permute-start) | collective-permute-done | bytes 229408 | tf_op jit(solution)/shard_map/ppermute | solution.py:308
  12.5 1.6 %collective-permute-start.7 = (f32[112,256]{1,0:T(8,128)S(1)}, f32[112,256]{1,0:T(8,128)S(1)}, u32[]{:S(2)}, u32[]{:S(2)}) collective-permute-start(f32[112,256]{1,0:T(8,128)S(1)} %slice.144), channel_id=1, source_target_pairs={{0,2},{1,3},{2,0},{3,1},{4,6},{5,7},{6,4},{7,5},{8,10},{9,11},{10,... | collective-permute-start | bytes 344072 | tf_op jit(solution)/shard_map/ppermute | solution.py:308
  14.4 1.7 %collective-permute-start.6 = (f32[112,256]{1,0:T(8,128)S(1)}, f32[112,256]{1,0:T(8,128)S(1)}, u32[]{:S(2)}, u32[]{:S(2)}) collective-permute-start(f32[112,256]{1,0:T(8,128)S(1)} %slice.143), channel_id=1, source_target_pairs={{0,4},{1,5},{2,6},{3,7},{4,0},{5,1},{6,2},{7,3},{8,12},{9,13},{10,... | collective-permute-start | bytes 344072 | tf_op jit(solution)/shard_map/ppermute | solution.py:308
  16.6 1.6 %collective-permute-start.5 = (f32[112,256]{1,0:T(8,128)S(1)}, f32[112,256]{1,0:T(8,128)S(1)}, u32[]{:S(2)}, u32[]{:S(2)}) collective-permute-start(f32[112,256]{1,0:T(8,128)S(1)} %slice.179), channel_id=1, source_target_pairs={{0,2},{1,3},{2,0},{3,1},{4,6},{5,7},{6,4},{7,5},{8,10},{9,11},{10,... | collective-permute-start | bytes 344072 | tf_op jit(solution)/shard_map/ppermute | solution.py:308
  19.8 1.0 %slice_bitcast_fusion.12 = (bf16[240,256]{1,0:T(8,128)(2,1)S(1)}, bf16[240,256]{1,0:T(8,128)(2,1)S(1)}) fusion(bf16[2,240,256]{2,1,0:T(8,128)(2,1)} %get-tuple-element.56), kind=kLoop, calls=%fused_computation.19 | loop fusion | bytes 491520 | tf_op jit(solution)/shard_map/squeeze | solution.py:428
  20.9 0.7 %shard_map.95 = (bf16[1792,256]{1,0:T(8,128)(2,1)S(1)}, bf16[1792,256]{1,0:T(8,128)(2,1)S(1)}) custom-call(s32[6]{0:T(128)S(1)} %stack.94.starts_ref, f32[224,256]{1,0:T(8,128)S(1)} %bitcast.95, f32[224,256]{1,0:T(8,128)S(1)} %collective-permute-done.10.refs_1_, f32[224,256]{1,0:T(8,128)S(1)} %collective-permute-done.refs_2_, ...), custom_call_target="tpu_custom_call" | custom-call | bytes 3211288 | tf_op jit(solution)/shard_map/pallas_call | solution.py:26
  22.3 1.6 %shard_map.96 = (f32[240,256]{1,0:T(8,128)S(1)}, bf16[1792,256]{1,0:T(8,128)(2,1)S(1)}, bf16[1792,256]{1,0:T(8,128)(2,1)S(1)}) custom-call(s32[4]{0:T(128)S(1)} %pad_add_fusion.1.refs_0_, f32[240,256]{1,0:T(8,128)S(1)} %bitcast.90, bf16[240,256]{1,0:T(8,128)(2,1)S(1)} %get-tuple-element.111.refs_2_, ...), custom_call_target="tpu_custom_call", output_to_operand_aliasing={{1}: (7, {}), {2}: (8, {})} | custom-call | flops 660602880 | bytes 4743184 | tf_op jit(solution)/shard_map/pallas_call | solution.py:26
  24.6 0.7 %shard_map.97 = (bf16[1792,256]{1,0:T(8,128)(2,1)S(1)}, bf16[1792,256]{1,0:T(8,128)(2,1)S(1)}) custom-call(s32[14]{0:T(128)S(1)} %stack.101.starts_ref, f32[224,256]{1,0:T(8,128)S(1)} %bitcast.99, f32[224,256]{1,0:T(8,128)S(1)} %collective-permute-done.15.refs_1_, f32[224,256]{1,0:T(8,128)S(1)} %collective-permute-done.2.refs_2_, ...), custom_call_target="tpu_custom_call" | custom-call | bytes 3440696 | tf_op jit(solution)/shard_map/pallas_call | solution.py:26
  25.8 1.6 %shard_map.98 = (f32[240,256]{1,0:T(8,128)S(1)}, bf16[1792,256]{1,0:T(8,128)(2,1)S(1)}, bf16[1792,256]{1,0:T(8,128)(2,1)S(1)}) custom-call(s32[2]{0:T(128)S(1)} %pad_add_fusion.refs_0_, f32[240,256]{1,0:T(8,128)S(1)} %get-tuple-element.74.refs_1_.refs_5_, ...), custom_call_target="tpu_custom_call", output_to_operand_aliasing={{1}: (4, {}), {2}: (5, {})} | custom-call | flops 660602880 | bytes 4390920 | tf_op jit(solution)/shard_map/pallas_call | solution.py:26
  27.3 1.3 %collective-permute-start.18 = (f32[240,256]{1,0:T(8,128)S(1)}, f32[240,256]{1,0:T(8,128)S(1)}, u32[]{:S(2)}, u32[]{:S(2)}) collective-permute-start(f32[240,256]{1,0:T(8,128)S(1)} %get-tuple-element.67.refs_3_), channel_id=1, source_target_pairs={{8,0},{16,8},{24,16},{9,1},{17,9},{25,17},{10,2},{18,10},{26,18},{... | collective-permute-start | bytes 737288 | tf_op jit(solution)/shard_map/ppermute | solution.py:418
  28.7 1.6 %shard_map.99 = (f32[1792,256]{1,0:T(8,128)S(1)}, f32[1792,256]{1,0:T(8,128)S(1)}) custom-call(bf16[256,240]{1,0:T(8,128)(2,1)S(1)} %get-tuple-element.112.refs_0_, bf16[256,240]{1,0:T(8,128)(2,1)S(1)} %get-tuple-element.107.refs_1_, f32[240,256]{1,0:T(8,128)S(1)} %bitcast.91, bf16[256,240]{1,0:T(8,128)(2,1)S(1)} %get-tuple-element.114.refs_3_, ...), custom_call_target="tpu_custom_call" | custom-call | flops 1321205760 | bytes 4653056 | tf_op jit(solution)/shard_map/pallas_call | solution.py:26
  30.3 6.9 %collective-permute-done.18 = f32[240,256]{1,0:T(8,128)S(1)} collective-permute-done((f32[240,256]{1,0:T(8,128)S(1)}, f32[240,256]{1,0:T(8,128)S(1)}, u32[]{:S(2)}, u32[]{:S(2)}) %collective-permute-start.18) | collective-permute-done | bytes 245792 | tf_op jit(solution)/shard_map/ppermute | solution.py:418
  37.3 0.9 %shard_map.101 = f32[2,4,224,256]{3,2,1,0:T(8,128)S(1)} custom-call(s32[1]{0:T(128)} %bitcast.31.refs_0_, bf16[256,240]{1,0:T(8,128)(2,1)S(1)} %get-tuple-element.113.refs_1_, bf16[256,240]{1,0:T(8,128)(2,1)S(1)} %get-tuple-element.106.refs_2_, f32[240,256]{1,0:T(8,128)S(1)} %bitcast_select_fusion.refs_0_.refs_3_, f32[1792,256]{1,0:T(8,128)S(1)} %get-tuple-element.80.refs_4_), custom_call_target="tpu_custom_call" | custom-call | flops 660602880 | bytes 4161540 | tf_op jit(solution)/shard_map/pallas_call | solution.py:26
  38.4 1.0 %shard_map.100.refs_0_.refs_3_ = f32[240,256]{1,0:T(8,128)S(1)} custom-call(f32[240,256]{1,0:T(8,128)S(1)} %bitcast_select_fusion.refs_0_.refs_3_, bf16[240,256]{1,0:T(8,128)(2,1)S(1)} %get-tuple-element.110.refs_1_, bf16[1792,256]{1,0:T(8,128)(2,1)S(1)} %get-tuple-element.78.refs_2_, bf16[1792,256]{1,0:T(8,128)(2,1)S(1)} %get-tuple-element.79.refs_3_), custom_call_target="tpu_custom_call" | custom-call | flops 660602880 | bytes 2449408 | tf_op jit(solution)/shard_map/pallas_call | solution.py:26
  39.4 0.9 %shard_map.103 = f32[2,4,224,256]{3,2,1,0:T(8,128)S(1)} custom-call(s32[1]{0:T(128)} %bitcast.31.refs_0_, bf16[256,240]{1,0:T(8,128)(2,1)S(1)} %get-tuple-element.115.refs_1_, bf16[256,240]{1,0:T(8,128)(2,1)S(1)} %get-tuple-element.102.refs_2_, f32[240,256]{1,0:T(8,128)S(1)} %shard_map.100.refs_0_.refs_3_, f32[1792,256]{1,0:T(8,128)S(1)} %get-tuple-element.84.refs_4_), custom_call_target="tpu_custom_call" | custom-call | flops 660602880 | bytes 4161540 | tf_op jit(solution)/shard_map/pallas_call | solution.py:26
  41.1 1.7 %collective-permute-start.20 = (f32[2,112,256]{2,1,0:T(8,128)S(1)}, f32[2,112,256]{2,1,0:T(8,128)S(1)}, u32[]{:S(2)}, u32[]{:S(2)}) collective-permute-start(f32[2,112,256]{2,1,0:T(8,128)S(1)} %pad_maximum_fusion), channel_id=1, source_target_pairs={{0,2},{1,3},{2,0},{3,1},{4,6},{5,7},{6,4},{7,5},{8,10},{9,11},{10,... | collective-permute-start | bytes 688136 | tf_op jit(solution)/shard_map/ppermute | solution.py:308
  42.8 1.5 %collective-permute-start.21 = (f32[2,112,256]{2,1,0:T(8,128)S(1)}, f32[2,112,256]{2,1,0:T(8,128)S(1)}, u32[]{:S(2)}, u32[]{:S(2)}) collective-permute-start(f32[2,112,256]{2,1,0:T(8,128)S(1)} %stack.106), channel_id=1, source_target_pairs={{0,4},{1,5},{2,6},{3,7},{4,0},{5,1},{6,2},{7,3},{8,12},{9,13},{10,... | collective-permute-start | bytes 688136 | tf_op jit(solution)/shard_map/ppermute | solution.py:308
  44.5 0.6 collective-permute-start.23
  45.1 1.3 %collective-permute-start.24 = (f32[2,112,256]{2,1,0:T(8,128)S(1)}, f32[2,112,256]{2,1,0:T(8,128)S(1)}, u32[]{:S(2)}, u32[]{:S(2)}) collective-permute-start(f32[2,112,256]{2,1,0:T(8,128)S(1)} %stack.107), channel_id=1, source_target_pairs={{0,4},{1,5},{2,6},{3,7},{4,0},{5,1},{6,2},{7,3},{8,12},{9,13},{10,... | collective-permute-start | bytes 688136 | tf_op jit(solution)/shard_map/ppermute | solution.py:308
  46.4 3.2 %collective-permute-done.20 = f32[2,112,256]{2,1,0:T(8,128)S(1)} collective-permute-done((f32[2,112,256]{2,1,0:T(8,128)S(1)}, f32[2,112,256]{2,1,0:T(8,128)S(1)}, u32[]{:S(2)}, u32[]{:S(2)}) %collective-permute-start.20) | collective-permute-done | bytes 229408 | tf_op jit(solution)/shard_map/ppermute | solution.py:308
  49.6 1.7 %collective-permute-done.21 = f32[2,112,256]{2,1,0:T(8,128)S(1)} collective-permute-done((f32[2,112,256]{2,1,0:T(8,128)S(1)}, f32[2,112,256]{2,1,0:T(8,128)S(1)}, u32[]{:S(2)}, u32[]{:S(2)}) %collective-permute-start.21) | collective-permute-done | bytes 229408 | tf_op jit(solution)/shard_map/ppermute | solution.py:308
  51.8 1.7 %collective-permute-start.27 = (f32[112,256]{1,0:T(8,128)S(1)}, f32[112,256]{1,0:T(8,128)S(1)}, u32[]{:S(2)}, u32[]{:S(2)}) collective-permute-start(f32[112,256]{1,0:T(8,128)S(1)} %fusion.5), channel_id=1, source_target_pairs={{0,4},{1,5},{2,6},{3,7},{4,0},{5,1},{6,2},{7,3},{8,12},{9,13},{10,... | collective-permute-start | bytes 344072 | tf_op jit(solution)/shard_map/ppermute | solution.py:308
  53.5 1.1 %collective-permute-done.23 = f32[2,112,256]{2,1,0:T(8,128)S(1)} collective-permute-done((f32[2,112,256]{2,1,0:T(8,128)S(1)}, f32[2,112,256]{2,1,0:T(8,128)S(1)}, u32[]{:S(2)}, u32[]{:S(2)}) %collective-permute-start.23) | collective-permute-done | bytes 229408 | tf_op jit(solution)/shard_map/ppermute | solution.py:308
  54.6 1.6 %collective-permute-done.24 = f32[2,112,256]{2,1,0:T(8,128)S(1)} collective-permute-done((f32[2,112,256]{2,1,0:T(8,128)S(1)}, f32[2,112,256]{2,1,0:T(8,128)S(1)}, u32[]{:S(2)}, u32[]{:S(2)}) %collective-permute-start.24) | collective-permute-done | bytes 229408 | tf_op jit(solution)/shard_map/ppermute | solution.py:308
  56.7 1.7 %collective-permute-start.25 = (f32[112,256]{1,0:T(8,128)S(1)}, f32[112,256]{1,0:T(8,128)S(1)}, u32[]{:S(2)}, u32[]{:S(2)}) collective-permute-start(f32[112,256]{1,0:T(8,128)S(1)} %fusion.11), channel_id=1, source_target_pairs={{0,4},{1,5},{2,6},{3,7},{4,0},{5,1},{6,2},{7,3},{8,12},{9,13},{10,... | collective-permute-start | bytes 344072 | tf_op jit(solution)/shard_map/ppermute | solution.py:308
  58.4 1.9 %shard_map.102 = f32[450,1,256]{2,1,0:T(1,128)} custom-call(f32[240,256]{1,0:T(8,128)S(1)} %shard_map.100.refs_0_.refs_3_, bf16[1792,256]{1,0:T(8,128)(2,1)S(1)} %get-tuple-element.82.refs_1_, bf16[1792,256]{1,0:T(8,128)(2,1)S(1)} %get-tuple-element.83.refs_2_, f32[240,256]{1,0:T(8,128)S(1)} %get-tuple-element.67.refs_3_), custom_call_target="tpu_custom_call" | custom-call | flops 660602880 | bytes 2787328 | tf_op jit(solution)/shard_map/pallas_call | solution.py:26
  60.3 0.7 %maximum_bitcast_fusion.1 = f32[1,224,256]{2,1,0:T(8,128)} fusion(f32[112,256]{1,0:T(8,128)S(1)} %get-tuple-element.95, f32[112,256]{1,0:T(8,128)S(1)} %get-tuple-element.94), kind=kLoop, calls=%fused_computation.10 | loop fusion | flops 57344 | bytes 458752 | tf_op jit(solution)/shard_map/broadcast_in_dim | solution.py:370
  61.5 0.7 %maximum_bitcast_fusion = f32[1,224,256]{2,1,0:T(8,128)} fusion(f32[112,256]{1,0:T(8,128)S(1)} %get-tuple-element.97, f32[112,256]{1,0:T(8,128)S(1)} %get-tuple-element.96), kind=kLoop, calls=%fused_computation.9 | loop fusion | flops 57344 | bytes 458752 | tf_op jit(solution)/shard_map/broadcast_in_dim | solution.py:370
  (82 shorter events, 7.6 us)
Async XLA Ops:
  0.6 20.3 %copy-start.1 = (f32[1,224,256]{2,1,0:T(8,128)S(1)}, f32[1,224,256]{2,1,0:T(8,128)}, u32[]{:S(2)}) copy-start(f32[1,224,256]{2,1,0:T(8,128)} %param.13) | copy-start | bytes 688132
  0.6 20.2 %copy-start.2 = (f32[1,224,256]{2,1,0:T(8,128)S(1)}, f32[1,224,256]{2,1,0:T(8,128)}, u32[]{:S(2)}) copy-start(f32[1,224,256]{2,1,0:T(8,128)} %param.12) | copy-start | bytes 688132
  0.7 9.7 %collective-permute-start.1 = (f32[224,256]{1,0:T(8,128)}, f32[224,256]{1,0:T(8,128)S(1)}, u32[]{:S(2)}, u32[]{:S(2)}) collective-permute-start(f32[224,256]{1,0:T(8,128)} %bitcast.92), channel_id=1, source_target_pairs={{0,4},{1,5},{2,6},{3,7},{4,0},{5,1},{6,2},{7,3},{8,12},{9,13},{10,... | collective-permute-start | bytes 688136 | tf_op jit(solution)/shard_map/ppermute | solution.py:308
  3.7 8.7 %collective-permute-start = (f32[224,256]{1,0:T(8,128)}, f32[224,256]{1,0:T(8,128)S(1)}, u32[]{:S(2)}, u32[]{:S(2)}) collective-permute-start(f32[224,256]{1,0:T(8,128)} %bitcast.93), channel_id=1, source_target_pairs={{0,2},{1,3},{2,0},{3,1},{4,6},{5,7},{6,4},{7,5},{8,10},{9,11},{10,... | collective-permute-start | bytes 688136 | tf_op jit(solution)/shard_map/ppermute | solution.py:308
  5.2 9.2 %collective-permute-start.4 = (f32[224,256]{1,0:T(8,128)}, f32[224,256]{1,0:T(8,128)S(1)}, u32[]{:S(2)}, u32[]{:S(2)}) collective-permute-start(f32[224,256]{1,0:T(8,128)} %bitcast.96), channel_id=1, source_target_pairs={{0,4},{1,5},{2,6},{3,7},{4,0},{5,1},{6,2},{7,3},{8,12},{9,13},{10,... | collective-permute-start | bytes 688136 | tf_op jit(solution)/shard_map/ppermute | solution.py:308
  5.7 10.8 %collective-permute-start.2 = (f32[224,256]{1,0:T(8,128)}, f32[224,256]{1,0:T(8,128)S(1)}, u32[]{:S(2)}, u32[]{:S(2)}) collective-permute-start(f32[224,256]{1,0:T(8,128)} %bitcast.97), channel_id=1, source_target_pairs={{0,2},{1,3},{2,0},{3,1},{4,6},{5,7},{6,4},{7,5},{8,10},{9,11},{10,... | collective-permute-start | bytes 688136 | tf_op jit(solution)/shard_map/ppermute | solution.py:308
  5.8 10.8 %collective-permute-start.10 = (f32[224,256]{1,0:T(8,128)}, f32[224,256]{1,0:T(8,128)S(1)}, u32[]{:S(2)}, u32[]{:S(2)}) collective-permute-start(f32[224,256]{1,0:T(8,128)} %bitcast.94), channel_id=1, source_target_pairs={{0,1},{1,0},{2,3},{3,2},{4,5},{5,4},{6,7},{7,6},{8,9},{9,8},{10,11... | collective-permute-start | bytes 688136 | tf_op jit(solution)/shard_map/ppermute | solution.py:308
  9.0 13.3 %copy-start = (f32[1,240,256]{2,1,0:T(8,128)S(1)}, f32[1,240,256]{2,1,0:T(8,128)}, u32[]{:S(2)}) copy-start(f32[1,240,256]{2,1,0:T(8,128)} %get-tuple-element.49) | copy-start | bytes 737284
  12.4 6.9 %collective-permute-start.11 = (f32[224,256]{1,0:T(8,128)S(1)}, f32[224,256]{1,0:T(8,128)S(1)}, u32[]{:S(2)}, u32[]{:S(2)}) collective-permute-start(f32[224,256]{1,0:T(8,128)S(1)} %collective-permute-done.refs_2_), channel_id=1, source_target_pairs={{0,1},{1,0},{2,3},{3,2},{4,5},{5,4},{6,7},{7,6},{8,9},{9,8},{10,11... | collective-permute-start | bytes 688136 | tf_op jit(solution)/shard_map/ppermute | solution.py:308
  12.5 5.9 %collective-permute-start.7 = (f32[112,256]{1,0:T(8,128)S(1)}, f32[112,256]{1,0:T(8,128)S(1)}, u32[]{:S(2)}, u32[]{:S(2)}) collective-permute-start(f32[112,256]{1,0:T(8,128)S(1)} %slice.144), channel_id=1, source_target_pairs={{0,2},{1,3},{2,0},{3,1},{4,6},{5,7},{6,4},{7,5},{8,10},{9,11},{10,... | collective-permute-start | bytes 344072 | tf_op jit(solution)/shard_map/ppermute | solution.py:308
  14.4 4.9 %collective-permute-start.6 = (f32[112,256]{1,0:T(8,128)S(1)}, f32[112,256]{1,0:T(8,128)S(1)}, u32[]{:S(2)}, u32[]{:S(2)}) collective-permute-start(f32[112,256]{1,0:T(8,128)S(1)} %slice.143), channel_id=1, source_target_pairs={{0,4},{1,5},{2,6},{3,7},{4,0},{5,1},{6,2},{7,3},{8,12},{9,13},{10,... | collective-permute-start | bytes 344072 | tf_op jit(solution)/shard_map/ppermute | solution.py:308
  16.5 4.3 %collective-permute-start.12 = (f32[224,256]{1,0:T(8,128)S(1)}, f32[224,256]{1,0:T(8,128)S(1)}, u32[]{:S(2)}, u32[]{:S(2)}) collective-permute-start(f32[224,256]{1,0:T(8,128)S(1)} %collective-permute-done.1.refs_3_), channel_id=1, source_target_pairs={{0,1},{1,0},{2,3},{3,2},{4,5},{5,4},{6,7},{7,6},{8,9},{9,8},{10,11... | collective-permute-start | bytes 688136 | tf_op jit(solution)/shard_map/ppermute | solution.py:308
  16.6 7.3 %collective-permute-start.5 = (f32[112,256]{1,0:T(8,128)S(1)}, f32[112,256]{1,0:T(8,128)S(1)}, u32[]{:S(2)}, u32[]{:S(2)}) collective-permute-start(f32[112,256]{1,0:T(8,128)S(1)} %slice.179), channel_id=1, source_target_pairs={{0,2},{1,3},{2,0},{3,1},{4,6},{5,7},{6,4},{7,5},{8,10},{9,11},{10,... | collective-permute-start | bytes 344072 | tf_op jit(solution)/shard_map/ppermute | solution.py:308
  18.3 5.6 %collective-permute-start.3 = (f32[112,256]{1,0:T(8,128)S(1)}, f32[112,256]{1,0:T(8,128)S(1)}, u32[]{:S(2)}, u32[]{:S(2)}) collective-permute-start(f32[112,256]{1,0:T(8,128)S(1)} %slice.178), channel_id=1, source_target_pairs={{0,4},{1,5},{2,6},{3,7},{4,0},{5,1},{6,2},{7,3},{8,12},{9,13},{10,... | collective-permute-start | bytes 344072 | tf_op jit(solution)/shard_map/ppermute | solution.py:308
  19.3 2.4 %collective-permute-start.9 = (f32[112,256]{1,0:T(8,128)S(1)}, f32[112,256]{1,0:T(8,128)S(1)}, u32[]{:S(2)}, u32[]{:S(2)}) collective-permute-start(f32[112,256]{1,0:T(8,128)S(1)} %collective-permute-done.7.refs_4_), channel_id=1, source_target_pairs={{0,1},{1,0},{2,3},{3,2},{4,5},{5,4},{6,7},{7,6},{8,9},{9,8},{10,11... | collective-permute-start | bytes 344072 | tf_op jit(solution)/shard_map/ppermute | solution.py:308
  19.3 2.9 %collective-permute-start.8 = (f32[112,256]{1,0:T(8,128)S(1)}, f32[112,256]{1,0:T(8,128)S(1)}, u32[]{:S(2)}, u32[]{:S(2)}) collective-permute-start(f32[112,256]{1,0:T(8,128)S(1)} %collective-permute-done.6.refs_3_), channel_id=1, source_target_pairs={{0,1},{1,0},{2,3},{3,2},{4,5},{5,4},{6,7},{7,6},{8,9},{9,8},{10,11... | collective-permute-start | bytes 344072 | tf_op jit(solution)/shard_map/ppermute | solution.py:308
  20.8 3.8 %collective-permute-start.15 = (f32[224,256]{1,0:T(8,128)S(1)}, f32[224,256]{1,0:T(8,128)S(1)}, u32[]{:S(2)}, u32[]{:S(2)}) collective-permute-start(f32[224,256]{1,0:T(8,128)S(1)} %bitcast.98), channel_id=1, source_target_pairs={{0,1},{1,0},{2,3},{3,2},{4,5},{5,4},{6,7},{7,6},{8,9},{9,8},{10,11... | collective-permute-start | bytes 688136 | tf_op jit(solution)/shard_map/ppermute | solution.py:308
  21.7 2.9 %collective-permute-start.17 = (f32[224,256]{1,0:T(8,128)S(1)}, f32[224,256]{1,0:T(8,128)S(1)}, u32[]{:S(2)}, u32[]{:S(2)}) collective-permute-start(f32[224,256]{1,0:T(8,128)S(1)} %collective-permute-done.4.refs_3_), channel_id=1, source_target_pairs={{0,1},{1,0},{2,3},{3,2},{4,5},{5,4},{6,7},{7,6},{8,9},{9,8},{10,11... | collective-permute-start | bytes 688136 | tf_op jit(solution)/shard_map/ppermute | solution.py:308
  22.2 2.4 %collective-permute-start.16 = (f32[224,256]{1,0:T(8,128)S(1)}, f32[224,256]{1,0:T(8,128)S(1)}, u32[]{:S(2)}, u32[]{:S(2)}) collective-permute-start(f32[224,256]{1,0:T(8,128)S(1)} %collective-permute-done.2.refs_2_), channel_id=1, source_target_pairs={{0,1},{1,0},{2,3},{3,2},{4,5},{5,4},{6,7},{7,6},{8,9},{9,8},{10,11... | collective-permute-start | bytes 688136 | tf_op jit(solution)/shard_map/ppermute | solution.py:308
  23.9 1.5 %collective-permute-start.13 = (f32[112,256]{1,0:T(8,128)S(1)}, f32[112,256]{1,0:T(8,128)S(1)}, u32[]{:S(2)}, u32[]{:S(2)}) collective-permute-start(f32[112,256]{1,0:T(8,128)S(1)} %collective-permute-done.3.refs_6_), channel_id=1, source_target_pairs={{0,1},{1,0},{2,3},{3,2},{4,5},{5,4},{6,7},{7,6},{8,9},{9,8},{10,11... | collective-permute-start | bytes 344072 | tf_op jit(solution)/shard_map/ppermute | solution.py:308
  24.4 1.3 %collective-permute-start.14 = (f32[112,256]{1,0:T(8,128)S(1)}, f32[112,256]{1,0:T(8,128)S(1)}, u32[]{:S(2)}, u32[]{:S(2)}) collective-permute-start(f32[112,256]{1,0:T(8,128)S(1)} %collective-permute-done.5.refs_7_), channel_id=1, source_target_pairs={{0,1},{1,0},{2,3},{3,2},{4,5},{5,4},{6,7},{7,6},{8,9},{9,8},{10,11... | collective-permute-start | bytes 344072 | tf_op jit(solution)/shard_map/ppermute | solution.py:308
  27.3 9.9 %collective-permute-start.18 = (f32[240,256]{1,0:T(8,128)S(1)}, f32[240,256]{1,0:T(8,128)S(1)}, u32[]{:S(2)}, u32[]{:S(2)}) collective-permute-start(f32[240,256]{1,0:T(8,128)S(1)} %get-tuple-element.67.refs_3_), channel_id=1, source_target_pairs={{8,0},{16,8},{24,16},{9,1},{17,9},{25,17},{10,2},{18,10},{26,18},{... | collective-permute-start | bytes 737288 | tf_op jit(solution)/shard_map/ppermute | solution.py:418
  38.3 2.6 %collective-permute-start.19 = (f32[4,224,256]{2,1,0:T(8,128)S(1)}, f32[4,224,256]{2,1,0:T(8,128)S(1)}, u32[]{:S(2)}, u32[]{:S(2)}) collective-permute-start(f32[4,224,256]{2,1,0:T(8,128)S(1)} %slice_bitcast_fusion.2), channel_id=1, source_target_pairs={{0,1},{1,0},{2,3},{3,2},{4,5},{5,4},{6,7},{7,6},{8,9},{9,8},{10,11... | collective-permute-start | bytes 2752520 | tf_op jit(solution)/shard_map/ppermute | solution.py:308
  40.4 4.0 %collective-permute-start.22 = (f32[4,224,256]{2,1,0:T(8,128)S(1)}, f32[4,224,256]{2,1,0:T(8,128)S(1)}, u32[]{:S(2)}, u32[]{:S(2)}) collective-permute-start(f32[4,224,256]{2,1,0:T(8,128)S(1)} %slice_bitcast_fusion), channel_id=1, source_target_pairs={{0,1},{1,0},{2,3},{3,2},{4,5},{5,4},{6,7},{7,6},{8,9},{9,8},{10,11... | collective-permute-start | bytes 2752520 | tf_op jit(solution)/shard_map/ppermute | solution.py:308
  41.1 8.5 %collective-permute-start.20 = (f32[2,112,256]{2,1,0:T(8,128)S(1)}, f32[2,112,256]{2,1,0:T(8,128)S(1)}, u32[]{:S(2)}, u32[]{:S(2)}) collective-permute-start(f32[2,112,256]{2,1,0:T(8,128)S(1)} %pad_maximum_fusion), channel_id=1, source_target_pairs={{0,2},{1,3},{2,0},{3,1},{4,6},{5,7},{6,4},{7,5},{8,10},{9,11},{10,... | collective-permute-start | bytes 688136 | tf_op jit(solution)/shard_map/ppermute | solution.py:308
  42.8 8.5 %collective-permute-start.21 = (f32[2,112,256]{2,1,0:T(8,128)S(1)}, f32[2,112,256]{2,1,0:T(8,128)S(1)}, u32[]{:S(2)}, u32[]{:S(2)}) collective-permute-start(f32[2,112,256]{2,1,0:T(8,128)S(1)} %stack.106), channel_id=1, source_target_pairs={{0,4},{1,5},{2,6},{3,7},{4,0},{5,1},{6,2},{7,3},{8,12},{9,13},{10,... | collective-permute-start | bytes 688136 | tf_op jit(solution)/shard_map/ppermute | solution.py:308
  44.5 10.0 %collective-permute-start.23 = (f32[2,112,256]{2,1,0:T(8,128)S(1)}, f32[2,112,256]{2,1,0:T(8,128)S(1)}, u32[]{:S(2)}, u32[]{:S(2)}) collective-permute-start(f32[2,112,256]{2,1,0:T(8,128)S(1)} %pad_maximum_fusion.1), channel_id=1, source_target_pairs={{0,2},{1,3},{2,0},{3,1},{4,6},{5,7},{6,4},{7,5},{8,10},{9,11},{10,... | collective-permute-start | bytes 688136 | tf_op jit(solution)/shard_map/ppermute | solution.py:308
  45.1 11.1 %collective-permute-start.24 = (f32[2,112,256]{2,1,0:T(8,128)S(1)}, f32[2,112,256]{2,1,0:T(8,128)S(1)}, u32[]{:S(2)}, u32[]{:S(2)}) collective-permute-start(f32[2,112,256]{2,1,0:T(8,128)S(1)} %stack.107), channel_id=1, source_target_pairs={{0,4},{1,5},{2,6},{3,7},{4,0},{5,1},{6,2},{7,3},{8,12},{9,13},{10,... | collective-permute-start | bytes 688136 | tf_op jit(solution)/shard_map/ppermute | solution.py:308
  51.4 8.9 %collective-permute-start.28 = (f32[112,256]{1,0:T(8,128)S(1)}, f32[112,256]{1,0:T(8,128)S(1)}, u32[]{:S(2)}, u32[]{:S(2)}) collective-permute-start(f32[112,256]{1,0:T(8,128)S(1)} %fusion.2), channel_id=1, source_target_pairs={{0,2},{1,3},{2,0},{3,1},{4,6},{5,7},{6,4},{7,5},{8,10},{9,11},{10,... | collective-permute-start | bytes 344072 | tf_op jit(solution)/shard_map/ppermute | solution.py:308
  51.8 8.4 %collective-permute-start.27 = (f32[112,256]{1,0:T(8,128)S(1)}, f32[112,256]{1,0:T(8,128)S(1)}, u32[]{:S(2)}, u32[]{:S(2)}) collective-permute-start(f32[112,256]{1,0:T(8,128)S(1)} %fusion.5), channel_id=1, source_target_pairs={{0,4},{1,5},{2,6},{3,7},{4,0},{5,1},{6,2},{7,3},{8,12},{9,13},{10,... | collective-permute-start | bytes 344072 | tf_op jit(solution)/shard_map/ppermute | solution.py:308
  56.2 4.9 %collective-permute-start.26 = (f32[112,256]{1,0:T(8,128)S(1)}, f32[112,256]{1,0:T(8,128)S(1)}, u32[]{:S(2)}, u32[]{:S(2)}) collective-permute-start(f32[112,256]{1,0:T(8,128)S(1)} %fusion.8), channel_id=1, source_target_pairs={{0,2},{1,3},{2,0},{3,1},{4,6},{5,7},{6,4},{7,5},{8,10},{9,11},{10,... | collective-permute-start | bytes 344072 | tf_op jit(solution)/shard_map/ppermute | solution.py:308
  56.7 4.8 %collective-permute-start.25 = (f32[112,256]{1,0:T(8,128)S(1)}, f32[112,256]{1,0:T(8,128)S(1)}, u32[]{:S(2)}, u32[]{:S(2)}) collective-permute-start(f32[112,256]{1,0:T(8,128)S(1)} %fusion.11), channel_id=1, source_target_pairs={{0,4},{1,5},{2,6},{3,7},{4,0},{5,1},{6,2},{7,3},{8,12},{9,13},{10,... | collective-permute-start | bytes 344072 | tf_op jit(solution)/shard_map/ppermute | solution.py:308
  (5 other events, 24.1 us)

commit v6 on v4

--- a/solution.py
+++ b/solution.py
@@ -359,9 +359,10 @@
     return a, b, swap(jnp.stack([a[1], a[3]]), 2), swap(jnp.stack([b[2], b[3]]), 4)
 
 
-def far_phase(a, b, a_there, b_there):
+def far_phase(a, b, a_there, b_there, tied):
     a_near, a_far = a[0] + a_there[0], a[2] + a_there[1]
-    a_far, b_there = together(a_far, b_there)
+    if tied:
+        a_far, b_there = together(a_far, b_there)
     b_near, b_far = b[0] + b_there[0], b[1] + b_there[1]
     return a_near, b_near, swap(a_far, 4), swap(b_far, 2)
 
@@ -430,9 +431,9 @@
     a, b, a_there, b_there = near_phase(kept + other)
     first_a, first_b, first_a_there, first_b_there = near_phase(first_kept + first_other)
     pre, a_there, b_there = together(pre, a_there, b_there)
-    last = far_phase(a, b, a_there, b_there)
+    last = far_phase(a, b, a_there, b_there, False)
     data_grad = last_conv(pre, first_parts, outs, height, width)
-    first_last = far_phase(first_a, first_b, first_a_there, first_b_there)
+    first_last = far_phase(first_a, first_b, first_a_there, first_b_there, True)
     return data_grad.reshape((1, ticks, images, height, width, channels)), join(*first_last), join(*last)
 
 

time: 62.4 us -> 62.4 us (level)
  no operation moved by 1% of the time
where the time goes in v6:
time: 62.4 us; the launch traced here: 62.3 us
  starting transfers between devices  23.5 us (38%)
  waiting for transfers between devices  20.2 us (32%)
  Pallas kernels  14.2 us (23%)
  other arithmetic  1.93 us (3%)
  local copies, waits for them, and re-layouts  1.42 us (2%)
  between operations  1.05 us (2%)
    ppermute x28, starting transfers between devices, swap(): return lax.ppermute(shard, 'dp', [(i, i ^ bit) for i in range(peers)])  22.2 us
    pallas_call x10, Pallas kernels, call(): pl.pallas_call(kernel, out_shape=out_shapes, in_specs=[SMEM] * scalars +...  14.2 us
    ppermute x28, waiting for transfers between devices, swap(): return lax.ppermute(shard, 'dp', [(i, i ^ bit) for i in range(peers)])  13.2 us
    ppermute x1, waiting for transfers between devices, local_eight(): lax.ppermute(outs[-1], 'section', [(i, i - 1) for i in range(1, sections)])  6.94 us
    broadcast_in_dim x2, other arithmetic, join(): return jnp.concatenate([a_near + a_last, b_near + b_last], axis=0)[None]  1.41 us
    ppermute x1, starting transfers between devices, local_eight(): lax.ppermute(outs[-1], 'section', [(i, i - 1) for i in range(1, sections)])  1.29 us
  transfers between devices with their start and end apart: 29, of which 13 were waited for; matrix products, arithmetic and copies ran while one was open for 4% of the time, Pallas kernels for 19%

profile of v6, /device:TPU:0, one launch (start us, length us, event | category | flops | bytes accessed | tf_op | source)
XLA Modules:
  0.0 62.3 jit_solution(8317162088003365594)
XLA Ops:
  0.7 3.0 %collective-permute-start.1 = (f32[224,256]{1,0:T(8,128)}, f32[224,256]{1,0:T(8,128)S(1)}, u32[]{:S(2)}, u32[]{:S(2)}) collective-permute-start(f32[224,256]{1,0:T(8,128)} %bitcast.86), channel_id=1, source_target_pairs={{0,4},{1,5},{2,6},{3,7},{4,0},{5,1},{6,2},{7,3},{8,12},{9,13},{10,... | collective-permute-start | bytes 688136 | tf_op jit(solution)/shard_map/ppermute | solution.py:308
  3.7 1.5 %collective-permute-start = (f32[224,256]{1,0:T(8,128)}, f32[224,256]{1,0:T(8,128)S(1)}, u32[]{:S(2)}, u32[]{:S(2)}) collective-permute-start(f32[224,256]{1,0:T(8,128)} %bitcast.87), channel_id=1, source_target_pairs={{0,2},{1,3},{2,0},{3,1},{4,6},{5,7},{6,4},{7,5},{8,10},{9,11},{10,... | collective-permute-start | bytes 688136 | tf_op jit(solution)/shard_map/ppermute | solution.py:308
  5.8 3.2 %shard_map.94 = (f32[1,240,256]{2,1,0:T(8,128)}, bf16[2,240,256]{2,1,0:T(8,128)(2,1)}, f32[1,240,256]{2,1,0:T(8,128)}, bf16[2,256,240]{2,1,0:T(8,128)(2,1)}, bf1...) custom-call(f32[225,1,256]{2,1,0:T(1,128)} %bitcast.98, ...), custom_call_target="tpu_custom_call" | custom-call | bytes 3563520 | tf_op jit(solution)/shard_map/pallas_call | solution.py:26
  9.0 1.3 %collective-permute-done.1.refs_3_ = f32[224,256]{1,0:T(8,128)S(1)} collective-permute-done((f32[224,256]{1,0:T(8,128)}, f32[224,256]{1,0:T(8,128)S(1)}, u32[]{:S(2)}, u32[]{:S(2)}) %collective-permute-start.1) | collective-permute-done | bytes 229408 | tf_op jit(solution)/shard_map/ppermute | solution.py:308
  10.3 2.1 %collective-permute-done.refs_2_ = f32[224,256]{1,0:T(8,128)S(1)} collective-permute-done((f32[224,256]{1,0:T(8,128)}, f32[224,256]{1,0:T(8,128)S(1)}, u32[]{:S(2)}, u32[]{:S(2)}) %collective-permute-start) | collective-permute-done | bytes 229408 | tf_op jit(solution)/shard_map/ppermute | solution.py:308
  12.5 1.6 %collective-permute-start.7 = (f32[112,256]{1,0:T(8,128)S(1)}, f32[112,256]{1,0:T(8,128)S(1)}, u32[]{:S(2)}, u32[]{:S(2)}) collective-permute-start(f32[112,256]{1,0:T(8,128)S(1)} %slice.144), channel_id=1, source_target_pairs={{0,2},{1,3},{2,0},{3,1},{4,6},{5,7},{6,4},{7,5},{8,10},{9,11},{10,... | collective-permute-start | bytes 344072 | tf_op jit(solution)/shard_map/ppermute | solution.py:308
  14.4 1.7 %collective-permute-start.6 = (f32[112,256]{1,0:T(8,128)S(1)}, f32[112,256]{1,0:T(8,128)S(1)}, u32[]{:S(2)}, u32[]{:S(2)}) collective-permute-start(f32[112,256]{1,0:T(8,128)S(1)} %slice.143), channel_id=1, source_target_pairs={{0,4},{1,5},{2,6},{3,7},{4,0},{5,1},{6,2},{7,3},{8,12},{9,13},{10,... | collective-permute-start | bytes 344072 | tf_op jit(solution)/shard_map/ppermute | solution.py:308
  16.4 1.6 %collective-permute-start.5 = (f32[112,256]{1,0:T(8,128)S(1)}, f32[112,256]{1,0:T(8,128)S(1)}, u32[]{:S(2)}, u32[]{:S(2)}) collective-permute-start(f32[112,256]{1,0:T(8,128)S(1)} %slice.179), channel_id=1, source_target_pairs={{0,2},{1,3},{2,0},{3,1},{4,6},{5,7},{6,4},{7,5},{8,10},{9,11},{10,... | collective-permute-start | bytes 344072 | tf_op jit(solution)/shard_map/ppermute | solution.py:308
  18.7 0.6 collective-permute-done.6.refs_3_
  19.8 1.0 %slice_bitcast_fusion.12 = (bf16[240,256]{1,0:T(8,128)(2,1)S(1)}, bf16[240,256]{1,0:T(8,128)(2,1)S(1)}) fusion(bf16[2,240,256]{2,1,0:T(8,128)(2,1)} %get-tuple-element.54), kind=kLoop, calls=%fused_computation.19 | loop fusion | bytes 491520 | tf_op jit(solution)/shard_map/squeeze | solution.py:428
  20.9 0.7 %shard_map.95 = (bf16[1792,256]{1,0:T(8,128)(2,1)S(1)}, bf16[1792,256]{1,0:T(8,128)(2,1)S(1)}) custom-call(s32[6]{0:T(128)S(1)} %stack.71.starts_ref, f32[224,256]{1,0:T(8,128)S(1)} %bitcast.89, f32[224,256]{1,0:T(8,128)S(1)} %collective-permute-done.10.refs_1_, f32[224,256]{1,0:T(8,128)S(1)} %collective-permute-done.refs_2_, ...), custom_call_target="tpu_custom_call" | custom-call | bytes 3211288 | tf_op jit(solution)/shard_map/pallas_call | solution.py:26
  22.3 1.6 %shard_map.96 = (f32[240,256]{1,0:T(8,128)S(1)}, bf16[1792,256]{1,0:T(8,128)(2,1)S(1)}, bf16[1792,256]{1,0:T(8,128)(2,1)S(1)}) custom-call(s32[4]{0:T(128)S(1)} %pad_add_fusion.refs_0_, f32[240,256]{1,0:T(8,128)S(1)} %bitcast.84, bf16[240,256]{1,0:T(8,128)(2,1)S(1)} %get-tuple-element.109.refs_2_, ...), custom_call_target="tpu_custom_call", output_to_operand_aliasing={{1}: (7, {}), {2}: (8, {})} | custom-call | flops 660602880 | bytes 4743184 | tf_op jit(solution)/shard_map/pallas_call | solution.py:26
  24.6 0.8 %shard_map.97 = (bf16[1792,256]{1,0:T(8,128)(2,1)S(1)}, bf16[1792,256]{1,0:T(8,128)(2,1)S(1)}) custom-call(s32[6]{0:T(128)S(1)} %stack.71.starts_ref, f32[224,256]{1,0:T(8,128)S(1)} %bitcast.93, f32[224,256]{1,0:T(8,128)S(1)} %collective-permute-done.15.refs_1_, f32[224,256]{1,0:T(8,128)S(1)} %collective-permute-done.2.refs_2_, ...), custom_call_target="tpu_custom_call" | custom-call | bytes 3211288 | tf_op jit(solution)/shard_map/pallas_call | solution.py:26
  25.8 1.6 %shard_map.98 = (f32[240,256]{1,0:T(8,128)S(1)}, bf16[1792,256]{1,0:T(8,128)(2,1)S(1)}, bf16[1792,256]{1,0:T(8,128)(2,1)S(1)}) custom-call(s32[4]{0:T(128)S(1)} %pad_add_fusion.refs_0_, f32[240,256]{1,0:T(8,128)S(1)} %get-tuple-element.72.refs_1_.refs_5_, ...), custom_call_target="tpu_custom_call", output_to_operand_aliasing={{1}: (6, {}), {2}: (7, {})} | custom-call | flops 660602880 | bytes 4620304 | tf_op jit(solution)/shard_map/pallas_call | solution.py:26
  27.3 1.3 %collective-permute-start.18 = (f32[240,256]{1,0:T(8,128)S(1)}, f32[240,256]{1,0:T(8,128)S(1)}, u32[]{:S(2)}, u32[]{:S(2)}) collective-permute-start(f32[240,256]{1,0:T(8,128)S(1)} %get-tuple-element.65.refs_3_), channel_id=1, source_target_pairs={{8,0},{16,8},{24,16},{9,1},{17,9},{25,17},{10,2},{18,10},{26,18},{... | collective-permute-start | bytes 737288 | tf_op jit(solution)/shard_map/ppermute | solution.py:418
  28.7 1.6 %shard_map.99 = (f32[1792,256]{1,0:T(8,128)S(1)}, f32[1792,256]{1,0:T(8,128)S(1)}) custom-call(bf16[256,240]{1,0:T(8,128)(2,1)S(1)} %get-tuple-element.110.refs_0_, bf16[256,240]{1,0:T(8,128)(2,1)S(1)} %get-tuple-element.105.refs_1_, f32[240,256]{1,0:T(8,128)S(1)} %bitcast.85, bf16[256,240]{1,0:T(8,128)(2,1)S(1)} %get-tuple-element.112.refs_3_, ...), custom_call_target="tpu_custom_call" | custom-call | flops 1321205760 | bytes 4653056 | tf_op jit(solution)/shard_map/pallas_call | solution.py:26
  30.3 6.9 %collective-permute-done.18 = f32[240,256]{1,0:T(8,128)S(1)} collective-permute-done((f32[240,256]{1,0:T(8,128)S(1)}, f32[240,256]{1,0:T(8,128)S(1)}, u32[]{:S(2)}, u32[]{:S(2)}) %collective-permute-start.18) | collective-permute-done | bytes 245792 | tf_op jit(solution)/shard_map/ppermute | solution.py:418
  37.3 0.9 %shard_map.101 = f32[2,4,224,256]{3,2,1,0:T(8,128)S(1)} custom-call(s32[1]{0:T(128)} %bitcast.25.refs_0_, bf16[256,240]{1,0:T(8,128)(2,1)S(1)} %get-tuple-element.111.refs_1_, bf16[256,240]{1,0:T(8,128)(2,1)S(1)} %get-tuple-element.104.refs_2_, f32[240,256]{1,0:T(8,128)S(1)} %bitcast_select_fusion.refs_0_.refs_3_, f32[1792,256]{1,0:T(8,128)S(1)} %get-tuple-element.78.refs_4_), custom_call_target="tpu_custom_call" | custom-call | flops 660602880 | bytes 4161540 | tf_op jit(solution)/shard_map/pallas_call | solution.py:26
  38.4 1.0 %shard_map.100.refs_0_.refs_3_ = f32[240,256]{1,0:T(8,128)S(1)} custom-call(f32[240,256]{1,0:T(8,128)S(1)} %bitcast_select_fusion.refs_0_.refs_3_, bf16[240,256]{1,0:T(8,128)(2,1)S(1)} %get-tuple-element.108.refs_1_, bf16[1792,256]{1,0:T(8,128)(2,1)S(1)} %get-tuple-element.76.refs_2_, bf16[1792,256]{1,0:T(8,128)(2,1)S(1)} %get-tuple-element.77.refs_3_), custom_call_target="tpu_custom_call" | custom-call | flops 660602880 | bytes 2449408 | tf_op jit(solution)/shard_map/pallas_call | solution.py:26
  39.4 0.9 %shard_map.103 = f32[2,4,224,256]{3,2,1,0:T(8,128)S(1)} custom-call(s32[1]{0:T(128)} %bitcast.25.refs_0_, bf16[256,240]{1,0:T(8,128)(2,1)S(1)} %get-tuple-element.113.refs_1_, bf16[256,240]{1,0:T(8,128)(2,1)S(1)} %get-tuple-element.100.refs_2_, f32[240,256]{1,0:T(8,128)S(1)} %shard_map.100.refs_0_.refs_3_, f32[1792,256]{1,0:T(8,128)S(1)} %get-tuple-element.82.refs_4_), custom_call_target="tpu_custom_call" | custom-call | flops 660602880 | bytes 4161540 | tf_op jit(solution)/shard_map/pallas_call | solution.py:26
  41.1 1.7 %collective-permute-start.20 = (f32[2,112,256]{2,1,0:T(8,128)S(1)}, f32[2,112,256]{2,1,0:T(8,128)S(1)}, u32[]{:S(2)}, u32[]{:S(2)}) collective-permute-start(f32[2,112,256]{2,1,0:T(8,128)S(1)} %pad_maximum_fusion), channel_id=1, source_target_pairs={{0,2},{1,3},{2,0},{3,1},{4,6},{5,7},{6,4},{7,5},{8,10},{9,11},{10,... | collective-permute-start | bytes 688136 | tf_op jit(solution)/shard_map/ppermute | solution.py:308
  42.8 1.5 %collective-permute-start.21 = (f32[2,112,256]{2,1,0:T(8,128)S(1)}, f32[2,112,256]{2,1,0:T(8,128)S(1)}, u32[]{:S(2)}, u32[]{:S(2)}) collective-permute-start(f32[2,112,256]{2,1,0:T(8,128)S(1)} %stack.76), channel_id=1, source_target_pairs={{0,4},{1,5},{2,6},{3,7},{4,0},{5,1},{6,2},{7,3},{8,12},{9,13},{10,... | collective-permute-start | bytes 688136 | tf_op jit(solution)/shard_map/ppermute | solution.py:308
  45.1 1.3 %collective-permute-start.24 = (f32[2,112,256]{2,1,0:T(8,128)S(1)}, f32[2,112,256]{2,1,0:T(8,128)S(1)}, u32[]{:S(2)}, u32[]{:S(2)}) collective-permute-start(f32[2,112,256]{2,1,0:T(8,128)S(1)} %stack.77), channel_id=1, source_target_pairs={{0,4},{1,5},{2,6},{3,7},{4,0},{5,1},{6,2},{7,3},{8,12},{9,13},{10,... | collective-permute-start | bytes 688136 | tf_op jit(solution)/shard_map/ppermute | solution.py:308
  46.4 3.2 %collective-permute-done.20 = f32[2,112,256]{2,1,0:T(8,128)S(1)} collective-permute-done((f32[2,112,256]{2,1,0:T(8,128)S(1)}, f32[2,112,256]{2,1,0:T(8,128)S(1)}, u32[]{:S(2)}, u32[]{:S(2)}) %collective-permute-start.20) | collective-permute-done | bytes 229408 | tf_op jit(solution)/shard_map/ppermute | solution.py:308
  49.7 1.7 %collective-permute-done.21 = f32[2,112,256]{2,1,0:T(8,128)S(1)} collective-permute-done((f32[2,112,256]{2,1,0:T(8,128)S(1)}, f32[2,112,256]{2,1,0:T(8,128)S(1)}, u32[]{:S(2)}, u32[]{:S(2)}) %collective-permute-start.21) | collective-permute-done | bytes 229408 | tf_op jit(solution)/shard_map/ppermute | solution.py:308
  51.4 1.6 %collective-permute-start.27 = (f32[112,256]{1,0:T(8,128)S(1)}, f32[112,256]{1,0:T(8,128)S(1)}, u32[]{:S(2)}, u32[]{:S(2)}) collective-permute-start(f32[112,256]{1,0:T(8,128)S(1)} %get-tuple-element.92), channel_id=1, source_target_pairs={{0,4},{1,5},{2,6},{3,7},{4,0},{5,1},{6,2},{7,3},{8,12},{9,13},{10,... | collective-permute-start | bytes 344072 | tf_op jit(solution)/shard_map/ppermute | solution.py:308
  53.5 0.9 %collective-permute-done.23 = f32[2,112,256]{2,1,0:T(8,128)S(1)} collective-permute-done((f32[2,112,256]{2,1,0:T(8,128)S(1)}, f32[2,112,256]{2,1,0:T(8,128)S(1)}, u32[]{:S(2)}, u32[]{:S(2)}) %collective-permute-start.23) | collective-permute-done | bytes 229408 | tf_op jit(solution)/shard_map/ppermute | solution.py:308
  54.4 1.9 %collective-permute-done.24 = f32[2,112,256]{2,1,0:T(8,128)S(1)} collective-permute-done((f32[2,112,256]{2,1,0:T(8,128)S(1)}, f32[2,112,256]{2,1,0:T(8,128)S(1)}, u32[]{:S(2)}, u32[]{:S(2)}) %collective-permute-start.24) | collective-permute-done | bytes 229408 | tf_op jit(solution)/shard_map/ppermute | solution.py:308
  56.7 1.7 %collective-permute-start.25 = (f32[112,256]{1,0:T(8,128)S(1)}, f32[112,256]{1,0:T(8,128)S(1)}, u32[]{:S(2)}, u32[]{:S(2)}) collective-permute-start(f32[112,256]{1,0:T(8,128)S(1)} %fusion.11), channel_id=1, source_target_pairs={{0,4},{1,5},{2,6},{3,7},{4,0},{5,1},{6,2},{7,3},{8,12},{9,13},{10,... | collective-permute-start | bytes 344072 | tf_op jit(solution)/shard_map/ppermute | solution.py:308
  58.4 1.9 %shard_map.102 = f32[450,1,256]{2,1,0:T(1,128)} custom-call(f32[240,256]{1,0:T(8,128)S(1)} %shard_map.100.refs_0_.refs_3_, bf16[1792,256]{1,0:T(8,128)(2,1)S(1)} %get-tuple-element.80.refs_1_, bf16[1792,256]{1,0:T(8,128)(2,1)S(1)} %get-tuple-element.81.refs_2_, f32[240,256]{1,0:T(8,128)S(1)} %get-tuple-element.65.refs_3_), custom_call_target="tpu_custom_call" | custom-call | flops 660602880 | bytes 2787328 | tf_op jit(solution)/shard_map/pallas_call | solution.py:26
  60.3 0.7 %maximum_bitcast_fusion.1 = f32[1,224,256]{2,1,0:T(8,128)} fusion(f32[112,256]{1,0:T(8,128)S(1)} %get-tuple-element.91, f32[112,256]{1,0:T(8,128)S(1)} %get-tuple-element.90), kind=kLoop, calls=%fused_computation.10 | loop fusion | flops 57344 | bytes 458752 | tf_op jit(solution)/shard_map/broadcast_in_dim | solution.py:371
  61.6 0.7 %maximum_bitcast_fusion = f32[1,224,256]{2,1,0:T(8,128)} fusion(f32[112,256]{1,0:T(8,128)S(1)} %get-tuple-element.95, f32[112,256]{1,0:T(8,128)S(1)} %get-tuple-element.94), kind=kLoop, calls=%fused_computation.9 | loop fusion | flops 57344 | bytes 458752 | tf_op jit(solution)/shard_map/broadcast_in_dim | solution.py:371
  (79 shorter events, 7.7 us)
Async XLA Ops:
  0.6 20.3 %copy-start.1 = (f32[1,224,256]{2,1,0:T(8,128)S(1)}, f32[1,224,256]{2,1,0:T(8,128)}, u32[]{:S(2)}) copy-start(f32[1,224,256]{2,1,0:T(8,128)} %param.13) | copy-start | bytes 688132
  0.6 20.2 %copy-start.2 = (f32[1,224,256]{2,1,0:T(8,128)S(1)}, f32[1,224,256]{2,1,0:T(8,128)}, u32[]{:S(2)}) copy-start(f32[1,224,256]{2,1,0:T(8,128)} %param.12) | copy-start | bytes 688132
  0.7 9.7 %collective-permute-start.1 = (f32[224,256]{1,0:T(8,128)}, f32[224,256]{1,0:T(8,128)S(1)}, u32[]{:S(2)}, u32[]{:S(2)}) collective-permute-start(f32[224,256]{1,0:T(8,128)} %bitcast.86), channel_id=1, source_target_pairs={{0,4},{1,5},{2,6},{3,7},{4,0},{5,1},{6,2},{7,3},{8,12},{9,13},{10,... | collective-permute-start | bytes 688136 | tf_op jit(solution)/shard_map/ppermute | solution.py:308
  3.7 8.7 %collective-permute-start = (f32[224,256]{1,0:T(8,128)}, f32[224,256]{1,0:T(8,128)S(1)}, u32[]{:S(2)}, u32[]{:S(2)}) collective-permute-start(f32[224,256]{1,0:T(8,128)} %bitcast.87), channel_id=1, source_target_pairs={{0,2},{1,3},{2,0},{3,1},{4,6},{5,7},{6,4},{7,5},{8,10},{9,11},{10,... | collective-permute-start | bytes 688136 | tf_op jit(solution)/shard_map/ppermute | solution.py:308
  5.2 9.2 %collective-permute-start.4 = (f32[224,256]{1,0:T(8,128)}, f32[224,256]{1,0:T(8,128)S(1)}, u32[]{:S(2)}, u32[]{:S(2)}) collective-permute-start(f32[224,256]{1,0:T(8,128)} %bitcast.90), channel_id=1, source_target_pairs={{0,4},{1,5},{2,6},{3,7},{4,0},{5,1},{6,2},{7,3},{8,12},{9,13},{10,... | collective-permute-start | bytes 688136 | tf_op jit(solution)/shard_map/ppermute | solution.py:308
  5.7 10.6 %collective-permute-start.2 = (f32[224,256]{1,0:T(8,128)}, f32[224,256]{1,0:T(8,128)S(1)}, u32[]{:S(2)}, u32[]{:S(2)}) collective-permute-start(f32[224,256]{1,0:T(8,128)} %bitcast.91), channel_id=1, source_target_pairs={{0,2},{1,3},{2,0},{3,1},{4,6},{5,7},{6,4},{7,5},{8,10},{9,11},{10,... | collective-permute-start | bytes 688136 | tf_op jit(solution)/shard_map/ppermute | solution.py:308
  5.8 10.6 %collective-permute-start.10 = (f32[224,256]{1,0:T(8,128)}, f32[224,256]{1,0:T(8,128)S(1)}, u32[]{:S(2)}, u32[]{:S(2)}) collective-permute-start(f32[224,256]{1,0:T(8,128)} %bitcast.88), channel_id=1, source_target_pairs={{0,1},{1,0},{2,3},{3,2},{4,5},{5,4},{6,7},{7,6},{8,9},{9,8},{10,11... | collective-permute-start | bytes 688136 | tf_op jit(solution)/shard_map/ppermute | solution.py:308
  9.0 13.3 %copy-start = (f32[1,240,256]{2,1,0:T(8,128)S(1)}, f32[1,240,256]{2,1,0:T(8,128)}, u32[]{:S(2)}) copy-start(f32[1,240,256]{2,1,0:T(8,128)} %get-tuple-element.47) | copy-start | bytes 737284
  12.4 6.9 %collective-permute-start.11 = (f32[224,256]{1,0:T(8,128)S(1)}, f32[224,256]{1,0:T(8,128)S(1)}, u32[]{:S(2)}, u32[]{:S(2)}) collective-permute-start(f32[224,256]{1,0:T(8,128)S(1)} %collective-permute-done.refs_2_), channel_id=1, source_target_pairs={{0,1},{1,0},{2,3},{3,2},{4,5},{5,4},{6,7},{7,6},{8,9},{9,8},{10,11... | collective-permute-start | bytes 688136 | tf_op jit(solution)/shard_map/ppermute | solution.py:308
  12.5 5.9 %collective-permute-start.7 = (f32[112,256]{1,0:T(8,128)S(1)}, f32[112,256]{1,0:T(8,128)S(1)}, u32[]{:S(2)}, u32[]{:S(2)}) collective-permute-start(f32[112,256]{1,0:T(8,128)S(1)} %slice.144), channel_id=1, source_target_pairs={{0,2},{1,3},{2,0},{3,1},{4,6},{5,7},{6,4},{7,5},{8,10},{9,11},{10,... | collective-permute-start | bytes 344072 | tf_op jit(solution)/shard_map/ppermute | solution.py:308
  14.4 4.9 %collective-permute-start.6 = (f32[112,256]{1,0:T(8,128)S(1)}, f32[112,256]{1,0:T(8,128)S(1)}, u32[]{:S(2)}, u32[]{:S(2)}) collective-permute-start(f32[112,256]{1,0:T(8,128)S(1)} %slice.143), channel_id=1, source_target_pairs={{0,4},{1,5},{2,6},{3,7},{4,0},{5,1},{6,2},{7,3},{8,12},{9,13},{10,... | collective-permute-start | bytes 344072 | tf_op jit(solution)/shard_map/ppermute | solution.py:308
  16.3 4.5 %collective-permute-start.12 = (f32[224,256]{1,0:T(8,128)S(1)}, f32[224,256]{1,0:T(8,128)S(1)}, u32[]{:S(2)}, u32[]{:S(2)}) collective-permute-start(f32[224,256]{1,0:T(8,128)S(1)} %collective-permute-done.1.refs_3_), channel_id=1, source_target_pairs={{0,1},{1,0},{2,3},{3,2},{4,5},{5,4},{6,7},{7,6},{8,9},{9,8},{10,11... | collective-permute-start | bytes 688136 | tf_op jit(solution)/shard_map/ppermute | solution.py:308
  16.4 7.5 %collective-permute-start.5 = (f32[112,256]{1,0:T(8,128)S(1)}, f32[112,256]{1,0:T(8,128)S(1)}, u32[]{:S(2)}, u32[]{:S(2)}) collective-permute-start(f32[112,256]{1,0:T(8,128)S(1)} %slice.179), channel_id=1, source_target_pairs={{0,2},{1,3},{2,0},{3,1},{4,6},{5,7},{6,4},{7,5},{8,10},{9,11},{10,... | collective-permute-start | bytes 344072 | tf_op jit(solution)/shard_map/ppermute | solution.py:308
  18.3 5.6 %collective-permute-start.3 = (f32[112,256]{1,0:T(8,128)S(1)}, f32[112,256]{1,0:T(8,128)S(1)}, u32[]{:S(2)}, u32[]{:S(2)}) collective-permute-start(f32[112,256]{1,0:T(8,128)S(1)} %slice.178), channel_id=1, source_target_pairs={{0,4},{1,5},{2,6},{3,7},{4,0},{5,1},{6,2},{7,3},{8,12},{9,13},{10,... | collective-permute-start | bytes 344072 | tf_op jit(solution)/shard_map/ppermute | solution.py:308
  19.3 2.4 %collective-permute-start.9 = (f32[112,256]{1,0:T(8,128)S(1)}, f32[112,256]{1,0:T(8,128)S(1)}, u32[]{:S(2)}, u32[]{:S(2)}) collective-permute-start(f32[112,256]{1,0:T(8,128)S(1)} %collective-permute-done.7.refs_4_), channel_id=1, source_target_pairs={{0,1},{1,0},{2,3},{3,2},{4,5},{5,4},{6,7},{7,6},{8,9},{9,8},{10,11... | collective-permute-start | bytes 344072 | tf_op jit(solution)/shard_map/ppermute | solution.py:308
  19.3 2.9 %collective-permute-start.8 = (f32[112,256]{1,0:T(8,128)S(1)}, f32[112,256]{1,0:T(8,128)S(1)}, u32[]{:S(2)}, u32[]{:S(2)}) collective-permute-start(f32[112,256]{1,0:T(8,128)S(1)} %collective-permute-done.6.refs_3_), channel_id=1, source_target_pairs={{0,1},{1,0},{2,3},{3,2},{4,5},{5,4},{6,7},{7,6},{8,9},{9,8},{10,11... | collective-permute-start | bytes 344072 | tf_op jit(solution)/shard_map/ppermute | solution.py:308
  20.8 3.8 %collective-permute-start.15 = (f32[224,256]{1,0:T(8,128)S(1)}, f32[224,256]{1,0:T(8,128)S(1)}, u32[]{:S(2)}, u32[]{:S(2)}) collective-permute-start(f32[224,256]{1,0:T(8,128)S(1)} %bitcast.92), channel_id=1, source_target_pairs={{0,1},{1,0},{2,3},{3,2},{4,5},{5,4},{6,7},{7,6},{8,9},{9,8},{10,11... | collective-permute-start | bytes 688136 | tf_op jit(solution)/shard_map/ppermute | solution.py:308
  21.7 2.9 %collective-permute-start.17 = (f32[224,256]{1,0:T(8,128)S(1)}, f32[224,256]{1,0:T(8,128)S(1)}, u32[]{:S(2)}, u32[]{:S(2)}) collective-permute-start(f32[224,256]{1,0:T(8,128)S(1)} %collective-permute-done.4.refs_3_), channel_id=1, source_target_pairs={{0,1},{1,0},{2,3},{3,2},{4,5},{5,4},{6,7},{7,6},{8,9},{9,8},{10,11... | collective-permute-start | bytes 688136 | tf_op jit(solution)/shard_map/ppermute | solution.py:308
  22.2 2.4 %collective-permute-start.16 = (f32[224,256]{1,0:T(8,128)S(1)}, f32[224,256]{1,0:T(8,128)S(1)}, u32[]{:S(2)}, u32[]{:S(2)}) collective-permute-start(f32[224,256]{1,0:T(8,128)S(1)} %collective-permute-done.2.refs_2_), channel_id=1, source_target_pairs={{0,1},{1,0},{2,3},{3,2},{4,5},{5,4},{6,7},{7,6},{8,9},{9,8},{10,11... | collective-permute-start | bytes 688136 | tf_op jit(solution)/shard_map/ppermute | solution.py:308
  23.9 1.5 %collective-permute-start.13 = (f32[112,256]{1,0:T(8,128)S(1)}, f32[112,256]{1,0:T(8,128)S(1)}, u32[]{:S(2)}, u32[]{:S(2)}) collective-permute-start(f32[112,256]{1,0:T(8,128)S(1)} %collective-permute-done.3.refs_2_), channel_id=1, source_target_pairs={{0,1},{1,0},{2,3},{3,2},{4,5},{5,4},{6,7},{7,6},{8,9},{9,8},{10,11... | collective-permute-start | bytes 344072 | tf_op jit(solution)/shard_map/ppermute | solution.py:308
  24.4 1.3 %collective-permute-start.14 = (f32[112,256]{1,0:T(8,128)S(1)}, f32[112,256]{1,0:T(8,128)S(1)}, u32[]{:S(2)}, u32[]{:S(2)}) collective-permute-start(f32[112,256]{1,0:T(8,128)S(1)} %collective-permute-done.5.refs_3_), channel_id=1, source_target_pairs={{0,1},{1,0},{2,3},{3,2},{4,5},{5,4},{6,7},{7,6},{8,9},{9,8},{10,11... | collective-permute-start | bytes 344072 | tf_op jit(solution)/shard_map/ppermute | solution.py:308
  27.3 9.9 %collective-permute-start.18 = (f32[240,256]{1,0:T(8,128)S(1)}, f32[240,256]{1,0:T(8,128)S(1)}, u32[]{:S(2)}, u32[]{:S(2)}) collective-permute-start(f32[240,256]{1,0:T(8,128)S(1)} %get-tuple-element.65.refs_3_), channel_id=1, source_target_pairs={{8,0},{16,8},{24,16},{9,1},{17,9},{25,17},{10,2},{18,10},{26,18},{... | collective-permute-start | bytes 737288 | tf_op jit(solution)/shard_map/ppermute | solution.py:418
  38.3 2.6 %collective-permute-start.19 = (f32[4,224,256]{2,1,0:T(8,128)S(1)}, f32[4,224,256]{2,1,0:T(8,128)S(1)}, u32[]{:S(2)}, u32[]{:S(2)}) collective-permute-start(f32[4,224,256]{2,1,0:T(8,128)S(1)} %slice_bitcast_fusion.2), channel_id=1, source_target_pairs={{0,1},{1,0},{2,3},{3,2},{4,5},{5,4},{6,7},{7,6},{8,9},{9,8},{10,11... | collective-permute-start | bytes 2752520 | tf_op jit(solution)/shard_map/ppermute | solution.py:308
  40.4 4.0 %collective-permute-start.22 = (f32[4,224,256]{2,1,0:T(8,128)S(1)}, f32[4,224,256]{2,1,0:T(8,128)S(1)}, u32[]{:S(2)}, u32[]{:S(2)}) collective-permute-start(f32[4,224,256]{2,1,0:T(8,128)S(1)} %slice_bitcast_fusion), channel_id=1, source_target_pairs={{0,1},{1,0},{2,3},{3,2},{4,5},{5,4},{6,7},{7,6},{8,9},{9,8},{10,11... | collective-permute-start | bytes 2752520 | tf_op jit(solution)/shard_map/ppermute | solution.py:308
  41.1 8.5 %collective-permute-start.20 = (f32[2,112,256]{2,1,0:T(8,128)S(1)}, f32[2,112,256]{2,1,0:T(8,128)S(1)}, u32[]{:S(2)}, u32[]{:S(2)}) collective-permute-start(f32[2,112,256]{2,1,0:T(8,128)S(1)} %pad_maximum_fusion), channel_id=1, source_target_pairs={{0,2},{1,3},{2,0},{3,1},{4,6},{5,7},{6,4},{7,5},{8,10},{9,11},{10,... | collective-permute-start | bytes 688136 | tf_op jit(solution)/shard_map/ppermute | solution.py:308
  42.8 8.5 %collective-permute-start.21 = (f32[2,112,256]{2,1,0:T(8,128)S(1)}, f32[2,112,256]{2,1,0:T(8,128)S(1)}, u32[]{:S(2)}, u32[]{:S(2)}) collective-permute-start(f32[2,112,256]{2,1,0:T(8,128)S(1)} %stack.76), channel_id=1, source_target_pairs={{0,4},{1,5},{2,6},{3,7},{4,0},{5,1},{6,2},{7,3},{8,12},{9,13},{10,... | collective-permute-start | bytes 688136 | tf_op jit(solution)/shard_map/ppermute | solution.py:308
  44.5 9.8 %collective-permute-start.23 = (f32[2,112,256]{2,1,0:T(8,128)S(1)}, f32[2,112,256]{2,1,0:T(8,128)S(1)}, u32[]{:S(2)}, u32[]{:S(2)}) collective-permute-start(f32[2,112,256]{2,1,0:T(8,128)S(1)} %pad_maximum_fusion.1), channel_id=1, source_target_pairs={{0,2},{1,3},{2,0},{3,1},{4,6},{5,7},{6,4},{7,5},{8,10},{9,11},{10,... | collective-permute-start | bytes 688136 | tf_op jit(solution)/shard_map/ppermute | solution.py:308
  45.1 11.1 %collective-permute-start.24 = (f32[2,112,256]{2,1,0:T(8,128)S(1)}, f32[2,112,256]{2,1,0:T(8,128)S(1)}, u32[]{:S(2)}, u32[]{:S(2)}) collective-permute-start(f32[2,112,256]{2,1,0:T(8,128)S(1)} %stack.77), channel_id=1, source_target_pairs={{0,4},{1,5},{2,6},{3,7},{4,0},{5,1},{6,2},{7,3},{8,12},{9,13},{10,... | collective-permute-start | bytes 688136 | tf_op jit(solution)/shard_map/ppermute | solution.py:308
  51.4 8.9 %collective-permute-start.27 = (f32[112,256]{1,0:T(8,128)S(1)}, f32[112,256]{1,0:T(8,128)S(1)}, u32[]{:S(2)}, u32[]{:S(2)}) collective-permute-start(f32[112,256]{1,0:T(8,128)S(1)} %get-tuple-element.92), channel_id=1, source_target_pairs={{0,4},{1,5},{2,6},{3,7},{4,0},{5,1},{6,2},{7,3},{8,12},{9,13},{10,... | collective-permute-start | bytes 344072 | tf_op jit(solution)/shard_map/ppermute | solution.py:308
  52.9 7.3 %collective-permute-start.28 = (f32[112,256]{1,0:T(8,128)S(1)}, f32[112,256]{1,0:T(8,128)S(1)}, u32[]{:S(2)}, u32[]{:S(2)}) collective-permute-start(f32[112,256]{1,0:T(8,128)S(1)} %get-tuple-element.93), channel_id=1, source_target_pairs={{0,2},{1,3},{2,0},{3,1},{4,6},{5,7},{6,4},{7,5},{8,10},{9,11},{10,... | collective-permute-start | bytes 344072 | tf_op jit(solution)/shard_map/ppermute | solution.py:308
  56.3 4.9 %collective-permute-start.26 = (f32[112,256]{1,0:T(8,128)S(1)}, f32[112,256]{1,0:T(8,128)S(1)}, u32[]{:S(2)}, u32[]{:S(2)}) collective-permute-start(f32[112,256]{1,0:T(8,128)S(1)} %fusion.8), channel_id=1, source_target_pairs={{0,2},{1,3},{2,0},{3,1},{4,6},{5,7},{6,4},{7,5},{8,10},{9,11},{10,... | collective-permute-start | bytes 344072 | tf_op jit(solution)/shard_map/ppermute | solution.py:308
  56.7 4.8 %collective-permute-start.25 = (f32[112,256]{1,0:T(8,128)S(1)}, f32[112,256]{1,0:T(8,128)S(1)}, u32[]{:S(2)}, u32[]{:S(2)}) collective-permute-start(f32[112,256]{1,0:T(8,128)S(1)} %fusion.11), channel_id=1, source_target_pairs={{0,4},{1,5},{2,6},{3,7},{4,0},{5,1},{6,2},{7,3},{8,12},{9,13},{10,... | collective-permute-start | bytes 344072 | tf_op jit(solution)/shard_map/ppermute | solution.py:308
  (5 other events, 24.2 us)
